TPU v7x, 32 devices: a whole 2x2x4 slice. The times are simulated.
32 devices in a mesh: hours: 2 (over y), pairs: 16 (over z, x, core).
Axes of the slice: x: 2, y: 2, z: 4, core: 2. Of those that a mesh axis runs over, the one named last changes fastest.
Arguments:
- spectra: bfloat16 [32, 2, 8, 256, 256], P(('hours', 'pairs')), parts along dimension 0, may hold values from -6 to 6
- pair_offset: int32 [32, 4], P(('hours', 'pairs')), parts along dimension 0, may hold values from 0 to 4
- lag_limit: int32 [32, 4], P(('hours', 'pairs')), parts along dimension 0, may hold values from 64 to 256
Outputs:
- correlations: bfloat16 [32, 4, 256, 512], P(('hours', 'pairs')), parts along dimension 0
There are 2 independent parts, one for each index of `hours`. A program takes and returns all parts, laid end to end along the dimension named above; each array names one. Nothing has to cross between parts.
Inputs may be any that keep to these rules, and one draw needn't show every extreme that they name: `pair_offset`: slot k of block a pairs it with block a + value; 0 marks an empty slot; partners past the last block of the last fibre have zero spectra.
All inputs are finite; a program needn't handle non-finite values.
Results may differ from a plain program's by a relative error of at most 0.011.
Values may be sent and summed in bfloat16 or wider, within the bound.
No kernel may reach another device: no remote copies, remote signals or barrier semaphores. Data moves between devices by JAX's collectives and lax.ppermute only.
A program may use at most 128 MiB of HBM per device.

v0:
```python
import math

import jax
import jax.numpy as jnp
from jax import lax
from jax.sharding import PartitionSpec as P

LAGS = 512
BAND_LO = 16
REACH = 4


def shifted(array, axis, by):
    devices = lax.axis_size(axis)
    pairs = [(i, i + by) for i in range(devices) if 0 <= i + by < devices]
    return lax.ppermute(array, axis, pairs)


def whiten(block):
    values = block.astype(jnp.float32)
    power = jnp.mean(values * values, axis=(-4, -1), keepdims=True)
    return (values * lax.rsqrt(power + 1e-06)).astype(jnp.bfloat16)


def phase_table(bins, lag_count):
    freq = jnp.arange(bins, dtype=jnp.int32) + BAND_LO
    lag_index = jnp.arange(lag_count, dtype=jnp.int32)
    phase = freq[:, None] * lag_index[None, :] % lag_count
    angle = 2.0 * math.pi / lag_count * phase.astype(jnp.float32)
    scale = 1.0 / math.sqrt(bins)
    return jnp.concatenate([jnp.cos(angle) * scale, -jnp.sin(angle) * scale], axis=0).astype(
        jnp.bfloat16
    )


def cross_spectra(own_block, partners):
    windows = own_block.shape[1]
    first = own_block.astype(jnp.float32)
    second = partners.astype(jnp.float32)
    real_part = jnp.sum(first[0] * second[:, 0] + first[1] * second[:, 1], axis=1) / windows
    imag_part = jnp.sum(first[0] * second[:, 1] - first[1] * second[:, 0], axis=1) / windows
    return jnp.concatenate([real_part, imag_part], axis=-1).astype(jnp.bfloat16)


def lag_products(spectrum, offsets, limits, table):
    slot_count, channels = (spectrum.shape[0], spectrum.shape[1])
    lag_count = table.shape[1]
    lagged = jnp.dot(
        spectrum.reshape(slot_count * channels, -1), table, preferred_element_type=jnp.float32
    )
    lagged = lagged.reshape(slot_count, channels, lag_count)
    lag_index = jnp.arange(lag_count, dtype=jnp.int32)
    distance = jnp.minimum(lag_index, lag_count - lag_index)
    keep = (distance[None, :] < limits[:, None]) & (offsets[:, None] > 0)
    return jnp.where(keep[:, None, :], lagged, 0.0).astype(jnp.bfloat16)


def local(spectra, pair_offset, lag_limit):
    own_block = whiten(spectra)
    table = phase_table(spectra.shape[4], LAGS)
    received = []
    for step in range(1, REACH + 1):
        received.append(shifted(own_block, "pairs", -step))
    candidates = jnp.concatenate([own_block] + received, axis=0)
    partners = jnp.take(candidates, pair_offset[0], axis=0)
    spectrum = cross_spectra(own_block[0], partners)
    result = lag_products(spectrum, pair_offset[0], lag_limit[0], table)
    return result[None]


def solution(mesh):
    in_specs = (
        P(("hours", "pairs"), None, None, None, None),
        P(("hours", "pairs"), None),
        P(("hours", "pairs"), None),
    )
    out_specs = P(("hours", "pairs"), None, None, None)
    return jax.shard_map(local, mesh=mesh, in_specs=in_specs, out_specs=out_specs, check_vma=False)
```

profile of v0, /device:TPU:0, one launch (start us, length us, event | category | flops | bytes accessed | tf_op | source)
XLA Modules:
  0.0 211.9 jit_solution(12800202429391208543)
XLA Ops:
  0.0 2.1 fusion.1
  2.1 0.0 copy-start.1
  2.1 2.2 %fusion.17 = (f32[1,2,8,256,256]{4,3,2,1,0:T(8,128)S(1)}, bf16[1,2,8,256,256]{4,3,2,1,0:T(8,128)(2,1)S(1)}) fusion(f32[8,256]{1,0:T(8,128)S(1)} %add_rsqrt_fusion, bf16[1,2,8,256,256]{4,3,2,1,0:T(8,128)(2,1)} %param.3), kind=kLoop, calls=%fused_computation.51 | loop fusion | flops 4194304 | bytes 8396800 | tf_op jit(solution)/shard_map/convert_element_type | solution.py:38
  4.3 0.0 copy-start
  4.3 1.3 collective-permute-start
  5.6 1.3 collective-permute-start.1
  6.9 1.3 collective-permute-start.2
  8.2 1.3 collective-permute-start.3
  9.5 0.0 copy-done.1
  9.6 1.5 constant_dynamic-update-slice_fusion.4
  11.1 0.0 copy-done
  11.1 0.1 compare_and_fusion
  11.2 2.5 %multiply_convert_fusion.3 = (bf16[256,512]{1,0:T(8,128)(2,1)S(1)}, bf16[256,512]{1,0:T(8,128)(2,1)S(1)}) fusion(s32[256]{0:T(256)S(1)} %iota_add_fusion), kind=kLoop, calls=%fused_computation.31 | loop fusion | flops 2490368 | bytes 525312 | tf_op jit(solution)/shard_map/convert
  13.6 1.7 slice_bitcast_fusion.3
  15.4 0.0 collective-permute-done
  15.4 1.5 constant_dynamic-update-slice_fusion.3
  16.9 81.9 %collective-permute-done.1 = bf16[1,2,8,256,256]{4,3,2,1,0:T(8,128)(2,1)S(1)} collective-permute-done((bf16[1,2,8,256,256]{4,3,2,1,0:T(8,128)(2,1)S(1)}, bf16[1,2,8,256,256]{4,3,2,1,0:T(8,128)(2,1)S(1)}, u32[]{:S(2)}, u32[]{:S(2)}) %collective-permute-start.1) | collective-permute-done | bytes 2097184 | tf_op jit(solution)/shard_map/ppermute | solution.py:16
  98.8 1.5 constant_dynamic-update-slice_fusion.2
  100.3 0.3 collective-permute-done.2
  100.6 1.5 constant_dynamic-update-slice_fusion.1
  102.1 66.8 %collective-permute-done.3 = bf16[1,2,8,256,256]{4,3,2,1,0:T(8,128)(2,1)S(1)} collective-permute-done((bf16[1,2,8,256,256]{4,3,2,1,0:T(8,128)(2,1)S(1)}, bf16[1,2,8,256,256]{4,3,2,1,0:T(8,128)(2,1)S(1)}, u32[]{:S(2)}, u32[]{:S(2)}) %collective-permute-start.3) | collective-permute-done | bytes 2097184 | tf_op jit(solution)/shard_map/ppermute | solution.py:16
  168.9 1.5 constant_dynamic-update-slice_fusion
  170.4 9.7 %fusion.19 = (bf16[5,2,8,128,256]{4,3,2,1,0:T(8,128)(2,1)}, bf16[5,2,8,128,256]{4,3,2,1,0:T(8,128)(2,1)}) fusion(bf16[5,2,8,256,256]{4,3,2,1,0:T(8,128)(2,1)} %constant_dynamic-update-slice_fusion), kind=kLoop, calls=%fused_computation.52 | loop fusion | bytes 20971520 | tf_op jit(solution)/shard_map/jit(_take)/gather | solution.py:65
  180.1 5.3 %gather_fusion = bf16[4,2,8,128,256]{4,3,2,1,0:T(8,128)(2,1)} fusion(bf16[5,2,8,128,256]{4,3,2,1,0:T(8,128)(2,1)} %get-tuple-element.9, s32[1024]{0:T(1024)S(1)} %pad_clamp_fusion), kind=kCustom, calls=%fused_computation | custom fusion | bytes 8388624 | tf_op jit(solution)/shard_map/jit(_take)/gather | solution.py:65
  185.3 5.2 %gather_fusion.1 = bf16[4,2,8,128,256]{4,3,2,1,0:T(8,128)(2,1)} fusion(bf16[5,2,8,128,256]{4,3,2,1,0:T(8,128)(2,1)} %get-tuple-element.10, s32[1024]{0:T(1024)S(1)} %pad_clamp_fusion), kind=kCustom, calls=%fused_computation.1 | custom fusion | bytes 8388624 | tf_op jit(solution)/shard_map/jit(_take)/gather | solution.py:65
  190.6 11.6 %fusion = f32[4,2,8,256,256]{4,3,2,1,0:T(8,128)} fusion(bf16[4,2,8,128,256]{4,3,2,1,0:T(8,128)(2,1)} %gather_fusion.1, bf16[4,2,8,128,256]{4,3,2,1,0:T(8,128)(2,1)} %gather_fusion, pred[4]{0:T(512)(128)(4,1)S(1)} %get-tuple-element.16), kind=kLoop, calls=%fused_computation.5 | loop fusion | flops 25165824 | bytes 25165828 | tf_op jit(solution)/shard_map/convert_element_type | solution.py:39
  202.1 7.9 %add_reduce_fusion = (f32[4,256,256]{2,1,0:T(8,128)S(1)}, f32[4,256,256]{2,1,0:T(8,128)S(1)}) fusion(f32[4,2,8,256,256]{4,3,2,1,0:T(8,128)} %fusion, f32[8,256,256]{2,1,0:T(8,128)} %get-tuple-element.12, f32[8,256,256]{2,1,0:T(8,128)S(1)} %get-tuple-element.11), kind=kLoop, calls=%fused_computation.7 | loop fusion | flops 16252928 | bytes 23068672 | tf_op jit(solution)/shard_map/reduce_sum | solution.py:40
  210.0 0.2 multiply_convert_fusion
  210.2 1.7 fusion.3
  (6 shorter events, 0.0 us)
Async XLA Ops:
  2.1 7.4 %copy-start.1 = (s32[1,4]{1,0:T(1,128)S(1)}, s32[1,4]{1,0:T(1,128)}, u32[]{:S(2)}) copy-start(s32[1,4]{1,0:T(1,128)} %param.4) | copy-start | bytes 52
  4.3 6.8 %copy-start = (s32[1,4]{1,0:T(1,128)S(1)}, s32[1,4]{1,0:T(1,128)}, u32[]{:S(2)}) copy-start(s32[1,4]{1,0:T(1,128)} %param.5) | copy-start | bytes 52
  4.3 11.1 %collective-permute-start = (bf16[1,2,8,256,256]{4,3,2,1,0:T(8,128)(2,1)S(1)}, bf16[1,2,8,256,256]{4,3,2,1,0:T(8,128)(2,1)S(1)}, u32[]{:S(2)}, u32[]{:S(2)}) collective-permute-start(bf16[1,2,8,256,256]{4,3,2,1,0:T(8,128)(2,1)S(1)} %get-tuple-element.8), channel_id=1, source_target_pairs={{1,0},{2,1},{3,2},{4,3},{5,4},{6,5},{7,6},{8,7},{9,8},{10,9},{11,1... | collective-permute-start | bytes 6291464 | tf_op jit(solution)/shard_map/ppermute | solution.py:16
  5.6 93.2 %collective-permute-start.1 = (bf16[1,2,8,256,256]{4,3,2,1,0:T(8,128)(2,1)S(1)}, bf16[1,2,8,256,256]{4,3,2,1,0:T(8,128)(2,1)S(1)}, u32[]{:S(2)}, u32[]{:S(2)}) collective-permute-start(bf16[1,2,8,256,256]{4,3,2,1,0:T(8,128)(2,1)S(1)} %get-tuple-element.8), channel_id=1, source_target_pairs={{2,0},{3,1},{4,2},{5,3},{6,4},{7,5},{8,6},{9,7},{10,8},{11,9},{12,... | collective-permute-start | bytes 6291464 | tf_op jit(solution)/shard_map/ppermute | solution.py:16
  6.9 93.7 %collective-permute-start.2 = (bf16[1,2,8,256,256]{4,3,2,1,0:T(8,128)(2,1)S(1)}, bf16[1,2,8,256,256]{4,3,2,1,0:T(8,128)(2,1)S(1)}, u32[]{:S(2)}, u32[]{:S(2)}) collective-permute-start(bf16[1,2,8,256,256]{4,3,2,1,0:T(8,128)(2,1)S(1)} %get-tuple-element.8), channel_id=1, source_target_pairs={{3,0},{4,1},{5,2},{6,3},{7,4},{8,5},{9,6},{10,7},{11,8},{12,9},{13... | collective-permute-start | bytes 6291464 | tf_op jit(solution)/shard_map/ppermute | solution.py:16
  8.2 160.7 %collective-permute-start.3 = (bf16[1,2,8,256,256]{4,3,2,1,0:T(8,128)(2,1)S(1)}, bf16[1,2,8,256,256]{4,3,2,1,0:T(8,128)(2,1)S(1)}, u32[]{:S(2)}, u32[]{:S(2)}) collective-permute-start(bf16[1,2,8,256,256]{4,3,2,1,0:T(8,128)(2,1)S(1)} %get-tuple-element.8), channel_id=1, source_target_pairs={{4,0},{5,1},{6,2},{7,3},{8,4},{9,5},{10,6},{11,7},{12,8},{13,9},{1... | collective-permute-start | bytes 6291464 | tf_op jit(solution)/shard_map/ppermute | solution.py:16
where the time goes:
time: 212 us
  waiting for transfers between devices  149 us (70%)
  local copies, waits for them, and re-layouts  29.5 us (14%)
  other arithmetic  26.5 us (12%)
  starting transfers between devices  5.17 us (2%)
    ppermute x4, waiting for transfers between devices, shifted(): return lax.ppermute(array, axis, pairs)  149 us
    gather x3, local copies, waits for them, and re-layouts, local(): partners = jnp.take(candidates, pair_offset[0], axis=0)  20.1 us
    convert_element_type x1, other arithmetic, cross_spectra(): second = partners.astype(jnp.float32)  11.6 us
    reduce_sum x1, other arithmetic, cross_spectra(): jnp.sum(first[0] * second[:, 0] + first[1] * second[:, 1], axis=1) / windows  7.88 us
    unnamed x8, local copies, waits for them, and re-layouts  6.08 us
    ppermute x4, starting transfers between devices, shifted(): return lax.ppermute(array, axis, pairs)  5.17 us
  transfers between devices with their start and end apart: 4, of which 3 were waited for; matrix products, arithmetic and copies ran while one was open for 5% of the time, Pallas kernels for 0%

commit v1 on v0

v1 whole, which is shorter than its diff:
```python
import functools
import math

import jax
import jax.numpy as jnp
import numpy as np
from jax import lax
from jax.experimental import pallas as pl
from jax.experimental.pallas import tpu as pltpu
from jax.sharding import PartitionSpec as P

BAND_LO = 16
TILE = 16
LANES = 128
VMEM_LIMIT = 56 * 1024 * 1024


def whiten_kernel(position, mine_in, theirs_in, mine_out, theirs_out):
    windows, rows = mine_in.shape[2], mine_in.shape[3]
    for source, target in ((theirs_in, theirs_out), (mine_in, mine_out)):

        def one_window(w, _):
            for row in range(0, rows, TILE):
                block = pl.ds(row, TILE)
                values = source[0, :, w, block, :].astype(jnp.float32)
                power = jnp.sum(jnp.sum(values * values, axis=0), axis=-1, keepdims=True)
                power = power / (values.shape[0] * values.shape[-1])
                scaled = values * lax.rsqrt(power + 1e-06)
                target[0, :, w, block, :] = scaled.astype(jnp.bfloat16)
            return 0

        lax.fori_loop(0, windows, one_window, 0)


def whiten(position, spectra):
    parts, windows, channels, bins = spectra.shape[1:]
    rows = channels // 4
    block = (1, parts, windows, rows, bins)
    shape = jax.ShapeDtypeStruct((2, parts, windows, rows, bins), jnp.bfloat16)
    own = lambda k, position: (0, 0, 0, 2 * k + position[0], 0)
    other = lambda k, position: (0, 0, 0, 2 * k + 1 - position[0], 0)
    out = lambda k, position: (k, 0, 0, 0, 0)
    return pl.pallas_call(
        whiten_kernel,
        out_shape=(shape, shape),
        grid_spec=pltpu.PrefetchScalarGridSpec(
            num_scalar_prefetch=1,
            grid=(2,),
            in_specs=[pl.BlockSpec(block, own), pl.BlockSpec(block, other)],
            out_specs=[pl.BlockSpec(block, out), pl.BlockSpec(block, out)],
        ),
        compiler_params=pltpu.CompilerParams(vmem_limit_bytes=VMEM_LIMIT),
        cost_estimate=pl.CostEstimate(flops=5_000_000, bytes_accessed=4_000_000, transcendentals=0),
        name="whiten",
    )(position, spectra, spectra)


def products(first, second, stores, rows, bins, windows):
    def one_tile(step, _):
        row = pl.multiple_of(step * TILE, TILE)
        for lane in range(0, bins, LANES):
            reals = [[0.0] * len(second) for _ in first]
            imags = [[0.0] * len(second) for _ in first]
            for w in range(windows):
                a = [[f(part, w, row, lane) for part in range(2)] for f in first]
                b = [[f(part, w, row, lane) for part in range(2)] for f in second]
                for i, (ar, ai) in enumerate(a):
                    for j, (br, bi) in enumerate(b):
                        if not stores[i][j]:
                            continue
                        reals[i][j] = reals[i][j] + (ar * br + ai * bi)
                        imags[i][j] = imags[i][j] + (ar * bi - ai * br)
            for i in range(len(first)):
                for j in range(len(second)):
                    for ref, spot in stores[i][j]:
                        scale = 1.0 / windows
                        ref[spot, pl.ds(row, TILE), pl.ds(lane, LANES)] = (
                            reals[i][j] * scale
                        ).astype(jnp.bfloat16)
                        ref[spot, pl.ds(row, TILE), pl.ds(bins + lane, LANES)] = (
                            imags[i][j] * scale
                        ).astype(jnp.bfloat16)
        return 0

    lax.fori_loop(0, rows // TILE, one_tile, 0)


def reader(ref, *lead):
    def read(part, w, row, lane):
        index = lead + (part, w, pl.ds(row, TILE), pl.ds(lane, LANES))
        return ref[index].astype(jnp.float32)

    return read


def cross_kernel(position, mine, got, down0, down1, up0, up1, side0, side1, xs, xd, zs, zd, here, chip):
    windows, rows, bins = mine.shape[2], mine.shape[3], mine.shape[4]
    core, x = position[0], position[1]
    run = functools.partial(products, rows=rows, bins=bins, windows=windows)
    own_p = [reader(mine, 0), reader(got, 0)]
    own_q = [reader(mine, 1), reader(got, 1)]
    down = [reader(down0), reader(down1)]
    up = [reader(up0), reader(up1)]
    side = [reader(side0), reader(side1)]

    def spots(straight, crossed, base):
        return [
            [[(straight, base + core)], [(straight, base + 1 - core)]],
            [[(crossed, base + core)], [(crossed, base + 1 - core)]],
        ]

    @pl.when(x == 0)
    def _():
        run(up, own_q, spots(zs, zd, 2))
        run(side, down, spots(xs, xd, 0))
        run(own_p, side, spots(here, chip, 0))
        run(own_p, down, spots(here, chip, 2))

    @pl.when(x == 1)
    def _():
        run(up, side, spots(zs, zd, 0))
        run(up, own_q, spots(zs, zd, 2))
        run(side, own_q, spots(xs, xd, 0))
        run(own_p, down, spots(here, chip, 2))

    for own, spot in ((own_p, 4), (own_q, 5)):
        both = [[(here, spot), (chip, spot)]]

        @pl.when(core == 0)
        def _():
            run([own[0]], [own[1]], [both])

        @pl.when(core == 1)
        def _():
            run([own[1]], [own[0]], [both])


def cross(position, mine, got, received):
    rows, bins = mine.shape[3], mine.shape[4]
    out = lambda n: jax.ShapeDtypeStruct((n, rows, 2 * bins), jnp.bfloat16)
    vmem = pl.BlockSpec(memory_space=pltpu.VMEM)
    return pl.pallas_call(
        cross_kernel,
        out_shape=(out(2), out(2), out(4), out(4), out(6), out(6)),
        in_specs=[pl.BlockSpec(memory_space=pltpu.SMEM)] + [vmem] * 8,
        out_specs=[vmem] * 6,
        compiler_params=pltpu.CompilerParams(vmem_limit_bytes=VMEM_LIMIT),
        cost_estimate=pl.CostEstimate(flops=20_000_000, bytes_accessed=6_000_000, transcendentals=0),
        name="cross",
    )(position, mine, got, *received)


def lag_kernel(position, offsets, limits, here, chip, xs, xd, zs, zd, table, out, cand):
    core, x = position[0], position[1]
    rows, lags = here.shape[1], table.shape[1]
    for near_side, (local, side, far) in enumerate(((here, xs, zs), (chip, xd, zd))):
        half = core if near_side == 0 else 1 - core
        p_rows = pl.ds(pl.multiple_of(half * rows, rows), rows)
        q_rows = pl.ds(pl.multiple_of((2 + half) * rows, rows), rows)
        cand[0, p_rows, :] = local[4]
        cand[0, q_rows, :] = local[5]
        cand[3:5, p_rows, :] = local[2:4]
        cand[3:5, q_rows, :] = far[2:4]

        @pl.when(x == 0)
        def _():
            cand[1:3, p_rows, :] = local[0:2]
            cand[1:3, q_rows, :] = side[...]

        @pl.when(x == 1)
        def _():
            cand[1:3, p_rows, :] = side[...]
            cand[1:3, q_rows, :] = far[0:2]

    lag = lax.broadcasted_iota(jnp.int32, (1, lags), 1)
    distance = jnp.minimum(lag, lags - lag)
    for slot in range(out.shape[1]):
        offset = offsets[0, slot]
        lagged = jnp.dot(
            cand[jnp.clip(offset - 1 + core, 0, 4)],
            table[...],
            preferred_element_type=jnp.float32,
        )
        limit = jnp.where(offset > 0, limits[0, slot], 0)
        out[0, slot] = jnp.where(distance < limit, lagged, 0.0).astype(jnp.bfloat16)


def lag_products(position, offsets, limits, pieces, table):
    rows, width = pieces[0].shape[1:]
    channels, lags = 4 * rows, table.shape[1]
    vmem = pl.BlockSpec(memory_space=pltpu.VMEM)
    smem = pl.BlockSpec(memory_space=pltpu.SMEM)
    return pl.pallas_call(
        lag_kernel,
        out_shape=jax.ShapeDtypeStruct((1, offsets.shape[1], channels, lags), jnp.bfloat16),
        in_specs=[smem] * 3 + [vmem] * 7,
        out_specs=vmem,
        scratch_shapes=[pltpu.VMEM((5, channels, width), jnp.bfloat16)],
        compiler_params=pltpu.CompilerParams(vmem_limit_bytes=VMEM_LIMIT),
        cost_estimate=pl.CostEstimate(flops=500_000_000, bytes_accessed=4_000_000, transcendentals=0),
        name="lags",
    )(position, offsets, limits, *pieces, table)


def phase_table(bins, lag_count):
    freq = np.arange(bins, dtype=np.int64) + BAND_LO
    phase = freq[:, None] * np.arange(lag_count, dtype=np.int64)[None, :] % lag_count
    angle = (2.0 * math.pi / lag_count * phase).astype(np.float32)
    scale = np.float32(1.0 / math.sqrt(bins))
    rows = [np.cos(angle) * scale, -np.sin(angle) * scale]
    return np.concatenate(rows, axis=0).astype(jnp.bfloat16)


def moves(n):
    every = range(n)
    return dict(
        chip=[(i, i ^ 1) for i in every],
        xs=[(i, i ^ 2) for i in every],
        xd=[(i, i ^ 3) for i in every],
        down=[(i, i - 4) for i in every if i >= 4],
        crossed=[(i, (i - 4) ^ 1) for i in every if i >= 4],
        up=[(i, i + 4) for i in every if i + 4 < n],
    )


def local(spectra, pair_offset, lag_limit):
    n = lax.axis_size("pairs")
    move = {name: functools.partial(lax.ppermute, axis_name="pairs", perm=perm) for name, perm in moves(n).items()}
    index = lax.axis_index("pairs")
    core, x = index % 2, index // 2 % 2
    position = jnp.stack([core, x]).astype(jnp.int32)
    mine, theirs = whiten(position, spectra)
    table = jnp.asarray(phase_table(spectra.shape[4], 2 * spectra.shape[4]))

    got = move["chip"](theirs)
    received = {}
    for s, own in enumerate((mine, got)):
        received["down", s] = move["down"](own[0])
        received["up", s] = move["up"](own[1])
        received["side", s] = move["xs"](lax.dynamic_index_in_dim(own, 1 - x, keepdims=False))
    order = [received[name, s] for name in ("down", "up", "side") for s in range(2)]
    xs, xd, zs, zd, here, chip = cross(position, mine, got, order)
    zs = move["down"](zs)
    zd = move["crossed"](zd)
    xs = move["xs"](xs)
    xd = move["xd"](xd)
    chip = move["chip"](chip)
    return lag_products(position, pair_offset, lag_limit, (here, chip, xs, xd, zs, zd), table)


def solution(mesh):
    in_specs = (
        P(("hours", "pairs"), None, None, None, None),
        P(("hours", "pairs"), None),
        P(("hours", "pairs"), None),
    )
    out_specs = P(("hours", "pairs"), None, None, None)
    return jax.shard_map(local, mesh=mesh, in_specs=in_specs, out_specs=out_specs, check_vma=False)
```

time: 212 us -> 70.6 us (0.33)
  waiting for transfers between devices: 149 us -> 30.5 us
  local copies, waits for them, and re-layouts: 29.5 us -> 3.27 us
  other arithmetic: 26.5 us -> 0.61 us
  Pallas kernels: 0 us -> 17 us
  starting transfers between devices: 5.17 us -> 18.7 us
    ppermute x4 -> x12, waiting for transfers between devices: 149 us -> 30.5 us  [the longest x2 8.6 us: local(): received['down', s] = move['down'](own[0])]
    gather x3 -> x0, local copies, waits for them, and re-layouts: 20.1 us -> none  [local(): partners = jnp.take(candidates, pair_offset[0], axis=0)]
    pallas_call x0 -> x3, Pallas kernels: none -> 17 us  [the longest x1 7.52 us: cross(): pl.pallas_call(cross_kernel, out_shape=(out(2), out(2), out(4), out(4), o...]
    convert_element_type x2 -> x0, other arithmetic: 13.8 us -> none  [the longest x1 11.6 us: cross_spectra(): second = partners.astype(jnp.float32)]
    ppermute x4 -> x12, starting transfers between devices: 5.17 us -> 18.7 us  [the longest x2 8.07 us: local(): received['up', s] = move['up'](own[1])]
    reduce_sum x2 -> x0, other arithmetic: 9.95 us -> none  [the longest x1 7.88 us: cross_spectra(): jnp.sum(first[0] * second[:, 0] + first[1] * second[:, 1], axis=1) / windows]
    unnamed x8 -> x24, local copies, waits for them, and re-layouts: 6.08 us -> 1.63 us
  transfers between devices with their start and end apart: 4 -> 12, of which waited for: 3 -> 9; matrix products, arithmetic and copies ran while one was open for 5% -> 2% of each run, Pallas kernels for 0% -> 0%
where the time goes in v1:
time: 70.6 us; the launch traced here: 70.3 us
  waiting for transfers between devices  30.5 us (43%)
  starting transfers between devices  18.7 us (26%)
  Pallas kernels  17 us (24%)
  local copies, waits for them, and re-layouts  3.27 us (5%)
    ppermute x2, waiting for transfers between devices, local(): received['down', s] = move['down'](own[0])  8.6 us
    ppermute x2, starting transfers between devices, local(): received['up', s] = move['up'](own[1])  8.07 us
    pallas_call x1, Pallas kernels, cross(): pl.pallas_call(cross_kernel, out_shape=(out(2), out(2), out(4), out(4), o...  7.52 us
    ppermute x2, waiting for transfers between devices, local(): move['xs'](lax.dynamic_index_in_dim(own, 1 - x, keepdims=False))  6.31 us
    pallas_call x1, Pallas kernels, whiten(): pl.pallas_call(whiten_kernel, out_shape=(shape, shape), grid_spec=pltpu.P...  6.14 us
    ppermute x1, waiting for transfers between devices, local(): zd = move['crossed'](zd)  4.83 us
    ppermute x1, waiting for transfers between devices, local(): xs = move['xs'](xs)  4.65 us
    ppermute x2, waiting for transfers between devices, local(): received['up', s] = move['up'](own[1])  4.1 us
  transfers between devices with their start and end apart: 12, of which 9 were waited for; matrix products, arithmetic and copies ran while one was open for 2% of the time, Pallas kernels for 0%

profile of v1, /device:TPU:0, one launch (start us, length us, event | category | flops | bytes accessed | tf_op | source)
XLA Modules:
  0.0 70.3 jit_solution(12370608331615736468)
XLA Ops:
  0.0 0.6 pad_add_fusion.position
  0.6 6.1 %whiten.1 = (bf16[2,2,8,64,256]{4,3,2,1,0:T(8,128)(2,1)}, bf16[2,2,8,64,256]{4,3,2,1,0:T(8,128)(2,1)}) custom-call(s32[2]{0:T(128)} %pad_add_fusion.position, bf16[1,2,8,256,256]{4,3,2,1,0:T(8,128)(2,1)} %theirs_in.1, bf16[1,2,8,256,256]{4,3,2,1,0:T(8,128)(2,1)} %theirs_in.1), custom_call_target="tpu_custom_call" | custom-call | flops 5000000 | bytes 4000000 | tf_op jit(solution)/shard_map/whiten/pallas_call | solution.py:43
  6.8 0.5 collective-permute-start
  7.2 1.5 %dynamic-slice_bitcast_fusion.1 = (bf16[2,8,64,256]{3,2,1,0:T(8,128)(2,1)S(1)}, bf16[2,8,64,256]{3,2,1,0:T(8,128)(2,1)S(1)}, bf16[2,8,64,256]{3,2,1,0:T(8,128)(2,1)S(1)}) fusion(bf16[2,2,8,64,256]{4,3,2,1,0:T(8,128)(2,1)} %get-tuple-element.13.mine, s32[]{:T(128)S(6)} %select_n.23), kind=kLoop, calls=%fused_computation.3 | loop fusion | bytes 3145732 | tf_op jit(solution)/shard_map/jit(dynamic_index_in_dim)/squeeze | solution.py:240
  8.8 2.6 %collective-permute-start.5 = (bf16[2,8,64,256]{3,2,1,0:T(8,128)(2,1)S(1)}, bf16[2,8,64,256]{3,2,1,0:T(8,128)(2,1)S(1)}, u32[]{:S(2)}, u32[]{:S(2)}) collective-permute-start(bf16[2,8,64,256]{3,2,1,0:T(8,128)(2,1)S(1)} %get-tuple-element.24), channel_id=1, source_target_pairs={{0,2},{1,3},{2,0},{3,1},{4,6},{5,7},{6,4},{7,5},{8,10},{9,11},{10,... | collective-permute-start | bytes 1572872 | tf_op jit(solution)/shard_map/ppermute | solution.py:240
  11.3 3.5 %collective-permute-start.3 = (bf16[2,8,64,256]{3,2,1,0:T(8,128)(2,1)S(1)}, bf16[2,8,64,256]{3,2,1,0:T(8,128)(2,1)S(1)}, u32[]{:S(2)}, u32[]{:S(2)}) collective-permute-start(bf16[2,8,64,256]{3,2,1,0:T(8,128)(2,1)S(1)} %get-tuple-element.25), channel_id=1, source_target_pairs={{0,4},{1,5},{2,6},{3,7},{4,8},{5,9},{6,10},{7,11},{8,12},{9,13},{1... | collective-permute-start | bytes 1572872 | tf_op jit(solution)/shard_map/ppermute | solution.py:239
  14.8 1.3 %collective-permute-start.1 = (bf16[2,8,64,256]{3,2,1,0:T(8,128)(2,1)S(1)}, bf16[2,8,64,256]{3,2,1,0:T(8,128)(2,1)S(1)}, u32[]{:S(2)}, u32[]{:S(2)}) collective-permute-start(bf16[2,8,64,256]{3,2,1,0:T(8,128)(2,1)S(1)} %get-tuple-element.26), channel_id=1, source_target_pairs={{4,0},{5,1},{6,2},{7,3},{8,4},{9,5},{10,6},{11,7},{12,8},{13,9},{1... | collective-permute-start | bytes 1572872 | tf_op jit(solution)/shard_map/ppermute | solution.py:238
  16.1 0.0 collective-permute-done.got
  16.2 0.0 copy-start
  16.2 0.1 dynamic-slice_bitcast_fusion
  16.3 0.6 collective-permute-start.6
  16.9 4.6 %collective-permute-start.4 = (bf16[2,8,64,256]{3,2,1,0:T(8,128)(2,1)S(1)}, bf16[2,8,64,256]{3,2,1,0:T(8,128)(2,1)S(1)}, u32[]{:S(2)}, u32[]{:S(2)}) collective-permute-start(bf16[2,8,64,256]{3,2,1,0:T(8,128)(2,1)S(1)} %get-tuple-element.22), channel_id=1, source_target_pairs={{0,4},{1,5},{2,6},{3,7},{4,8},{5,9},{6,10},{7,11},{8,12},{9,13},{1... | collective-permute-start | bytes 1572872 | tf_op jit(solution)/shard_map/ppermute | solution.py:239
  21.4 2.7 %collective-permute-done.5.side0 = bf16[2,8,64,256]{3,2,1,0:T(8,128)(2,1)S(1)} collective-permute-done((bf16[2,8,64,256]{3,2,1,0:T(8,128)(2,1)S(1)}, bf16[2,8,64,256]{3,2,1,0:T(8,128)(2,1)S(1)}, u32[]{:S(2)}, u32[]{:S(2)}) %collective-permute-start.5) | collective-permute-done | bytes 524320 | tf_op jit(solution)/shard_map/ppermute | solution.py:240
  24.1 0.0 copy-start.1
  24.1 1.3 %collective-permute-start.2 = (bf16[2,8,64,256]{3,2,1,0:T(8,128)(2,1)S(1)}, bf16[2,8,64,256]{3,2,1,0:T(8,128)(2,1)S(1)}, u32[]{:S(2)}, u32[]{:S(2)}) collective-permute-start(bf16[2,8,64,256]{3,2,1,0:T(8,128)(2,1)S(1)} %get-tuple-element.23), channel_id=1, source_target_pairs={{4,0},{5,1},{6,2},{7,3},{8,4},{9,5},{10,6},{11,7},{12,8},{13,9},{1... | collective-permute-start | bytes 1572872 | tf_op jit(solution)/shard_map/ppermute | solution.py:238
  25.4 1.7 %collective-permute-done.3.up0 = bf16[2,8,64,256]{3,2,1,0:T(8,128)(2,1)S(1)} collective-permute-done((bf16[2,8,64,256]{3,2,1,0:T(8,128)(2,1)S(1)}, bf16[2,8,64,256]{3,2,1,0:T(8,128)(2,1)S(1)}, u32[]{:S(2)}, u32[]{:S(2)}) %collective-permute-start.3) | collective-permute-done | bytes 524320 | tf_op jit(solution)/shard_map/ppermute | solution.py:239
  27.1 0.0 copy-start.2
  27.1 4.5 %collective-permute-done.1.down0 = bf16[2,8,64,256]{3,2,1,0:T(8,128)(2,1)S(1)} collective-permute-done((bf16[2,8,64,256]{3,2,1,0:T(8,128)(2,1)S(1)}, bf16[2,8,64,256]{3,2,1,0:T(8,128)(2,1)S(1)}, u32[]{:S(2)}, u32[]{:S(2)}) %collective-permute-start.1) | collective-permute-done | bytes 524320 | tf_op jit(solution)/shard_map/ppermute | solution.py:238
  31.5 0.0 copy-start.3
  31.5 3.6 %collective-permute-done.6.side1 = bf16[2,8,64,256]{3,2,1,0:T(8,128)(2,1)S(1)} collective-permute-done((bf16[2,8,64,256]{3,2,1,0:T(8,128)(2,1)S(1)}, bf16[2,8,64,256]{3,2,1,0:T(8,128)(2,1)S(1)}, u32[]{:S(2)}, u32[]{:S(2)}) %collective-permute-start.6) | collective-permute-done | bytes 524320 | tf_op jit(solution)/shard_map/ppermute | solution.py:240
  35.2 0.0 copy-start.4
  35.2 2.4 %collective-permute-done.4.up1 = bf16[2,8,64,256]{3,2,1,0:T(8,128)(2,1)S(1)} collective-permute-done((bf16[2,8,64,256]{3,2,1,0:T(8,128)(2,1)S(1)}, bf16[2,8,64,256]{3,2,1,0:T(8,128)(2,1)S(1)}, u32[]{:S(2)}, u32[]{:S(2)}) %collective-permute-start.4) | collective-permute-done | bytes 524320 | tf_op jit(solution)/shard_map/ppermute | solution.py:239
  37.6 0.0 copy-start.5
  37.6 4.1 %collective-permute-done.2.down1 = bf16[2,8,64,256]{3,2,1,0:T(8,128)(2,1)S(1)} collective-permute-done((bf16[2,8,64,256]{3,2,1,0:T(8,128)(2,1)S(1)}, bf16[2,8,64,256]{3,2,1,0:T(8,128)(2,1)S(1)}, u32[]{:S(2)}, u32[]{:S(2)}) %collective-permute-start.2) | collective-permute-done | bytes 524320 | tf_op jit(solution)/shard_map/ppermute | solution.py:238
  41.8 0.0 copy-done
  41.8 0.0 copy-done.1
  41.8 0.0 copy-done.2
  41.8 0.0 copy-done.3
  41.8 0.0 copy-done.4
  41.8 0.0 copy-done.5
  41.8 0.0 copy-start.6
  41.8 0.8 %copy-done.6 = bf16[2,8,64,256]{3,2,1,0:T(8,128)(2,1)} copy-done((bf16[2,8,64,256]{3,2,1,0:T(8,128)(2,1)}, bf16[2,8,64,256]{3,2,1,0:T(8,128)(2,1)S(1)}, u32[]{:S(2)}) %copy-start.6) | copy-done | bytes 524312
  42.6 7.5 %cross.1 = (bf16[2,64,512]{2,1,0:T(8,128)(2,1)}, bf16[2,64,512]{2,1,0:T(8,128)(2,1)}, bf16[4,64,512]{2,1,0:T(8,128)(2,1)}, bf16[4,64,512]{2,1,0:T(8,128)(2,1)}, ...) custom-call(s32[2]{0:T(128)} %pad_add_fusion.position, bf16[2,2,8,64,256]{4,3,2,1,0:T(8,128)(2,1)} %get-tuple-element.13.mine, ...), custom_call_target="tpu_custom_call" | custom-call | flops 20000000 | bytes 6000000 | tf_op jit(solution)/shard_map/cross/pallas_call | solution.py:142
  50.1 0.0 collective-permute-start.7
  50.1 1.3 %collective-permute-start.10 = (bf16[4,64,512]{2,1,0:T(8,128)(2,1)}, bf16[4,64,512]{2,1,0:T(8,128)(2,1)S(1)}, u32[]{:S(2)}, u32[]{:S(2)}) collective-permute-start(bf16[4,64,512]{2,1,0:T(8,128)(2,1)} %get-tuple-element.19), channel_id=1, source_target_pairs={{4,0},{5,1},{6,2},{7,3},{8,4},{9,5},{10,6},{11,7},{12,8},{13,9},{1... | collective-permute-start | bytes 786440 | tf_op jit(solution)/shard_map/ppermute | solution.py:243
  51.4 1.3 %collective-permute-start.11 = (bf16[4,64,512]{2,1,0:T(8,128)(2,1)}, bf16[4,64,512]{2,1,0:T(8,128)(2,1)S(1)}, u32[]{:S(2)}, u32[]{:S(2)}) collective-permute-start(bf16[4,64,512]{2,1,0:T(8,128)(2,1)} %get-tuple-element.20), channel_id=1, source_target_pairs={{4,1},{5,0},{6,3},{7,2},{8,5},{9,4},{10,7},{11,6},{12,9},{13,8},{1... | collective-permute-start | bytes 786440 | tf_op jit(solution)/shard_map/ppermute | solution.py:244
  52.7 0.6 collective-permute-start.8
  53.3 1.3 %collective-permute-start.9 = (bf16[2,64,512]{2,1,0:T(8,128)(2,1)}, bf16[2,64,512]{2,1,0:T(8,128)(2,1)S(1)}, u32[]{:S(2)}, u32[]{:S(2)}) collective-permute-start(bf16[2,64,512]{2,1,0:T(8,128)(2,1)} %get-tuple-element.18), channel_id=1, source_target_pairs={{0,3},{1,2},{2,1},{3,0},{4,7},{5,6},{6,5},{7,4},{8,11},{9,10},{10,... | collective-permute-start | bytes 393224 | tf_op jit(solution)/shard_map/ppermute | solution.py:246
  54.6 4.7 %collective-permute-done.8.xs = bf16[2,64,512]{2,1,0:T(8,128)(2,1)S(1)} collective-permute-done((bf16[2,64,512]{2,1,0:T(8,128)(2,1)}, bf16[2,64,512]{2,1,0:T(8,128)(2,1)S(1)}, u32[]{:S(2)}, u32[]{:S(2)}) %collective-permute-start.8) | collective-permute-done | bytes 131104 | tf_op jit(solution)/shard_map/ppermute | solution.py:245
  59.3 0.0 copy-start.10
  59.3 2.0 %collective-permute-done.9.xd = bf16[2,64,512]{2,1,0:T(8,128)(2,1)S(1)} collective-permute-done((bf16[2,64,512]{2,1,0:T(8,128)(2,1)}, bf16[2,64,512]{2,1,0:T(8,128)(2,1)S(1)}, u32[]{:S(2)}, u32[]{:S(2)}) %collective-permute-start.9) | collective-permute-done | bytes 131104 | tf_op jit(solution)/shard_map/ppermute | solution.py:246
  61.3 0.0 copy-start.11
  61.3 0.0 collective-permute-done.10.zs
  61.3 0.0 copy-start.8
  61.3 4.8 %collective-permute-done.11.zd = bf16[4,64,512]{2,1,0:T(8,128)(2,1)S(1)} collective-permute-done((bf16[4,64,512]{2,1,0:T(8,128)(2,1)}, bf16[4,64,512]{2,1,0:T(8,128)(2,1)S(1)}, u32[]{:S(2)}, u32[]{:S(2)}) %collective-permute-start.11) | collective-permute-done | bytes 262176 | tf_op jit(solution)/shard_map/ppermute | solution.py:244
  66.1 0.0 copy-start.9
  66.1 0.0 collective-permute-done.7.chip
  66.1 0.0 copy-start.7
  66.2 0.0 copy-done.10
  66.2 0.0 copy-done.11
  66.2 0.0 copy-done.8
  66.2 0.7 copy-done.9
  66.8 0.1 copy-done.7
  67.0 3.3 %lags.1 = bf16[1,4,256,512]{3,2,1,0:T(8,128)(2,1)} custom-call(s32[2]{0:T(128)} %pad_add_fusion.position, s32[1,4]{1,0:T(1,128)} %offsets.1, s32[1,4]{1,0:T(1,128)} %limits.1, bf16[6,64,512]{2,1,0:T(8,128)(2,1)} %get-tuple-element.15.here, bf16[6,64,512]{2,1,0:T(8,128)(2,1)} %copy-done.7, bf16[2,64,512]{2,1,0:T(8,128)(2,1)} %copy-done.10, ...), custom_call_target="tpu_custom_call" | custom-call | flops 500000000 | bytes 4000000 | tf_op jit(solution)/shard_map/lags/pallas_call | solution.py:193
Async XLA Ops:
  6.8 9.4 %collective-permute-start = (bf16[2,2,8,64,256]{4,3,2,1,0:T(8,128)(2,1)}, bf16[2,2,8,64,256]{4,3,2,1,0:T(8,128)(2,1)S(1)}, u32[]{:S(2)}, u32[]{:S(2)}) collective-permute-start(bf16[2,2,8,64,256]{4,3,2,1,0:T(8,128)(2,1)} %get-tuple-element.14), channel_id=1, source_target_pairs={{0,1},{1,0},{2,3},{3,2},{4,5},{5,4},{6,7},{7,6},{8,9},{9,8},{10,11... | collective-permute-start | bytes 3145736 | tf_op jit(solution)/shard_map/ppermute | solution.py:235
  8.8 15.4 %collective-permute-start.5 = (bf16[2,8,64,256]{3,2,1,0:T(8,128)(2,1)S(1)}, bf16[2,8,64,256]{3,2,1,0:T(8,128)(2,1)S(1)}, u32[]{:S(2)}, u32[]{:S(2)}) collective-permute-start(bf16[2,8,64,256]{3,2,1,0:T(8,128)(2,1)S(1)} %get-tuple-element.24), channel_id=1, source_target_pairs={{0,2},{1,3},{2,0},{3,1},{4,6},{5,7},{6,4},{7,5},{8,10},{9,11},{10,... | collective-permute-start | bytes 1572872 | tf_op jit(solution)/shard_map/ppermute | solution.py:240
  11.3 15.7 %collective-permute-start.3 = (bf16[2,8,64,256]{3,2,1,0:T(8,128)(2,1)S(1)}, bf16[2,8,64,256]{3,2,1,0:T(8,128)(2,1)S(1)}, u32[]{:S(2)}, u32[]{:S(2)}) collective-permute-start(bf16[2,8,64,256]{3,2,1,0:T(8,128)(2,1)S(1)} %get-tuple-element.25), channel_id=1, source_target_pairs={{0,4},{1,5},{2,6},{3,7},{4,8},{5,9},{6,10},{7,11},{8,12},{9,13},{1... | collective-permute-start | bytes 1572872 | tf_op jit(solution)/shard_map/ppermute | solution.py:239
  14.8 16.7 %collective-permute-start.1 = (bf16[2,8,64,256]{3,2,1,0:T(8,128)(2,1)S(1)}, bf16[2,8,64,256]{3,2,1,0:T(8,128)(2,1)S(1)}, u32[]{:S(2)}, u32[]{:S(2)}) collective-permute-start(bf16[2,8,64,256]{3,2,1,0:T(8,128)(2,1)S(1)} %get-tuple-element.26), channel_id=1, source_target_pairs={{4,0},{5,1},{6,2},{7,3},{8,4},{9,5},{10,6},{11,7},{12,8},{13,9},{1... | collective-permute-start | bytes 1572872 | tf_op jit(solution)/shard_map/ppermute | solution.py:238
  16.2 25.6 %copy-start = (bf16[2,2,8,64,256]{4,3,2,1,0:T(8,128)(2,1)}, bf16[2,2,8,64,256]{4,3,2,1,0:T(8,128)(2,1)S(1)}, u32[]{:S(2)}) copy-start(bf16[2,2,8,64,256]{4,3,2,1,0:T(8,128)(2,1)S(1)} %collective-permute-done.got) | copy-start | bytes 3145732
  16.3 18.9 %collective-permute-start.6 = (bf16[2,8,64,256]{3,2,1,0:T(8,128)(2,1)S(1)}, bf16[2,8,64,256]{3,2,1,0:T(8,128)(2,1)S(1)}, u32[]{:S(2)}, u32[]{:S(2)}) collective-permute-start(bf16[2,8,64,256]{3,2,1,0:T(8,128)(2,1)S(1)} %get-tuple-element.21), channel_id=1, source_target_pairs={{0,2},{1,3},{2,0},{3,1},{4,6},{5,7},{6,4},{7,5},{8,10},{9,11},{10,... | collective-permute-start | bytes 1572872 | tf_op jit(solution)/shard_map/ppermute | solution.py:240
  16.9 20.8 %collective-permute-start.4 = (bf16[2,8,64,256]{3,2,1,0:T(8,128)(2,1)S(1)}, bf16[2,8,64,256]{3,2,1,0:T(8,128)(2,1)S(1)}, u32[]{:S(2)}, u32[]{:S(2)}) collective-permute-start(bf16[2,8,64,256]{3,2,1,0:T(8,128)(2,1)S(1)} %get-tuple-element.22), channel_id=1, source_target_pairs={{0,4},{1,5},{2,6},{3,7},{4,8},{5,9},{6,10},{7,11},{8,12},{9,13},{1... | collective-permute-start | bytes 1572872 | tf_op jit(solution)/shard_map/ppermute | solution.py:239
  24.1 17.6 %copy-start.1 = (bf16[2,8,64,256]{3,2,1,0:T(8,128)(2,1)}, bf16[2,8,64,256]{3,2,1,0:T(8,128)(2,1)S(1)}, u32[]{:S(2)}) copy-start(bf16[2,8,64,256]{3,2,1,0:T(8,128)(2,1)S(1)} %collective-permute-done.5.side0) | copy-start | bytes 1572868
  24.1 17.6 %collective-permute-start.2 = (bf16[2,8,64,256]{3,2,1,0:T(8,128)(2,1)S(1)}, bf16[2,8,64,256]{3,2,1,0:T(8,128)(2,1)S(1)}, u32[]{:S(2)}, u32[]{:S(2)}) collective-permute-start(bf16[2,8,64,256]{3,2,1,0:T(8,128)(2,1)S(1)} %get-tuple-element.23), channel_id=1, source_target_pairs={{4,0},{5,1},{6,2},{7,3},{8,4},{9,5},{10,6},{11,7},{12,8},{13,9},{1... | collective-permute-start | bytes 1572872 | tf_op jit(solution)/shard_map/ppermute | solution.py:238
  27.1 14.7 %copy-start.2 = (bf16[2,8,64,256]{3,2,1,0:T(8,128)(2,1)}, bf16[2,8,64,256]{3,2,1,0:T(8,128)(2,1)S(1)}, u32[]{:S(2)}) copy-start(bf16[2,8,64,256]{3,2,1,0:T(8,128)(2,1)S(1)} %collective-permute-done.3.up0) | copy-start | bytes 1572868
  31.5 10.2 %copy-start.3 = (bf16[2,8,64,256]{3,2,1,0:T(8,128)(2,1)}, bf16[2,8,64,256]{3,2,1,0:T(8,128)(2,1)S(1)}, u32[]{:S(2)}) copy-start(bf16[2,8,64,256]{3,2,1,0:T(8,128)(2,1)S(1)} %collective-permute-done.1.down0) | copy-start | bytes 1572868
  35.2 6.6 %copy-start.4 = (bf16[2,8,64,256]{3,2,1,0:T(8,128)(2,1)}, bf16[2,8,64,256]{3,2,1,0:T(8,128)(2,1)S(1)}, u32[]{:S(2)}) copy-start(bf16[2,8,64,256]{3,2,1,0:T(8,128)(2,1)S(1)} %collective-permute-done.6.side1) | copy-start | bytes 1572868
  37.6 4.2 %copy-start.5 = (bf16[2,8,64,256]{3,2,1,0:T(8,128)(2,1)}, bf16[2,8,64,256]{3,2,1,0:T(8,128)(2,1)S(1)}, u32[]{:S(2)}) copy-start(bf16[2,8,64,256]{3,2,1,0:T(8,128)(2,1)S(1)} %collective-permute-done.4.up1) | copy-start | bytes 1572868
  41.8 0.8 %copy-start.6 = (bf16[2,8,64,256]{3,2,1,0:T(8,128)(2,1)}, bf16[2,8,64,256]{3,2,1,0:T(8,128)(2,1)S(1)}, u32[]{:S(2)}) copy-start(bf16[2,8,64,256]{3,2,1,0:T(8,128)(2,1)S(1)} %collective-permute-done.2.down1) | copy-start | bytes 1572868
  50.1 16.0 %collective-permute-start.7 = (bf16[6,64,512]{2,1,0:T(8,128)(2,1)}, bf16[6,64,512]{2,1,0:T(8,128)(2,1)S(1)}, u32[]{:S(2)}, u32[]{:S(2)}) collective-permute-start(bf16[6,64,512]{2,1,0:T(8,128)(2,1)} %get-tuple-element.16), channel_id=1, source_target_pairs={{0,1},{1,0},{2,3},{3,2},{4,5},{5,4},{6,7},{7,6},{8,9},{9,8},{10,11... | collective-permute-start | bytes 1179656 | tf_op jit(solution)/shard_map/ppermute | solution.py:247
  50.1 11.2 %collective-permute-start.10 = (bf16[4,64,512]{2,1,0:T(8,128)(2,1)}, bf16[4,64,512]{2,1,0:T(8,128)(2,1)S(1)}, u32[]{:S(2)}, u32[]{:S(2)}) collective-permute-start(bf16[4,64,512]{2,1,0:T(8,128)(2,1)} %get-tuple-element.19), channel_id=1, source_target_pairs={{4,0},{5,1},{6,2},{7,3},{8,4},{9,5},{10,6},{11,7},{12,8},{13,9},{1... | collective-permute-start | bytes 786440 | tf_op jit(solution)/shard_map/ppermute | solution.py:243
  51.4 14.7 %collective-permute-start.11 = (bf16[4,64,512]{2,1,0:T(8,128)(2,1)}, bf16[4,64,512]{2,1,0:T(8,128)(2,1)S(1)}, u32[]{:S(2)}, u32[]{:S(2)}) collective-permute-start(bf16[4,64,512]{2,1,0:T(8,128)(2,1)} %get-tuple-element.20), channel_id=1, source_target_pairs={{4,1},{5,0},{6,3},{7,2},{8,5},{9,4},{10,7},{11,6},{12,9},{13,8},{1... | collective-permute-start | bytes 786440 | tf_op jit(solution)/shard_map/ppermute | solution.py:244
  52.7 6.6 %collective-permute-start.8 = (bf16[2,64,512]{2,1,0:T(8,128)(2,1)}, bf16[2,64,512]{2,1,0:T(8,128)(2,1)S(1)}, u32[]{:S(2)}, u32[]{:S(2)}) collective-permute-start(bf16[2,64,512]{2,1,0:T(8,128)(2,1)} %get-tuple-element.17), channel_id=1, source_target_pairs={{0,2},{1,3},{2,0},{3,1},{4,6},{5,7},{6,4},{7,5},{8,10},{9,11},{10,... | collective-permute-start | bytes 393224 | tf_op jit(solution)/shard_map/ppermute | solution.py:245
  53.3 8.0 %collective-permute-start.9 = (bf16[2,64,512]{2,1,0:T(8,128)(2,1)}, bf16[2,64,512]{2,1,0:T(8,128)(2,1)S(1)}, u32[]{:S(2)}, u32[]{:S(2)}) collective-permute-start(bf16[2,64,512]{2,1,0:T(8,128)(2,1)} %get-tuple-element.18), channel_id=1, source_target_pairs={{0,3},{1,2},{2,1},{3,0},{4,7},{5,6},{6,5},{7,4},{8,11},{9,10},{10,... | collective-permute-start | bytes 393224 | tf_op jit(solution)/shard_map/ppermute | solution.py:246
  59.3 6.9 %copy-start.10 = (bf16[2,64,512]{2,1,0:T(8,128)(2,1)}, bf16[2,64,512]{2,1,0:T(8,128)(2,1)S(1)}, u32[]{:S(2)}) copy-start(bf16[2,64,512]{2,1,0:T(8,128)(2,1)S(1)} %collective-permute-done.8.xs) | copy-start | bytes 393220
  61.3 4.9 %copy-start.11 = (bf16[2,64,512]{2,1,0:T(8,128)(2,1)}, bf16[2,64,512]{2,1,0:T(8,128)(2,1)S(1)}, u32[]{:S(2)}) copy-start(bf16[2,64,512]{2,1,0:T(8,128)(2,1)S(1)} %collective-permute-done.9.xd) | copy-start | bytes 393220
  61.3 4.9 %copy-start.8 = (bf16[4,64,512]{2,1,0:T(8,128)(2,1)}, bf16[4,64,512]{2,1,0:T(8,128)(2,1)S(1)}, u32[]{:S(2)}) copy-start(bf16[4,64,512]{2,1,0:T(8,128)(2,1)S(1)} %collective-permute-done.10.zs) | copy-start | bytes 786436
  66.1 0.7 copy-start.9
  66.1 0.8 %copy-start.7 = (bf16[6,64,512]{2,1,0:T(8,128)(2,1)}, bf16[6,64,512]{2,1,0:T(8,128)(2,1)S(1)}, u32[]{:S(2)}) copy-start(bf16[6,64,512]{2,1,0:T(8,128)(2,1)S(1)} %collective-permute-done.7.chip) | copy-start | bytes 1179652

commit v2 on v1

v2 whole, which is shorter than its diff:
```python
import functools
import math

import jax
import jax.numpy as jnp
import numpy as np
from jax import lax
from jax.experimental import pallas as pl
from jax.experimental.pallas import tpu as pltpu
from jax.sharding import PartitionSpec as P

BAND_LO = 16
TILE = 16
LANES = 128
VMEM_LIMIT = 16 * 1024 * 1024
VMEM_ALL = 60 * 1024 * 1024
WHITEN_TILE = 16


def whiten_rows(read, write, windows, rows):
    def one_window(w, _):
        for row in range(0, rows, WHITEN_TILE):
            block = pl.ds(row, WHITEN_TILE)
            values = read(w, block).astype(jnp.float32)
            power = jnp.sum(jnp.sum(values * values, axis=0), axis=-1, keepdims=True)
            power = power / (values.shape[0] * values.shape[-1])
            write(w, block, (values * lax.rsqrt(power + 1e-06)).astype(jnp.bfloat16))
        return 0

    lax.fori_loop(0, windows, one_window, 0)


def quarters_kernel(position, spectra, theirs, side, up, down, sent):
    rows = side.shape[2]
    core, x = position[0], position[1]
    copies = []
    for k, half, target in (
        (0, 1 - core, theirs.at[0]),
        (1, 1 - core, theirs.at[1]),
        (1 - x, core, side),
        (1, core, up),
        (0, core, down),
    ):
        base = pl.multiple_of((2 * k + half) * rows, rows)
        source = spectra.at[0, :, :, pl.ds(base, rows), :]
        copies.append(pltpu.make_async_copy(source, target, sent.at[len(copies)]))
    for copy in copies:
        copy.start()
    for copy in copies:
        copy.wait()


def quarters(position, spectra):
    parts, windows, channels, bins = spectra.shape[1:]
    shape = (parts, windows, channels // 4, bins)
    return pl.pallas_call(
        quarters_kernel,
        out_shape=[jax.ShapeDtypeStruct((2,) + shape, jnp.bfloat16)]
        + [jax.ShapeDtypeStruct(shape, jnp.bfloat16)] * 3,
        in_specs=[pl.BlockSpec(memory_space=pltpu.SMEM), pl.BlockSpec(memory_space=pl.ANY)],
        out_specs=[pl.BlockSpec(memory_space=pltpu.VMEM)] * 4,
        scratch_shapes=[pltpu.SemaphoreType.DMA((5,))],
        compiler_params=pltpu.CompilerParams(vmem_limit_bytes=VMEM_ALL),
        cost_estimate=pl.CostEstimate(flops=1000, bytes_accessed=1000, transcendentals=0),
        name="quarters",
    )(position, spectra)


def whiten_got_kernel(position, got, p_out, q_out, side_out):
    windows, rows = got.shape[2], got.shape[3]
    for k, target in ((0, p_out), (1, q_out)):

        def read(w, block):
            return got[k, :, w, block, :]

        def write(w, block, values):
            target[:, w, block, :] = values

        whiten_rows(read, write, windows, rows)

    @pl.when(position[1] == 0)
    def _():
        side_out[...] = q_out[...]

    @pl.when(position[1] == 1)
    def _():
        side_out[...] = p_out[...]


def whiten_got(position, got):
    vmem = pl.BlockSpec(memory_space=pltpu.VMEM)
    return pl.pallas_call(
        whiten_got_kernel,
        out_shape=[jax.ShapeDtypeStruct(got.shape[1:], jnp.bfloat16)] * 3,
        in_specs=[pl.BlockSpec(memory_space=pltpu.SMEM), vmem],
        out_specs=[vmem] * 3,
        compiler_params=pltpu.CompilerParams(vmem_limit_bytes=VMEM_LIMIT),
        cost_estimate=pl.CostEstimate(flops=3_000_000, bytes_accessed=3_000_000, transcendentals=0),
        name="whiten_got",
    )(position, got)


def whiten_blocks_kernel(*refs):
    count = len(refs) // 2
    for source, target in zip(refs[:count], refs[count:]):

        def read(w, block):
            return source[:, w, block, :]

        def write(w, block, values):
            target[:, w, block, :] = values

        whiten_rows(read, write, source.shape[1], source.shape[2])


def whiten_blocks(*blocks):
    vmem = pl.BlockSpec(memory_space=pltpu.VMEM)
    return pl.pallas_call(
        whiten_blocks_kernel,
        out_shape=[jax.ShapeDtypeStruct(block.shape, jnp.bfloat16) for block in blocks],
        in_specs=[vmem] * len(blocks),
        out_specs=[vmem] * len(blocks),
        compiler_params=pltpu.CompilerParams(vmem_limit_bytes=VMEM_LIMIT),
        cost_estimate=pl.CostEstimate(flops=3_000_000, bytes_accessed=3_000_000, transcendentals=0),
        name="whiten_blocks",
    )(*blocks)


def products(first, second, stores, rows, bins, windows):
    def one_tile(step, _):
        row = pl.multiple_of(step * TILE, TILE)
        for lane in range(0, bins, LANES):
            reals = [[0.0] * len(second) for _ in first]
            imags = [[0.0] * len(second) for _ in first]
            for w in range(windows):
                a = [[f(part, w, row, lane) for part in range(2)] for f in first]
                b = [[f(part, w, row, lane) for part in range(2)] for f in second]
                for i, (ar, ai) in enumerate(a):
                    for j, (br, bi) in enumerate(b):
                        if not stores[i][j]:
                            continue
                        reals[i][j] = reals[i][j] + (ar * br + ai * bi)
                        imags[i][j] = imags[i][j] + (ar * bi - ai * br)
            for i in range(len(first)):
                for j in range(len(second)):
                    for ref, spot in stores[i][j]:
                        scale = 1.0 / windows
                        ref[spot, pl.ds(row, TILE), pl.ds(lane, LANES)] = (
                            reals[i][j] * scale
                        ).astype(jnp.bfloat16)
                        ref[spot, pl.ds(row, TILE), pl.ds(bins + lane, LANES)] = (
                            imags[i][j] * scale
                        ).astype(jnp.bfloat16)
        return 0

    lax.fori_loop(0, rows // TILE, one_tile, 0)


def reader(ref, *lead):
    def read(part, w, row, lane):
        index = lead + (part, w, pl.ds(row, TILE), pl.ds(lane, LANES))
        return ref[index].astype(jnp.float32)

    return read


def spots(core, straight, crossed, base):
    return [
        [[(straight, base + core)], [(straight, base + 1 - core)]],
        [[(crossed, base + core)], [(crossed, base + 1 - core)]],
    ]


def chip_kernel(position, mine_p, got_p, mine_q, got_q, here, chip):
    windows, rows, bins = mine_q.shape[1:]
    core = position[0]
    run = functools.partial(products, rows=rows, bins=bins, windows=windows)
    for spot, own in enumerate(((mine_p, got_p), (mine_q, got_q))):
        both = [[(here, spot), (chip, spot)]]

        @pl.when(core == 0)
        def _():
            run([reader(own[0])], [reader(own[1])], [both])

        @pl.when(core == 1)
        def _():
            run([reader(own[1])], [reader(own[0])], [both])


def back_kernel(position, mine_p, got_p, mine_q, got_q, up0, up1, side0, side1, zs, zd, here, chip):
    windows, rows, bins = mine_q.shape[1:]
    core, x = position[0], position[1]
    run = functools.partial(products, rows=rows, bins=bins, windows=windows)
    up = [reader(up0), reader(up1)]
    side = [reader(side0), reader(side1)]

    run(up, [reader(mine_q), reader(got_q)], spots(core, zs, zd, 2))

    @pl.when(x == 0)
    def _():
        run([reader(mine_p), reader(got_p)], side, spots(core, here, chip, 0))

    @pl.when(x == 1)
    def _():
        run(up, side, spots(core, zs, zd, 0))


def near_kernel(position, mine_q, got_q, down0, down1, side0, side1, after, xs, xd):
    windows, rows, bins = mine_q.shape[1:]
    core, x = position[0], position[1]
    run = functools.partial(products, rows=rows, bins=bins, windows=windows)
    side = [reader(side0), reader(side1)]

    @pl.when(x == 0)
    def _():
        run(side, [reader(down0), reader(down1)], spots(core, xs, xd, 0))

    @pl.when(x == 1)
    def _():
        run(side, [reader(mine_q), reader(got_q)], spots(core, xs, xd, 0))


def far_kernel(position, mine_p, got_p, down0, down1, after, here, chip):
    windows, rows, bins = mine_p.shape[1:]
    run = functools.partial(products, rows=rows, bins=bins, windows=windows)
    own = [reader(mine_p), reader(got_p)]
    run(own, [reader(down0), reader(down1)], spots(position[0], here, chip, 0))


def cross(kernel, counts, position, *blocks, after=()):
    rows, bins = blocks[0].shape[2:]
    vmem = pl.BlockSpec(memory_space=pltpu.VMEM)
    return pl.pallas_call(
        kernel,
        out_shape=[jax.ShapeDtypeStruct((n, rows, 2 * bins), jnp.bfloat16) for n in counts],
        in_specs=[pl.BlockSpec(memory_space=pltpu.SMEM)]
        + [vmem] * len(blocks)
        + [pl.BlockSpec(memory_space=pl.ANY)] * len(after),
        out_specs=[vmem] * len(counts),
        compiler_params=pltpu.CompilerParams(vmem_limit_bytes=VMEM_LIMIT),
        cost_estimate=pl.CostEstimate(flops=10_000_000, bytes_accessed=5_000_000, transcendentals=0),
        name=kernel.__name__,
    )(position, *blocks, *after)


def lag_kernel(position, offsets, limits, *refs):
    table, out, cand = refs[10:]
    core, x = position[0], position[1]
    rows, lags = refs[0].shape[1], table.shape[1]
    for half, pieces in ((core, refs[:5]), (1 - core, refs[5:10])):
        pair, near, far, side, back = pieces
        p_rows = pl.ds(pl.multiple_of(half * rows, rows), rows)
        q_rows = pl.ds(pl.multiple_of((2 + half) * rows, rows), rows)
        cand[0, p_rows, :] = pair[0]
        cand[0, q_rows, :] = pair[1]
        cand[3:5, p_rows, :] = far[...]
        cand[3:5, q_rows, :] = back[2:4]

        @pl.when(x == 0)
        def _():
            cand[1:3, p_rows, :] = near[...]
            cand[1:3, q_rows, :] = side[...]

        @pl.when(x == 1)
        def _():
            cand[1:3, p_rows, :] = side[...]
            cand[1:3, q_rows, :] = back[0:2]

    lag = lax.broadcasted_iota(jnp.int32, (1, lags), 1)
    distance = jnp.minimum(lag, lags - lag)
    for slot in range(out.shape[1]):
        offset = offsets[0, slot]
        lagged = jnp.dot(
            cand[jnp.clip(offset - 1 + core, 0, 4)],
            table[...],
            preferred_element_type=jnp.float32,
        )
        limit = jnp.where(offset > 0, limits[0, slot], 0)
        out[0, slot] = jnp.where(distance < limit, lagged, 0.0).astype(jnp.bfloat16)


def lag_products(position, offsets, limits, sides, table):
    pieces = sides[0] + sides[1]
    rows, width = pieces[0].shape[1:]
    channels, lags = 4 * rows, table.shape[1]
    vmem = pl.BlockSpec(memory_space=pltpu.VMEM)
    smem = pl.BlockSpec(memory_space=pltpu.SMEM)
    return pl.pallas_call(
        lag_kernel,
        out_shape=jax.ShapeDtypeStruct((1, offsets.shape[1], channels, lags), jnp.bfloat16),
        in_specs=[smem] * 3 + [vmem] * (len(pieces) + 1),
        out_specs=vmem,
        scratch_shapes=[pltpu.VMEM((5, channels, width), jnp.bfloat16)],
        compiler_params=pltpu.CompilerParams(vmem_limit_bytes=VMEM_LIMIT),
        cost_estimate=pl.CostEstimate(flops=500_000_000, bytes_accessed=4_000_000, transcendentals=0),
        name="lags",
    )(position, offsets, limits, *pieces, table)


def phase_table(bins, lag_count):
    freq = np.arange(bins, dtype=np.int64) + BAND_LO
    phase = freq[:, None] * np.arange(lag_count, dtype=np.int64)[None, :] % lag_count
    angle = (2.0 * math.pi / lag_count * phase).astype(np.float32)
    scale = np.float32(1.0 / math.sqrt(bins))
    rows = [np.cos(angle) * scale, -np.sin(angle) * scale]
    return np.concatenate(rows, axis=0).astype(jnp.bfloat16)


def moves(n):
    every = range(n)
    return dict(
        chip=[(i, i ^ 1) for i in every],
        xs=[(i, i ^ 2) for i in every],
        xd=[(i, i ^ 3) for i in every],
        down=[(i, i - 4) for i in every if i >= 4],
        crossed=[(i, (i - 4) ^ 1) for i in every if i >= 4],
        up=[(i, i + 4) for i in every if i + 4 < n],
    )


def local(spectra, pair_offset, lag_limit):
    n = lax.axis_size("pairs")
    move = {name: functools.partial(lax.ppermute, axis_name="pairs", perm=perm) for name, perm in moves(n).items()}
    index = lax.axis_index("pairs")
    core, x = index % 2, index // 2 % 2
    position = jnp.stack([core, x]).astype(jnp.int32)
    table = jnp.asarray(phase_table(spectra.shape[4], 2 * spectra.shape[4]))

    theirs, side_raw, up_raw, down_raw = quarters(position, spectra)
    got = move["chip"](theirs)
    side0 = move["xs"](side_raw)
    up0 = move["up"](up_raw)
    down0 = move["down"](down_raw)
    got_p, got_q, got_side = whiten_got(position, got)
    side1 = move["xs"](got_side)
    up1 = move["up"](got_q)
    down1 = move["down"](got_p)
    mine_p, mine_q = whiten_blocks(down_raw, up_raw)
    side0, up0, down0 = whiten_blocks(side0, up0, down0)

    own = (mine_p, got_p, mine_q, got_q)
    pair_here, pair_chip = cross(chip_kernel, (2, 2), position, *own)
    pair_chip = move["chip"](pair_chip)

    zs, zd, near_here, near_chip = cross(
        back_kernel, (4, 4, 2, 2), position, *own, up0, up1, side0, side1
    )
    xs, xd = cross(
        near_kernel, (2, 2), position, mine_q, got_q, down0, down1, side0, side1, after=(zd,)
    )
    far_here, far_chip = cross(
        far_kernel, (2, 2), position, mine_p, got_p, down0, down1, after=(xd,)
    )
    zs = move["down"](zs)
    zd = move["crossed"](zd)
    near_chip = move["chip"](near_chip)
    xs = move["xs"](xs)
    xd = move["xd"](xd)
    far_chip = move["chip"](far_chip)
    sides = ((pair_here, near_here, far_here, xs, zs), (pair_chip, near_chip, far_chip, xd, zd))
    return lag_products(position, pair_offset, lag_limit, sides, table)


def solution(mesh):
    in_specs = (
        P(("hours", "pairs"), None, None, None, None),
        P(("hours", "pairs"), None),
        P(("hours", "pairs"), None),
    )
    out_specs = P(("hours", "pairs"), None, None, None)
    return jax.shard_map(local, mesh=mesh, in_specs=in_specs, out_specs=out_specs, check_vma=False)
```

time: 70.6 us -> 59.9 us (0.85)
  waiting for transfers between devices: 30.5 us -> 18.8 us
  Pallas kernels: 17 us -> 18.6 us
  local copies, waits for them, and re-layouts: 3.27 us -> 2.09 us
    ppermute x7 -> x9, waiting for transfers between devices: 19 us -> 7.45 us  [the longest x1 2.69 us: local(): down0 = move['down'](down_raw)]
    ppermute x1, waiting for transfers between devices: 0.01 us -> 4.84 us  [local(): zs = move['down'](zs)]
    ppermute x1, waiting for transfers between devices: 4.83 us -> 0.01 us  [local(): zd = move['crossed'](zd)]
    pallas_call x2 -> x8, Pallas kernels: 13.7 us -> 16.3 us  [the longest x4 6.06 us: cross(): pl.pallas_call(kernel, out_shape=[jax.ShapeDtypeStruct((n, rows, 2 * bins...]
    squeeze x2 -> x0, local copies, waits for them, and re-layouts: 1.65 us -> none  [local(): lax.dynamic_index_in_dim(own, 1 - x, keepdims=False)]
    ppermute x1, waiting for transfers between devices: 4.65 us -> 3.43 us  [local(): xs = move['xs'](xs)]
    ppermute x1, waiting for transfers between devices: 2.02 us -> 3.05 us  [local(): xd = move['xd'](xd)]
    pallas_call x1, Pallas kernels: 3.33 us -> 2.34 us  [lag_products(): pl.pallas_call(lag_kernel, out_shape=jax.ShapeDtypeStruct((1, offsets.sha...]
  transfers between devices with their start and end apart: 12 -> 14, of which waited for: 9 -> 7; matrix products, arithmetic and copies ran while one was open for 2% -> 0% of each run, Pallas kernels for 0% -> 21%
where the time goes in v2:
time: 59.9 us; the launch traced here: 59.5 us
  starting transfers between devices  19.2 us (32%)
  waiting for transfers between devices  18.8 us (31%)
  Pallas kernels  18.6 us (31%)
  local copies, waits for them, and re-layouts  2.09 us (3%)
  other arithmetic  0.65 us (1%)
    pallas_call x4, Pallas kernels, cross(): pl.pallas_call(kernel, out_shape=[jax.ShapeDtypeStruct((n, rows, 2 * bins...  6.06 us
    ppermute x1, waiting for transfers between devices, local(): zs = move['down'](zs)  4.84 us
    ppermute x1, starting transfers between devices, local(): up1 = move['up'](got_q)  4.58 us
    pallas_call x2, Pallas kernels, whiten_blocks(): pl.pallas_call(whiten_blocks_kernel, out_shape=[jax.ShapeDtypeStruct(bloc...  4.04 us
    pallas_call x1, Pallas kernels, quarters(): pl.pallas_call(quarters_kernel, out_shape=[jax.ShapeDtypeStruct((2,) + sh...  3.95 us
    ppermute x1, starting transfers between devices, local(): up0 = move['up'](up_raw)  3.5 us
    ppermute x1, waiting for transfers between devices, local(): xs = move['xs'](xs)  3.43 us
    ppermute x1, waiting for transfers between devices, local(): xd = move['xd'](xd)  3.05 us
  transfers between devices with their start and end apart: 14, of which 7 were waited for; matrix products, arithmetic and copies ran while one was open for 0% of the time, Pallas kernels for 21%

profile of v2, /device:TPU:0, one launch (start us, length us, event | category | flops | bytes accessed | tf_op | source)
XLA Modules:
  0.0 59.5 jit_solution(7634579255409638905)
XLA Ops:
  0.0 0.6 %pad_add_fusion.position = s32[2]{0:T(128)} fusion(s32[1]{0:T(128)} %bitcast.1, s32[1]{0:T(128)} %bitcast), kind=kLoop, calls=%fused_computation | loop fusion | flops 2 | bytes 16 | tf_op jit(solution)/shard_map/stack | solution.py:326
  0.6 0.0 copy-start.3
  0.6 3.9 %quarters.1 = (bf16[2,2,8,64,256]{4,3,2,1,0:T(8,128)(2,1)}, bf16[2,8,64,256]{3,2,1,0:T(8,128)(2,1)}, bf16[2,8,64,256]{3,2,1,0:T(8,128)(2,1)}, bf16[2,8,64,256]{3,2,1,0:T(8,128)(2,1)}) custom-call(s32[2]{0:T(128)} %pad_add_fusion.position, bf16[1,2,8,256,256]{4,3,2,1,0:T(8,128)(2,1)} %spectra.1), custom_call_target="tpu_custom_call" | custom-call | flops 1000 | bytes 1000 | tf_op jit(solution)/shard_map/quarters/pallas_call | solution.py:56
  4.6 0.5 collective-permute-start
  5.1 2.6 %collective-permute-start.1 = (bf16[2,8,64,256]{3,2,1,0:T(8,128)(2,1)}, bf16[2,8,64,256]{3,2,1,0:T(8,128)(2,1)S(1)}, u32[]{:S(2)}, u32[]{:S(2)}) collective-permute-start(bf16[2,8,64,256]{3,2,1,0:T(8,128)(2,1)} %get-tuple-element.35), channel_id=1, source_target_pairs={{0,2},{1,3},{2,0},{3,1},{4,6},{5,7},{6,4},{7,5},{8,10},{9,11},{10,... | collective-permute-start | bytes 1572872 | tf_op jit(solution)/shard_map/ppermute | solution.py:331
  7.7 3.5 %collective-permute-start.2 = (bf16[2,8,64,256]{3,2,1,0:T(8,128)(2,1)}, bf16[2,8,64,256]{3,2,1,0:T(8,128)(2,1)S(1)}, u32[]{:S(2)}, u32[]{:S(2)}) collective-permute-start(bf16[2,8,64,256]{3,2,1,0:T(8,128)(2,1)} %get-tuple-element.28.refs_1_), channel_id=1, source_target_pairs={{0,4},{1,5},{2,6},{3,7},{4,8},{5,9},{6,10},{7,11},{8,12},{9,13},{1... | collective-permute-start | bytes 1572872 | tf_op jit(solution)/shard_map/ppermute | solution.py:332
  11.2 1.3 %collective-permute-start.3 = (bf16[2,8,64,256]{3,2,1,0:T(8,128)(2,1)}, bf16[2,8,64,256]{3,2,1,0:T(8,128)(2,1)S(1)}, u32[]{:S(2)}, u32[]{:S(2)}) collective-permute-start(bf16[2,8,64,256]{3,2,1,0:T(8,128)(2,1)} %get-tuple-element.27.refs_0_), channel_id=1, source_target_pairs={{4,0},{5,1},{6,2},{7,3},{8,4},{9,5},{10,6},{11,7},{12,8},{13,9},{1... | collective-permute-start | bytes 1572872 | tf_op jit(solution)/shard_map/ppermute | solution.py:333
  12.5 0.0 collective-permute-done.got
  12.5 0.0 copy-done.3
  12.5 2.2 %whiten_got.1 = (bf16[2,8,64,256]{3,2,1,0:T(8,128)(2,1)S(1)}, bf16[2,8,64,256]{3,2,1,0:T(8,128)(2,1)S(1)}, bf16[2,8,64,256]{3,2,1,0:T(8,128)(2,1)S(1)}) custom-call(s32[2]{0:T(128)S(1)} %copy-done.3, bf16[2,2,8,64,256]{4,3,2,1,0:T(8,128)(2,1)S(1)} %collective-permute-done.got), custom_call_target="tpu_custom_call" | custom-call | flops 3000000 | bytes 3000000 | tf_op jit(solution)/shard_map/whiten_got/pallas_call | solution.py:92
  14.7 4.6 %collective-permute-start.4 = (bf16[2,8,64,256]{3,2,1,0:T(8,128)(2,1)S(1)}, bf16[2,8,64,256]{3,2,1,0:T(8,128)(2,1)S(1)}, u32[]{:S(2)}, u32[]{:S(2)}) collective-permute-start(bf16[2,8,64,256]{3,2,1,0:T(8,128)(2,1)S(1)} %get-tuple-element.33.got_q), channel_id=1, source_target_pairs={{0,4},{1,5},{2,6},{3,7},{4,8},{5,9},{6,10},{7,11},{8,12},{9,13},{1... | collective-permute-start | bytes 1572872 | tf_op jit(solution)/shard_map/ppermute | solution.py:336
  19.3 0.6 collective-permute-start.5
  19.9 0.5 collective-permute-done.1.refs_0_
  20.4 1.3 %collective-permute-start.6 = (bf16[2,8,64,256]{3,2,1,0:T(8,128)(2,1)S(1)}, bf16[2,8,64,256]{3,2,1,0:T(8,128)(2,1)S(1)}, u32[]{:S(2)}, u32[]{:S(2)}) collective-permute-start(bf16[2,8,64,256]{3,2,1,0:T(8,128)(2,1)S(1)} %get-tuple-element.31.got_p), channel_id=1, source_target_pairs={{4,0},{5,1},{6,2},{7,3},{8,4},{9,5},{10,6},{11,7},{12,8},{13,9},{1... | collective-permute-start | bytes 1572872 | tf_op jit(solution)/shard_map/ppermute | solution.py:337
  21.7 0.0 copy-start.1
  21.7 1.0 %copy-done.1 = bf16[2,8,64,256]{3,2,1,0:T(8,128)(2,1)S(1)} copy-done((bf16[2,8,64,256]{3,2,1,0:T(8,128)(2,1)S(1)}, bf16[2,8,64,256]{3,2,1,0:T(8,128)(2,1)}, u32[]{:S(2)}) %copy-start.1) | copy-done | bytes 524312
  22.8 0.0 copy-start.2
  22.8 1.0 %copy-done.2 = bf16[2,8,64,256]{3,2,1,0:T(8,128)(2,1)S(1)} copy-done((bf16[2,8,64,256]{3,2,1,0:T(8,128)(2,1)S(1)}, bf16[2,8,64,256]{3,2,1,0:T(8,128)(2,1)}, u32[]{:S(2)}) %copy-start.2) | copy-done | bytes 524312
  23.8 1.6 %whiten_blocks.2 = (bf16[2,8,64,256]{3,2,1,0:T(8,128)(2,1)S(1)}, bf16[2,8,64,256]{3,2,1,0:T(8,128)(2,1)S(1)}) custom-call(bf16[2,8,64,256]{3,2,1,0:T(8,128)(2,1)S(1)} %copy-done.1, bf16[2,8,64,256]{3,2,1,0:T(8,128)(2,1)S(1)} %copy-done.2), custom_call_target="tpu_custom_call" | custom-call | flops 3000000 | bytes 3000000 | tf_op jit(solution)/shard_map/whiten_blocks/pallas_call | solution.py:118
  25.4 0.0 collective-permute-done.2.refs_1_
  25.4 2.7 %collective-permute-done.3.refs_2_ = bf16[2,8,64,256]{3,2,1,0:T(8,128)(2,1)S(1)} collective-permute-done((bf16[2,8,64,256]{3,2,1,0:T(8,128)(2,1)}, bf16[2,8,64,256]{3,2,1,0:T(8,128)(2,1)S(1)}, u32[]{:S(2)}, u32[]{:S(2)}) %collective-permute-start.3) | collective-permute-done | bytes 524320 | tf_op jit(solution)/shard_map/ppermute | solution.py:333
  28.1 2.4 %whiten_blocks.3 = (bf16[2,8,64,256]{3,2,1,0:T(8,128)(2,1)S(1)}, bf16[2,8,64,256]{3,2,1,0:T(8,128)(2,1)S(1)}, bf16[2,8,64,256]{3,2,1,0:T(8,128)(2,1)S(1)}) custom-call(bf16[2,8,64,256]{3,2,1,0:T(8,128)(2,1)S(1)} %collective-permute-done.1.refs_0_, bf16[2,8,64,256]{3,2,1,0:T(8,128)(2,1)S(1)} %collective-permute-done.2.refs_1_, ...), custom_call_target="tpu_custom_call" | custom-call | flops 3000000 | bytes 3000000 | tf_op jit(solution)/shard_map/whiten_blocks/pallas_call | solution.py:118
  30.5 1.3 %chip_kernel.1 = (bf16[2,64,512]{2,1,0:T(8,128)(2,1)S(1)}, bf16[2,64,512]{2,1,0:T(8,128)(2,1)S(1)}) custom-call(s32[2]{0:T(128)S(1)} %copy-done.3, bf16[2,8,64,256]{3,2,1,0:T(8,128)(2,1)S(1)} %get-tuple-element.29.mine_p, bf16[2,8,64,256]{3,2,1,0:T(8,128)(2,1)S(1)} %get-tuple-element.31.got_p, bf16[2,8,64,256]{3,2,1,0:T(8,128)(2,1)S(1)} %get-tuple-element.32.mine_q, ...), custom_call_target="tpu_custom_call" | custom-call | flops 10000000 | bytes 5000000 | tf_op jit(solution)/shard_map/chip_kernel/pallas_call | solution.py:233
  31.8 0.1 collective-permute-start.9
  31.9 2.2 %collective-permute-done.4.up1 = bf16[2,8,64,256]{3,2,1,0:T(8,128)(2,1)S(1)} collective-permute-done((bf16[2,8,64,256]{3,2,1,0:T(8,128)(2,1)S(1)}, bf16[2,8,64,256]{3,2,1,0:T(8,128)(2,1)S(1)}, u32[]{:S(2)}, u32[]{:S(2)}) %collective-permute-start.4) | collective-permute-done | bytes 524320 | tf_op jit(solution)/shard_map/ppermute | solution.py:336
  34.1 0.0 collective-permute-done.5.side1
  34.1 2.1 %back_kernel.1 = (bf16[4,64,512]{2,1,0:T(8,128)(2,1)S(1)}, bf16[4,64,512]{2,1,0:T(8,128)(2,1)S(1)}, bf16[2,64,512]{2,1,0:T(8,128)(2,1)S(1)}, bf16[2,64,512]{2,1,0:T(8,128)(2,1)S(1)}) custom-call(s32[2]{0:T(128)S(1)} %copy-done.3, bf16[2,8,64,256]{3,2,1,0:T(8,128)(2,1)S(1)} %get-tuple-element.29.mine_p, bf16[2,8,64,256]{3,2,1,0:T(8,128)(2,1)S(1)} %get-tuple-element.31.got_p, ...), custom_call_target="tpu_custom_call" | custom-call | flops 10000000 | bytes 5000000 | tf_op jit(solution)/shard_map/back_kernel/pallas_call | solution.py:233
  36.3 2.0 %collective-permute-done.6.down1 = bf16[2,8,64,256]{3,2,1,0:T(8,128)(2,1)S(1)} collective-permute-done((bf16[2,8,64,256]{3,2,1,0:T(8,128)(2,1)S(1)}, bf16[2,8,64,256]{3,2,1,0:T(8,128)(2,1)S(1)}, u32[]{:S(2)}, u32[]{:S(2)}) %collective-permute-start.6) | collective-permute-done | bytes 524320 | tf_op jit(solution)/shard_map/ppermute | solution.py:337
  38.3 0.0 copy-start
  38.3 0.0 copy-start.4
  38.3 0.0 copy-start.5
  38.3 1.3 %near_kernel.1 = (bf16[2,64,512]{2,1,0:T(8,128)(2,1)S(1)}, bf16[2,64,512]{2,1,0:T(8,128)(2,1)S(1)}) custom-call(s32[2]{0:T(128)S(1)} %copy-done.3, bf16[2,8,64,256]{3,2,1,0:T(8,128)(2,1)S(1)} %get-tuple-element.32.mine_q, bf16[2,8,64,256]{3,2,1,0:T(8,128)(2,1)S(1)} %get-tuple-element.33.got_q, bf16[2,8,64,256]{3,2,1,0:T(8,128)(2,1)S(1)} %get-tuple-element.40.down0, ...), custom_call_target="tpu_custom_call" | custom-call | flops 10000000 | bytes 5000000 | tf_op jit(solution)/shard_map/near_kernel/pallas_call | solution.py:233
  39.6 1.3 %far_kernel.1 = (bf16[2,64,512]{2,1,0:T(8,128)(2,1)S(1)}, bf16[2,64,512]{2,1,0:T(8,128)(2,1)S(1)}) custom-call(s32[2]{0:T(128)S(1)} %copy-done.3, bf16[2,8,64,256]{3,2,1,0:T(8,128)(2,1)S(1)} %get-tuple-element.29.mine_p, bf16[2,8,64,256]{3,2,1,0:T(8,128)(2,1)S(1)} %get-tuple-element.31.got_p, bf16[2,8,64,256]{3,2,1,0:T(8,128)(2,1)S(1)} %get-tuple-element.40.down0, ...), custom_call_target="tpu_custom_call" | custom-call | flops 10000000 | bytes 5000000 | tf_op jit(solution)/shard_map/far_kernel/pallas_call | solution.py:233
  41.0 0.1 collective-permute-start.11
  41.0 1.3 %collective-permute-start.13 = (bf16[4,64,512]{2,1,0:T(8,128)(2,1)S(1)}, bf16[4,64,512]{2,1,0:T(8,128)(2,1)S(1)}, u32[]{:S(2)}, u32[]{:S(2)}) collective-permute-start(bf16[4,64,512]{2,1,0:T(8,128)(2,1)S(1)} %get-tuple-element.41.after), channel_id=1, source_target_pairs={{4,1},{5,0},{6,3},{7,2},{8,5},{9,4},{10,7},{11,6},{12,9},{13,8},{1... | collective-permute-start | bytes 786440 | tf_op jit(solution)/shard_map/ppermute | solution.py:355
  42.3 1.3 %collective-permute-start.8 = (bf16[4,64,512]{2,1,0:T(8,128)(2,1)S(1)}, bf16[4,64,512]{2,1,0:T(8,128)(2,1)S(1)}, u32[]{:S(2)}, u32[]{:S(2)}) collective-permute-start(bf16[4,64,512]{2,1,0:T(8,128)(2,1)S(1)} %get-tuple-element.45), channel_id=1, source_target_pairs={{4,0},{5,1},{6,2},{7,3},{8,4},{9,5},{10,6},{11,7},{12,8},{13,9},{1... | collective-permute-start | bytes 786440 | tf_op jit(solution)/shard_map/ppermute | solution.py:354
  43.6 0.7 %collective-permute-start.12 = (bf16[2,64,512]{2,1,0:T(8,128)(2,1)S(1)}, bf16[2,64,512]{2,1,0:T(8,128)(2,1)S(1)}, u32[]{:S(2)}, u32[]{:S(2)}) collective-permute-start(bf16[2,64,512]{2,1,0:T(8,128)(2,1)S(1)} %get-tuple-element.42.after), channel_id=1, source_target_pairs={{0,3},{1,2},{2,1},{3,0},{4,7},{5,6},{6,5},{7,4},{8,11},{9,10},{10,... | collective-permute-start | bytes 393224 | tf_op jit(solution)/shard_map/ppermute | solution.py:358
  44.3 0.0 collective-permute-done.9.refs_5_
  44.3 1.5 %collective-permute-start.7 = (bf16[2,64,512]{2,1,0:T(8,128)(2,1)S(1)}, bf16[2,64,512]{2,1,0:T(8,128)(2,1)S(1)}, u32[]{:S(2)}, u32[]{:S(2)}) collective-permute-start(bf16[2,64,512]{2,1,0:T(8,128)(2,1)S(1)} %get-tuple-element.44), channel_id=1, source_target_pairs={{0,2},{1,3},{2,0},{3,1},{4,6},{5,7},{6,4},{7,5},{8,10},{9,11},{10,... | collective-permute-start | bytes 393224 | tf_op jit(solution)/shard_map/ppermute | solution.py:357
  45.8 0.0 collective-permute-done.11.refs_7_
  45.8 0.0 collective-permute-start.10
  45.8 3.1 %collective-permute-done.12.refs_8_ = bf16[2,64,512]{2,1,0:T(8,128)(2,1)S(1)} collective-permute-done((bf16[2,64,512]{2,1,0:T(8,128)(2,1)S(1)}, bf16[2,64,512]{2,1,0:T(8,128)(2,1)S(1)}, u32[]{:S(2)}, u32[]{:S(2)}) %collective-permute-start.12) | collective-permute-done | bytes 131104 | tf_op jit(solution)/shard_map/ppermute | solution.py:358
  48.9 3.4 %collective-permute-done.7.refs_3_ = bf16[2,64,512]{2,1,0:T(8,128)(2,1)S(1)} collective-permute-done((bf16[2,64,512]{2,1,0:T(8,128)(2,1)S(1)}, bf16[2,64,512]{2,1,0:T(8,128)(2,1)S(1)}, u32[]{:S(2)}, u32[]{:S(2)}) %collective-permute-start.7) | collective-permute-done | bytes 131104 | tf_op jit(solution)/shard_map/ppermute | solution.py:357
  52.3 0.0 collective-permute-done.10.refs_6_
  52.3 0.0 collective-permute-done.13.refs_9_
  52.3 4.8 %collective-permute-done.8.refs_4_ = bf16[4,64,512]{2,1,0:T(8,128)(2,1)S(1)} collective-permute-done((bf16[4,64,512]{2,1,0:T(8,128)(2,1)S(1)}, bf16[4,64,512]{2,1,0:T(8,128)(2,1)S(1)}, u32[]{:S(2)}, u32[]{:S(2)}) %collective-permute-start.8) | collective-permute-done | bytes 262176 | tf_op jit(solution)/shard_map/ppermute | solution.py:354
  57.2 0.0 copy-done
  57.2 0.0 copy-done.4
  57.2 0.0 copy-done.5
  57.2 2.3 %lags.1 = bf16[1,4,256,512]{3,2,1,0:T(8,128)(2,1)} custom-call(s32[2]{0:T(128)S(1)} %copy-done.3, s32[1,4]{1,0:T(1,128)S(1)} %copy-done.4, s32[1,4]{1,0:T(1,128)S(1)} %copy-done.5, bf16[2,64,512]{2,1,0:T(8,128)(2,1)S(1)} %get-tuple-element.34.refs_0_, bf16[2,64,512]{2,1,0:T(8,128)(2,1)S(1)} %get-tuple-element.39.refs_1_, ...), custom_call_target="tpu_custom_call" | custom-call | flops 500000000 | bytes 4000000 | tf_op jit(solution)/shard_map/lags/pallas_call | solution.py:288
Async XLA Ops:
  0.6 11.9 %copy-start.3 = (s32[2]{0:T(128)S(1)}, s32[2]{0:T(128)}, u32[]{:S(2)}) copy-start(s32[2]{0:T(128)} %pad_add_fusion.position) | copy-start | bytes 28
  4.6 7.9 %collective-permute-start = (bf16[2,2,8,64,256]{4,3,2,1,0:T(8,128)(2,1)}, bf16[2,2,8,64,256]{4,3,2,1,0:T(8,128)(2,1)S(1)}, u32[]{:S(2)}, u32[]{:S(2)}) collective-permute-start(bf16[2,2,8,64,256]{4,3,2,1,0:T(8,128)(2,1)} %get-tuple-element.30), channel_id=1, source_target_pairs={{0,1},{1,0},{2,3},{3,2},{4,5},{5,4},{6,7},{7,6},{8,9},{9,8},{10,11... | collective-permute-start | bytes 3145736 | tf_op jit(solution)/shard_map/ppermute | solution.py:330
  5.1 15.3 %collective-permute-start.1 = (bf16[2,8,64,256]{3,2,1,0:T(8,128)(2,1)}, bf16[2,8,64,256]{3,2,1,0:T(8,128)(2,1)S(1)}, u32[]{:S(2)}, u32[]{:S(2)}) collective-permute-start(bf16[2,8,64,256]{3,2,1,0:T(8,128)(2,1)} %get-tuple-element.35), channel_id=1, source_target_pairs={{0,2},{1,3},{2,0},{3,1},{4,6},{5,7},{6,4},{7,5},{8,10},{9,11},{10,... | collective-permute-start | bytes 1572872 | tf_op jit(solution)/shard_map/ppermute | solution.py:331
  7.7 17.7 %collective-permute-start.2 = (bf16[2,8,64,256]{3,2,1,0:T(8,128)(2,1)}, bf16[2,8,64,256]{3,2,1,0:T(8,128)(2,1)S(1)}, u32[]{:S(2)}, u32[]{:S(2)}) collective-permute-start(bf16[2,8,64,256]{3,2,1,0:T(8,128)(2,1)} %get-tuple-element.28.refs_1_), channel_id=1, source_target_pairs={{0,4},{1,5},{2,6},{3,7},{4,8},{5,9},{6,10},{7,11},{8,12},{9,13},{1... | collective-permute-start | bytes 1572872 | tf_op jit(solution)/shard_map/ppermute | solution.py:332
  11.2 16.9 %collective-permute-start.3 = (bf16[2,8,64,256]{3,2,1,0:T(8,128)(2,1)}, bf16[2,8,64,256]{3,2,1,0:T(8,128)(2,1)S(1)}, u32[]{:S(2)}, u32[]{:S(2)}) collective-permute-start(bf16[2,8,64,256]{3,2,1,0:T(8,128)(2,1)} %get-tuple-element.27.refs_0_), channel_id=1, source_target_pairs={{4,0},{5,1},{6,2},{7,3},{8,4},{9,5},{10,6},{11,7},{12,8},{13,9},{1... | collective-permute-start | bytes 1572872 | tf_op jit(solution)/shard_map/ppermute | solution.py:333
  14.7 19.4 %collective-permute-start.4 = (bf16[2,8,64,256]{3,2,1,0:T(8,128)(2,1)S(1)}, bf16[2,8,64,256]{3,2,1,0:T(8,128)(2,1)S(1)}, u32[]{:S(2)}, u32[]{:S(2)}) collective-permute-start(bf16[2,8,64,256]{3,2,1,0:T(8,128)(2,1)S(1)} %get-tuple-element.33.got_q), channel_id=1, source_target_pairs={{0,4},{1,5},{2,6},{3,7},{4,8},{5,9},{6,10},{7,11},{8,12},{9,13},{1... | collective-permute-start | bytes 1572872 | tf_op jit(solution)/shard_map/ppermute | solution.py:336
  19.3 14.8 %collective-permute-start.5 = (bf16[2,8,64,256]{3,2,1,0:T(8,128)(2,1)S(1)}, bf16[2,8,64,256]{3,2,1,0:T(8,128)(2,1)S(1)}, u32[]{:S(2)}, u32[]{:S(2)}) collective-permute-start(bf16[2,8,64,256]{3,2,1,0:T(8,128)(2,1)S(1)} %get-tuple-element.38), channel_id=1, source_target_pairs={{0,2},{1,3},{2,0},{3,1},{4,6},{5,7},{6,4},{7,5},{8,10},{9,11},{10,... | collective-permute-start | bytes 1572872 | tf_op jit(solution)/shard_map/ppermute | solution.py:335
  20.4 17.8 %collective-permute-start.6 = (bf16[2,8,64,256]{3,2,1,0:T(8,128)(2,1)S(1)}, bf16[2,8,64,256]{3,2,1,0:T(8,128)(2,1)S(1)}, u32[]{:S(2)}, u32[]{:S(2)}) collective-permute-start(bf16[2,8,64,256]{3,2,1,0:T(8,128)(2,1)S(1)} %get-tuple-element.31.got_p), channel_id=1, source_target_pairs={{4,0},{5,1},{6,2},{7,3},{8,4},{9,5},{10,6},{11,7},{12,8},{13,9},{1... | collective-permute-start | bytes 1572872 | tf_op jit(solution)/shard_map/ppermute | solution.py:337
  21.7 1.0 %copy-start.1 = (bf16[2,8,64,256]{3,2,1,0:T(8,128)(2,1)S(1)}, bf16[2,8,64,256]{3,2,1,0:T(8,128)(2,1)}, u32[]{:S(2)}) copy-start(bf16[2,8,64,256]{3,2,1,0:T(8,128)(2,1)} %get-tuple-element.27.refs_0_) | copy-start | bytes 1572868
  22.8 1.0 %copy-start.2 = (bf16[2,8,64,256]{3,2,1,0:T(8,128)(2,1)S(1)}, bf16[2,8,64,256]{3,2,1,0:T(8,128)(2,1)}, u32[]{:S(2)}) copy-start(bf16[2,8,64,256]{3,2,1,0:T(8,128)(2,1)} %get-tuple-element.28.refs_1_) | copy-start | bytes 1572868
  31.8 12.5 %collective-permute-start.9 = (bf16[2,64,512]{2,1,0:T(8,128)(2,1)S(1)}, bf16[2,64,512]{2,1,0:T(8,128)(2,1)S(1)}, u32[]{:S(2)}, u32[]{:S(2)}) collective-permute-start(bf16[2,64,512]{2,1,0:T(8,128)(2,1)S(1)} %get-tuple-element.46), channel_id=1, source_target_pairs={{0,1},{1,0},{2,3},{3,2},{4,5},{5,4},{6,7},{7,6},{8,9},{9,8},{10,11... | collective-permute-start | bytes 393224 | tf_op jit(solution)/shard_map/ppermute | solution.py:343
  38.3 18.9 %copy-start = (bf16[512,512]{1,0:T(8,128)(2,1)S(1)}, bf16[512,512]{1,0:T(8,128)(2,1)}, u32[]{:S(2)}) copy-start(bf16[512,512]{1,0:T(8,128)(2,1)} %constant.34.clone.refs_10_) | copy-start | bytes 1572868
  38.3 18.9 %copy-start.4 = (s32[1,4]{1,0:T(1,128)S(1)}, s32[1,4]{1,0:T(1,128)}, u32[]{:S(2)}) copy-start(s32[1,4]{1,0:T(1,128)} %offsets.1) | copy-start | bytes 52
  38.3 18.9 %copy-start.5 = (s32[1,4]{1,0:T(1,128)S(1)}, s32[1,4]{1,0:T(1,128)}, u32[]{:S(2)}) copy-start(s32[1,4]{1,0:T(1,128)} %limits.1) | copy-start | bytes 52
  41.0 4.9 %collective-permute-start.11 = (bf16[2,64,512]{2,1,0:T(8,128)(2,1)S(1)}, bf16[2,64,512]{2,1,0:T(8,128)(2,1)S(1)}, u32[]{:S(2)}, u32[]{:S(2)}) collective-permute-start(bf16[2,64,512]{2,1,0:T(8,128)(2,1)S(1)} %get-tuple-element.48), channel_id=1, source_target_pairs={{0,1},{1,0},{2,3},{3,2},{4,5},{5,4},{6,7},{7,6},{8,9},{9,8},{10,11... | collective-permute-start | bytes 393224 | tf_op jit(solution)/shard_map/ppermute | solution.py:359
  41.0 11.3 %collective-permute-start.13 = (bf16[4,64,512]{2,1,0:T(8,128)(2,1)S(1)}, bf16[4,64,512]{2,1,0:T(8,128)(2,1)S(1)}, u32[]{:S(2)}, u32[]{:S(2)}) collective-permute-start(bf16[4,64,512]{2,1,0:T(8,128)(2,1)S(1)} %get-tuple-element.41.after), channel_id=1, source_target_pairs={{4,1},{5,0},{6,3},{7,2},{8,5},{9,4},{10,7},{11,6},{12,9},{13,8},{1... | collective-permute-start | bytes 786440 | tf_op jit(solution)/shard_map/ppermute | solution.py:355
  42.3 14.8 %collective-permute-start.8 = (bf16[4,64,512]{2,1,0:T(8,128)(2,1)S(1)}, bf16[4,64,512]{2,1,0:T(8,128)(2,1)S(1)}, u32[]{:S(2)}, u32[]{:S(2)}) collective-permute-start(bf16[4,64,512]{2,1,0:T(8,128)(2,1)S(1)} %get-tuple-element.45), channel_id=1, source_target_pairs={{4,0},{5,1},{6,2},{7,3},{8,4},{9,5},{10,6},{11,7},{12,8},{13,9},{1... | collective-permute-start | bytes 786440 | tf_op jit(solution)/shard_map/ppermute | solution.py:354
  43.6 5.2 %collective-permute-start.12 = (bf16[2,64,512]{2,1,0:T(8,128)(2,1)S(1)}, bf16[2,64,512]{2,1,0:T(8,128)(2,1)S(1)}, u32[]{:S(2)}, u32[]{:S(2)}) collective-permute-start(bf16[2,64,512]{2,1,0:T(8,128)(2,1)S(1)} %get-tuple-element.42.after), channel_id=1, source_target_pairs={{0,3},{1,2},{2,1},{3,0},{4,7},{5,6},{6,5},{7,4},{8,11},{9,10},{10,... | collective-permute-start | bytes 393224 | tf_op jit(solution)/shard_map/ppermute | solution.py:358
  44.3 8.0 %collective-permute-start.7 = (bf16[2,64,512]{2,1,0:T(8,128)(2,1)S(1)}, bf16[2,64,512]{2,1,0:T(8,128)(2,1)S(1)}, u32[]{:S(2)}, u32[]{:S(2)}) collective-permute-start(bf16[2,64,512]{2,1,0:T(8,128)(2,1)S(1)} %get-tuple-element.44), channel_id=1, source_target_pairs={{0,2},{1,3},{2,0},{3,1},{4,6},{5,7},{6,4},{7,5},{8,10},{9,11},{10,... | collective-permute-start | bytes 393224 | tf_op jit(solution)/shard_map/ppermute | solution.py:357
  45.8 6.5 %collective-permute-start.10 = (bf16[2,64,512]{2,1,0:T(8,128)(2,1)S(1)}, bf16[2,64,512]{2,1,0:T(8,128)(2,1)S(1)}, u32[]{:S(2)}, u32[]{:S(2)}) collective-permute-start(bf16[2,64,512]{2,1,0:T(8,128)(2,1)S(1)} %get-tuple-element.47), channel_id=1, source_target_pairs={{0,1},{1,0},{2,3},{3,2},{4,5},{5,4},{6,7},{7,6},{8,9},{9,8},{10,11... | collective-permute-start | bytes 393224 | tf_op jit(solution)/shard_map/ppermute | solution.py:356

commit v3 on v2

v3 whole, which is shorter than its diff:
```python
import functools
import math

import jax
import jax.numpy as jnp
import numpy as np
from jax import lax
from jax.experimental import pallas as pl
from jax.experimental.pallas import tpu as pltpu
from jax.sharding import PartitionSpec as P

BAND_LO = 16
TILE = 16
LANES = 128
VMEM_LIMIT = 16 * 1024 * 1024
VMEM_ALL = 16 * 1024 * 1024
WHITEN_TILE = 16

SMALL = pl.CostEstimate(flops=1000, bytes_accessed=1000, transcendentals=0)
LARGE = pl.CostEstimate(flops=10_000_000_000, bytes_accessed=40_000_000, transcendentals=0)
OUT_SPACE = pl.ANY


def whiten_rows(read, write, windows, rows):
    def one_window(w, _):
        for row in range(0, rows, WHITEN_TILE):
            block = pl.ds(row, WHITEN_TILE)
            values = read(w, block).astype(jnp.float32)
            power = jnp.sum(jnp.sum(values * values, axis=0), axis=-1, keepdims=True)
            power = power / (values.shape[0] * values.shape[-1])
            write(w, block, (values * lax.rsqrt(power + 1e-06)).astype(jnp.bfloat16))
        return 0

    lax.fori_loop(0, windows, one_window, 0)


def place():
    index = lax.axis_index("pairs")
    return lax.rem(index, 2), lax.rem(lax.div(index, 2), 2)


def quarters_kernel(spectra, theirs, side, up, down, sent):
    rows = side.shape[2]
    core, x = place()
    copies = []
    for k, half, target in (
        (0, core, down),
        (1, core, up),
        (1 - x, core, side),
        (0, 1 - core, theirs.at[0]),
        (1, 1 - core, theirs.at[1]),
    ):
        base = pl.multiple_of((2 * k + half) * rows, rows)
        source = spectra.at[0, :, :, pl.ds(base, rows), :]
        copies.append(pltpu.make_async_copy(source, target, sent.at[len(copies)]))
    for copy in copies:
        copy.start()
    for copy in copies:
        copy.wait()


def quarters(spectra):
    parts, windows, channels, bins = spectra.shape[1:]
    shape = (parts, windows, channels // 4, bins)
    return pl.pallas_call(
        quarters_kernel,
        out_shape=[jax.ShapeDtypeStruct((2,) + shape, jnp.bfloat16)]
        + [jax.ShapeDtypeStruct(shape, jnp.bfloat16)] * 3,
        in_specs=[pl.BlockSpec(memory_space=pl.ANY)],
        out_specs=[pl.BlockSpec(memory_space=OUT_SPACE)] * 4,
        scratch_shapes=[pltpu.SemaphoreType.DMA((5,))],
        compiler_params=pltpu.CompilerParams(vmem_limit_bytes=VMEM_ALL),
        cost_estimate=SMALL,
        name="quarters",
    )(spectra)


def whiten_got_kernel(got, p_out, q_out, side_out):
    windows, rows = got.shape[2], got.shape[3]
    _, x = place()
    for k, target in ((0, p_out), (1, q_out)):

        def read(w, block):
            return got[k, :, w, block, :]

        def write(w, block, values):
            target[:, w, block, :] = values

        whiten_rows(read, write, windows, rows)

    @pl.when(x == 0)
    def _():
        side_out[...] = q_out[...]

    @pl.when(x == 1)
    def _():
        side_out[...] = p_out[...]


def whiten_got(got):
    vmem = pl.BlockSpec(memory_space=pltpu.VMEM)
    return pl.pallas_call(
        whiten_got_kernel,
        out_shape=[jax.ShapeDtypeStruct(got.shape[1:], jnp.bfloat16)] * 3,
        in_specs=[vmem],
        out_specs=[vmem] * 3,
        compiler_params=pltpu.CompilerParams(vmem_limit_bytes=VMEM_LIMIT),
        cost_estimate=SMALL,
        name="whiten_got",
    )(got)


def whiten_block_kernel(source, *rest):
    target = rest[-1]

    def read(w, block):
        return source[:, w, block, :]

    def write(w, block, values):
        target[:, w, block, :] = values

    whiten_rows(read, write, source.shape[1], source.shape[2])


def whiten_block(block, after=None):
    vmem = pl.BlockSpec(memory_space=pltpu.VMEM)
    extra = [] if after is None else [after]
    return pl.pallas_call(
        whiten_block_kernel,
        out_shape=jax.ShapeDtypeStruct(block.shape, jnp.bfloat16),
        in_specs=[vmem] + [pl.BlockSpec(memory_space=pl.ANY)] * len(extra),
        out_specs=vmem,
        compiler_params=pltpu.CompilerParams(vmem_limit_bytes=VMEM_LIMIT),
        cost_estimate=SMALL,
        name="whiten_block",
    )(block, *extra)


def products(first, second, stores, rows, bins, windows):
    def one_tile(step, _):
        row = pl.multiple_of(step * TILE, TILE)
        for lane in range(0, bins, LANES):
            reals = [[0.0] * len(second) for _ in first]
            imags = [[0.0] * len(second) for _ in first]
            for w in range(windows):
                a = [[f(part, w, row, lane) for part in range(2)] for f in first]
                b = [[f(part, w, row, lane) for part in range(2)] for f in second]
                for i, (ar, ai) in enumerate(a):
                    for j, (br, bi) in enumerate(b):
                        if not stores[i][j]:
                            continue
                        reals[i][j] = reals[i][j] + (ar * br + ai * bi)
                        imags[i][j] = imags[i][j] + (ar * bi - ai * br)
            for i in range(len(first)):
                for j in range(len(second)):
                    for ref, spot in stores[i][j]:
                        scale = 1.0 / windows
                        ref[spot, pl.ds(row, TILE), pl.ds(lane, LANES)] = (
                            reals[i][j] * scale
                        ).astype(jnp.bfloat16)
                        ref[spot, pl.ds(row, TILE), pl.ds(bins + lane, LANES)] = (
                            imags[i][j] * scale
                        ).astype(jnp.bfloat16)
        return 0

    lax.fori_loop(0, rows // TILE, one_tile, 0)


def reader(ref, *lead):
    def read(part, w, row, lane):
        index = lead + (part, w, pl.ds(row, TILE), pl.ds(lane, LANES))
        return ref[index].astype(jnp.float32)

    return read


def spots(core, ref, base):
    return [[(ref, base + core)], [(ref, base + 1 - core)]]


def chip_kernel(mine_p, got_p, mine_q, got_q, pair):
    windows, rows, bins = mine_q.shape[1:]
    core, _ = place()
    run = functools.partial(products, rows=rows, bins=bins, windows=windows)
    for spot, own in enumerate(((mine_p, got_p), (mine_q, got_q))):
        both = [[(pair, spot)]]

        @pl.when(core == 0)
        def _():
            run([reader(own[0])], [reader(own[1])], [both])

        @pl.when(core == 1)
        def _():
            run([reader(own[1])], [reader(own[0])], [both])


def back_kernel(mine_q, got_q, up, side0, side1, after, back):
    windows, rows, bins = mine_q.shape[1:]
    core, x = place()
    run = functools.partial(products, [reader(up)], rows=rows, bins=bins, windows=windows)
    run([reader(mine_q), reader(got_q)], [spots(core, back, 2)])

    @pl.when(x == 1)
    def _():
        run([reader(side0), reader(side1)], [spots(core, back, 0)])


def near_kernel(mine_q, got_q, down0, down1, side0, side1, after, xs, xd):
    windows, rows, bins = mine_q.shape[1:]
    core, x = place()
    side = [reader(side0), reader(side1)]
    stores = [spots(core, xs, 0), spots(core, xd, 0)]
    run = functools.partial(products, side, rows=rows, bins=bins, windows=windows)

    @pl.when(x == 0)
    def _():
        run([reader(down0), reader(down1)], stores)

    @pl.when(x == 1)
    def _():
        run([reader(mine_q), reader(got_q)], stores)


def own_kernel(mine_p, got_p, down0, down1, side0, side1, pair, after, here, chip):
    here[4:6] = pair[...]
    chip[4:6] = pair[...]
    windows, rows, bins = mine_p.shape[1:]
    core, x = place()
    own = [reader(mine_p), reader(got_p)]
    run = functools.partial(products, own, rows=rows, bins=bins, windows=windows)
    run([reader(down0), reader(down1)], [spots(core, here, 2), spots(core, chip, 2)])

    @pl.when(x == 0)
    def _():
        run([reader(side0), reader(side1)], [spots(core, here, 0), spots(core, chip, 0)])


def cross(kernel, counts, *blocks, after=None):
    rows, bins = blocks[0].shape[2:]
    extra = [] if after is None else [after]
    vmem = pl.BlockSpec(memory_space=pltpu.VMEM)
    return pl.pallas_call(
        kernel,
        out_shape=[jax.ShapeDtypeStruct((n, rows, 2 * bins), jnp.bfloat16) for n in counts],
        in_specs=[vmem] * len(blocks) + [pl.BlockSpec(memory_space=pl.ANY)] * len(extra),
        out_specs=[vmem] * len(counts),
        compiler_params=pltpu.CompilerParams(vmem_limit_bytes=VMEM_LIMIT),
        cost_estimate=SMALL,
        name=kernel.__name__,
    )(*blocks, *extra)


def lag_kernel(flip, offsets, limits, own, side, back, table, earlier, out, cand, lagged, sent):
    core, x = place()
    half = core if flip == 0 else 1 - core
    rows, lags = own.shape[1], table.shape[1]
    p_rows, q_rows = pl.ds(0, rows), pl.ds(rows, rows)
    cand[0, p_rows, :] = own[4]
    cand[0, q_rows, :] = own[5]
    cand[3:5, p_rows, :] = own[2:4]
    cand[3:5, q_rows, :] = back[2:4]

    @pl.when(x == 0)
    def _():
        cand[1:3, p_rows, :] = own[0:2]
        cand[1:3, q_rows, :] = side[...]

    @pl.when(x == 1)
    def _():
        cand[1:3, p_rows, :] = side[...]
        cand[1:3, q_rows, :] = back[0:2]

    lag = lax.broadcasted_iota(jnp.int32, (1, lags), 1)
    distance = jnp.minimum(lag, lags - lag)
    copies = []
    for slot in range(out.shape[1]):
        offset = offsets[0, slot]
        product = jnp.dot(
            cand[jnp.clip(offset - 1 + core, 0, 4)],
            table[...],
            preferred_element_type=jnp.float32,
        )
        limit = jnp.where(offset > 0, limits[0, slot], 0)
        lagged[slot] = jnp.where(distance < limit, product, 0.0).astype(jnp.bfloat16)
        for k in range(2):
            target = pl.multiple_of((2 * k + half) * rows, rows)
            copies.append(
                pltpu.make_async_copy(
                    lagged.at[slot, pl.ds(k * rows, rows), :],
                    out.at[0, slot, pl.ds(target, rows), :],
                    sent.at[slot, k],
                )
            )
            copies[-1].start()
    for copy in copies:
        copy.wait()


def lag_products(flip, cost, offsets, limits, pieces, table, earlier):
    rows, width = pieces[0].shape[1:]
    slots, lags = offsets.shape[1], table.shape[1]
    vmem = pl.BlockSpec(memory_space=pltpu.VMEM)
    smem = pl.BlockSpec(memory_space=pltpu.SMEM)
    kernel = functools.partial(lag_kernel, flip)
    extra = [earlier]
    if earlier is None:
        kernel = lambda *refs: lag_kernel(flip, *refs[:6], None, *refs[6:])
        extra = []
    return pl.pallas_call(
        kernel,
        out_shape=jax.ShapeDtypeStruct((1, slots, 4 * rows, lags), jnp.bfloat16),
        in_specs=[smem] * 2 + [vmem] * 4 + [pl.BlockSpec(memory_space=pl.ANY)] * len(extra),
        out_specs=pl.BlockSpec(memory_space=pl.ANY),
        scratch_shapes=[
            pltpu.VMEM((5, 2 * rows, width), jnp.bfloat16),
            pltpu.VMEM((slots, 2 * rows, lags), jnp.bfloat16),
            pltpu.SemaphoreType.DMA((slots, 2)),
        ],
        input_output_aliases={6: 0} if extra else {},
        compiler_params=pltpu.CompilerParams(vmem_limit_bytes=VMEM_LIMIT),
        cost_estimate=cost,
        name="lags",
    )(offsets, limits, *pieces, table, *extra)


def phase_table(bins, lag_count):
    freq = np.arange(bins, dtype=np.int64) + BAND_LO
    phase = freq[:, None] * np.arange(lag_count, dtype=np.int64)[None, :] % lag_count
    angle = (2.0 * math.pi / lag_count * phase).astype(np.float32)
    scale = np.float32(1.0 / math.sqrt(bins))
    rows = [np.cos(angle) * scale, -np.sin(angle) * scale]
    return np.concatenate(rows, axis=0).astype(jnp.bfloat16)


def moves(n):
    every = range(n)
    return dict(
        chip=[(i, i ^ 1) for i in every],
        xs=[(i, i ^ 2) for i in every],
        xd=[(i, i ^ 3) for i in every],
        down=[(i, i - 4) for i in every if i >= 4],
        crossed=[(i, (i - 4) ^ 1) for i in every if i >= 4],
        up=[(i, i + 4) for i in every if i + 4 < n],
    )


def local(spectra, pair_offset, lag_limit):
    n = lax.axis_size("pairs")
    move = {name: functools.partial(lax.ppermute, axis_name="pairs", perm=perm) for name, perm in moves(n).items()}
    table = jnp.asarray(phase_table(spectra.shape[4], 2 * spectra.shape[4]))

    theirs, side_raw, up_raw, down_raw = quarters(spectra)
    got = move["chip"](theirs)
    down0 = move["down"](down_raw)
    side0 = move["xs"](side_raw)
    up0 = move["up"](up_raw)
    got_p, got_q, got_side = whiten_got(got)
    down1 = move["down"](got_p)
    side1 = move["xs"](got_side)
    up1 = move["up"](got_q)
    mine_p = whiten_block(down_raw)
    mine_q = whiten_block(up_raw)
    (pair,) = cross(chip_kernel, (2,), mine_p, got_p, mine_q, got_q)
    down0 = whiten_block(down0, after=pair)
    side0 = whiten_block(side0, after=down0)
    up0 = whiten_block(up0, after=side0)

    (zs,) = cross(back_kernel, (4,), mine_q, got_q, up0, side0, side1, after=up0)
    xs, xd = cross(near_kernel, (2, 2), mine_q, got_q, down0, down1, side0, side1, after=zs)
    own_here, own_chip = cross(
        own_kernel, (6, 6), mine_p, got_p, down0, down1, side0, side1, pair, after=xd
    )
    (zd,) = cross(back_kernel, (4,), mine_q, got_q, up1, side0, side1, after=own_chip)
    zs = move["down"](zs)
    xs = move["xs"](xs)
    xd = move["xd"](xd)
    own_chip = move["chip"](own_chip)
    zd = move["crossed"](zd)
    straight = (own_here, xs, zs)
    crossed = (own_chip, xd, zd)
    out = lag_products(0, LARGE, pair_offset, lag_limit, straight, table, None)
    return lag_products(1, SMALL, pair_offset, lag_limit, crossed, table, out)


def solution(mesh):
    in_specs = (
        P(("hours", "pairs"), None, None, None, None),
        P(("hours", "pairs"), None),
        P(("hours", "pairs"), None),
    )
    out_specs = P(("hours", "pairs"), None, None, None)
    return jax.shard_map(local, mesh=mesh, in_specs=in_specs, out_specs=out_specs, check_vma=False)
```

time: 59.9 us -> 50.8 us (0.85)
  Pallas kernels: 18.6 us -> 13.6 us
  waiting for transfers between devices: 18.8 us -> 15.7 us
  other arithmetic: 0.65 us -> 0 us
    ppermute x1, waiting for transfers between devices: 0.01 us -> 5.91 us  [local(): zd = move['crossed'](zd)]
    pallas_call x1, Pallas kernels: 3.95 us -> 0.23 us  [quarters(): pl.pallas_call(quarters_kernel, out_shape=[jax.ShapeDtypeStruct((2,) + sh...]
    ppermute x1, waiting for transfers between devices: 3.43 us -> 0.21 us  [local(): xs = move['xs'](xs)]
    ppermute x1, waiting for transfers between devices: 3.05 us -> 0.01 us  [local(): xd = move['xd'](xd)]
    ppermute x1, waiting for transfers between devices: 2.69 us -> 5.68 us  [local(): down0 = move['down'](down_raw)]
    ppermute x1, waiting for transfers between devices: 4.84 us -> 2.19 us  [local(): zs = move['down'](zs)]
    ppermute x1, waiting for transfers between devices: 2.22 us -> 0.01 us  [local(): up1 = move['up'](got_q)]
    ppermute x1, waiting for transfers between devices: 2.01 us -> 0.01 us  [local(): down1 = move['down'](got_p)]
  transfers between devices with their start and end apart: 14 -> 12, of which waited for: 7 -> 5; matrix products, arithmetic and copies ran while one was open for 0% -> 0% of each run, Pallas kernels for 21% -> 23%
where the time goes in v3:
time: 50.8 us; the launch traced here: 50.5 us
  starting transfers between devices  19.4 us (38%)
  waiting for transfers between devices  15.7 us (31%)
  Pallas kernels  13.6 us (27%)
  local copies, waits for them, and re-layouts  1.61 us (3%)
    ppermute x1, waiting for transfers between devices, local(): zd = move['crossed'](zd)  5.91 us
    ppermute x1, waiting for transfers between devices, local(): down0 = move['down'](down_raw)  5.68 us
    ppermute x1, starting transfers between devices, local(): up0 = move['up'](up_raw)  4.57 us
    pallas_call x5, Pallas kernels, cross(): pl.pallas_call(kernel, out_shape=[jax.ShapeDtypeStruct((n, rows, 2 * bins...  4.11 us
    pallas_call x5, Pallas kernels, whiten_block(): pl.pallas_call(whiten_block_kernel, out_shape=jax.ShapeDtypeStruct(block....  4.06 us
    ppermute x1, starting transfers between devices, local(): up1 = move['up'](got_q)  3.86 us
    pallas_call x2, Pallas kernels, lag_products(): pl.pallas_call(kernel, out_shape=jax.ShapeDtypeStruct((1, slots, 4 * rows...  3.51 us
    ppermute x1, starting transfers between devices, local(): side0 = move['xs'](side_raw)  2.58 us
  transfers between devices with their start and end apart: 12, of which 5 were waited for; matrix products, arithmetic and copies ran while one was open for 0% of the time, Pallas kernels for 23%

profile of v3, /device:TPU:0, one launch (start us, length us, event | category | flops | bytes accessed | tf_op | source)
XLA Modules:
  0.0 50.5 jit_solution(1872238451229894747)
XLA Ops:
  0.0 0.0 copy-start
  0.0 1.6 %copy-done = bf16[1,2,8,256,256]{4,3,2,1,0:T(8,128)(2,1)S(1)} copy-done((bf16[1,2,8,256,256]{4,3,2,1,0:T(8,128)(2,1)S(1)}, bf16[1,2,8,256,256]{4,3,2,1,0:T(8,128)(2,1)}, u32[]{:S(2)}) %copy-start) | copy-done | bytes 2097176
  1.6 0.2 quarters.1
  1.8 0.5 %collective-permute-start = (bf16[2,2,8,64,256]{4,3,2,1,0:T(8,128)(2,1)S(1)}, bf16[2,2,8,64,256]{4,3,2,1,0:T(8,128)(2,1)S(1)}, u32[]{:S(2)}, u32[]{:S(2)}) collective-permute-start(bf16[2,2,8,64,256]{4,3,2,1,0:T(8,128)(2,1)S(1)} %get-tuple-element.17), channel_id=1, source_target_pairs={{0,1},{1,0},{2,3},{3,2},{4,5},{5,4},{6,7},{7,6},{8,9},{9,8},{10,11... | collective-permute-start | bytes 3145736 | tf_op jit(solution)/shard_map/ppermute | solution.py:353
  2.3 1.3 %collective-permute-start.1 = (bf16[2,8,64,256]{3,2,1,0:T(8,128)(2,1)S(1)}, bf16[2,8,64,256]{3,2,1,0:T(8,128)(2,1)S(1)}, u32[]{:S(2)}, u32[]{:S(2)}) collective-permute-start(bf16[2,8,64,256]{3,2,1,0:T(8,128)(2,1)S(1)} %get-tuple-element.16.source), channel_id=1, source_target_pairs={{4,0},{5,1},{6,2},{7,3},{8,4},{9,5},{10,6},{11,7},{12,8},{13,9},{1... | collective-permute-start | bytes 1572872 | tf_op jit(solution)/shard_map/ppermute | solution.py:354
  3.6 2.6 %collective-permute-start.3 = (bf16[2,8,64,256]{3,2,1,0:T(8,128)(2,1)S(1)}, bf16[2,8,64,256]{3,2,1,0:T(8,128)(2,1)S(1)}, u32[]{:S(2)}, u32[]{:S(2)}) collective-permute-start(bf16[2,8,64,256]{3,2,1,0:T(8,128)(2,1)S(1)} %get-tuple-element.21), channel_id=1, source_target_pairs={{0,2},{1,3},{2,0},{3,1},{4,6},{5,7},{6,4},{7,5},{8,10},{9,11},{10,... | collective-permute-start | bytes 1572872 | tf_op jit(solution)/shard_map/ppermute | solution.py:355
  6.2 4.6 %collective-permute-start.5 = (bf16[2,8,64,256]{3,2,1,0:T(8,128)(2,1)S(1)}, bf16[2,8,64,256]{3,2,1,0:T(8,128)(2,1)S(1)}, u32[]{:S(2)}, u32[]{:S(2)}) collective-permute-start(bf16[2,8,64,256]{3,2,1,0:T(8,128)(2,1)S(1)} %get-tuple-element.19.source), channel_id=1, source_target_pairs={{0,4},{1,5},{2,6},{3,7},{4,8},{5,9},{6,10},{7,11},{8,12},{9,13},{1... | collective-permute-start | bytes 1572872 | tf_op jit(solution)/shard_map/ppermute | solution.py:356
  10.8 0.0 collective-permute-done.got
  10.8 1.7 %whiten_got.1 = (bf16[2,8,64,256]{3,2,1,0:T(8,128)(2,1)S(1)}, bf16[2,8,64,256]{3,2,1,0:T(8,128)(2,1)S(1)}, bf16[2,8,64,256]{3,2,1,0:T(8,128)(2,1)S(1)}) custom-call(bf16[2,2,8,64,256]{4,3,2,1,0:T(8,128)(2,1)S(1)} %collective-permute-done.got), custom_call_target="tpu_custom_call" | custom-call | flops 1000 | bytes 1000 | tf_op jit(solution)/shard_map/whiten_got/pallas_call | solution.py:102
  12.5 0.2 collective-permute-start.4
  12.6 1.3 %collective-permute-start.2 = (bf16[2,8,64,256]{3,2,1,0:T(8,128)(2,1)S(1)}, bf16[2,8,64,256]{3,2,1,0:T(8,128)(2,1)S(1)}, u32[]{:S(2)}, u32[]{:S(2)}) collective-permute-start(bf16[2,8,64,256]{3,2,1,0:T(8,128)(2,1)S(1)} %get-tuple-element.18.got_p), channel_id=1, source_target_pairs={{4,0},{5,1},{6,2},{7,3},{8,4},{9,5},{10,6},{11,7},{12,8},{13,9},{1... | collective-permute-start | bytes 1572872 | tf_op jit(solution)/shard_map/ppermute | solution.py:358
  13.9 5.7 %collective-permute-done.1.source = bf16[2,8,64,256]{3,2,1,0:T(8,128)(2,1)S(1)} collective-permute-done((bf16[2,8,64,256]{3,2,1,0:T(8,128)(2,1)S(1)}, bf16[2,8,64,256]{3,2,1,0:T(8,128)(2,1)S(1)}, u32[]{:S(2)}, u32[]{:S(2)}) %collective-permute-start.1) | collective-permute-done | bytes 524320 | tf_op jit(solution)/shard_map/ppermute | solution.py:354
  19.6 3.9 %collective-permute-start.8 = (bf16[2,8,64,256]{3,2,1,0:T(8,128)(2,1)S(1)}, bf16[2,8,64,256]{3,2,1,0:T(8,128)(2,1)S(1)}, u32[]{:S(2)}, u32[]{:S(2)}) collective-permute-start(bf16[2,8,64,256]{3,2,1,0:T(8,128)(2,1)S(1)} %get-tuple-element.20.got_q), channel_id=1, source_target_pairs={{0,4},{1,5},{2,6},{3,7},{4,8},{5,9},{6,10},{7,11},{8,12},{9,13},{1... | collective-permute-start | bytes 1572872 | tf_op jit(solution)/shard_map/ppermute | solution.py:360
  23.5 0.8 %whiten_block.6.mine_q = bf16[2,8,64,256]{3,2,1,0:T(8,128)(2,1)S(1)} custom-call(bf16[2,8,64,256]{3,2,1,0:T(8,128)(2,1)S(1)} %get-tuple-element.19.source), custom_call_target="tpu_custom_call" | custom-call | flops 1000 | bytes 1000 | tf_op jit(solution)/shard_map/whiten_block/pallas_call | solution.py:128
  24.3 0.8 %whiten_block.5.mine_p = bf16[2,8,64,256]{3,2,1,0:T(8,128)(2,1)S(1)} custom-call(bf16[2,8,64,256]{3,2,1,0:T(8,128)(2,1)S(1)} %get-tuple-element.16.source), custom_call_target="tpu_custom_call" | custom-call | flops 1000 | bytes 1000 | tf_op jit(solution)/shard_map/whiten_block/pallas_call | solution.py:128
  25.1 0.7 %chip_kernel.1.rest_0_.pair = bf16[2,64,512]{2,1,0:T(8,128)(2,1)S(1)} custom-call(bf16[2,8,64,256]{3,2,1,0:T(8,128)(2,1)S(1)} %whiten_block.5.mine_p, bf16[2,8,64,256]{3,2,1,0:T(8,128)(2,1)S(1)} %get-tuple-element.18.got_p, bf16[2,8,64,256]{3,2,1,0:T(8,128)(2,1)S(1)} %whiten_block.6.mine_q, bf16[2,8,64,256]{3,2,1,0:T(8,128)(2,1)S(1)} %get-tuple-element.20.got_q), custom_call_target="tpu_custom_call" | custom-call | flops 1000 | bytes 1000 | tf_op jit(solution)/shard_map/chip_kernel/pallas_call | solution.py:242
  25.8 0.8 %whiten_block.7.rest_0_.down0 = bf16[2,8,64,256]{3,2,1,0:T(8,128)(2,1)S(1)} custom-call(bf16[2,8,64,256]{3,2,1,0:T(8,128)(2,1)S(1)} %collective-permute-done.1.source, bf16[2,64,512]{2,1,0:T(8,128)(2,1)S(1)} %chip_kernel.1.rest_0_.pair), custom_call_target="tpu_custom_call" | custom-call | flops 1000 | bytes 1000 | tf_op jit(solution)/shard_map/whiten_block/pallas_call | solution.py:128
  26.7 0.0 collective-permute-done.3.source
  26.7 0.8 %whiten_block.8.rest_0_.side0 = bf16[2,8,64,256]{3,2,1,0:T(8,128)(2,1)S(1)} custom-call(bf16[2,8,64,256]{3,2,1,0:T(8,128)(2,1)S(1)} %collective-permute-done.3.source, bf16[2,8,64,256]{3,2,1,0:T(8,128)(2,1)S(1)} %whiten_block.7.rest_0_.down0), custom_call_target="tpu_custom_call" | custom-call | flops 1000 | bytes 1000 | tf_op jit(solution)/shard_map/whiten_block/pallas_call | solution.py:128
  27.5 0.0 collective-permute-done.5.source
  27.5 0.8 %whiten_block.9.up.after = bf16[2,8,64,256]{3,2,1,0:T(8,128)(2,1)S(1)} custom-call(bf16[2,8,64,256]{3,2,1,0:T(8,128)(2,1)S(1)} %collective-permute-done.5.source, bf16[2,8,64,256]{3,2,1,0:T(8,128)(2,1)S(1)} %whiten_block.8.rest_0_.side0), custom_call_target="tpu_custom_call" | custom-call | flops 1000 | bytes 1000 | tf_op jit(solution)/shard_map/whiten_block/pallas_call | solution.py:128
  28.3 1.7 %collective-permute-done.4.side1 = bf16[2,8,64,256]{3,2,1,0:T(8,128)(2,1)S(1)} collective-permute-done((bf16[2,8,64,256]{3,2,1,0:T(8,128)(2,1)S(1)}, bf16[2,8,64,256]{3,2,1,0:T(8,128)(2,1)S(1)}, u32[]{:S(2)}, u32[]{:S(2)}) %collective-permute-start.4) | collective-permute-done | bytes 524320 | tf_op jit(solution)/shard_map/ppermute | solution.py:359
  30.0 0.5 back_kernel.2.after
  30.5 1.3 %collective-permute-start.11 = (bf16[4,64,512]{2,1,0:T(8,128)(2,1)S(1)}, bf16[4,64,512]{2,1,0:T(8,128)(2,1)S(1)}, u32[]{:S(2)}, u32[]{:S(2)}) collective-permute-start(bf16[4,64,512]{2,1,0:T(8,128)(2,1)S(1)} %back_kernel.2.after), channel_id=1, source_target_pairs={{4,0},{5,1},{6,2},{7,3},{8,4},{9,5},{10,6},{11,7},{12,8},{13,9},{1... | collective-permute-start | bytes 786440 | tf_op jit(solution)/shard_map/ppermute | solution.py:374
  31.8 0.0 collective-permute-done.2.down1
  31.8 0.8 %near_kernel.1 = (bf16[2,64,512]{2,1,0:T(8,128)(2,1)S(1)}, bf16[2,64,512]{2,1,0:T(8,128)(2,1)S(1)}) custom-call(bf16[2,8,64,256]{3,2,1,0:T(8,128)(2,1)S(1)} %whiten_block.6.mine_q, bf16[2,8,64,256]{3,2,1,0:T(8,128)(2,1)S(1)} %get-tuple-element.20.got_q, bf16[2,8,64,256]{3,2,1,0:T(8,128)(2,1)S(1)} %whiten_block.7.rest_0_.down0, ...), custom_call_target="tpu_custom_call" | custom-call | flops 1000 | bytes 1000 | tf_op jit(solution)/shard_map/near_kernel/pallas_call | solution.py:242
  32.6 2.3 %collective-permute-start.10 = (bf16[2,64,512]{2,1,0:T(8,128)(2,1)S(1)}, bf16[2,64,512]{2,1,0:T(8,128)(2,1)S(1)}, u32[]{:S(2)}, u32[]{:S(2)}) collective-permute-start(bf16[2,64,512]{2,1,0:T(8,128)(2,1)S(1)} %get-tuple-element.26), channel_id=1, source_target_pairs={{0,2},{1,3},{2,0},{3,1},{4,6},{5,7},{6,4},{7,5},{8,10},{9,11},{10,... | collective-permute-start | bytes 393224 | tf_op jit(solution)/shard_map/ppermute | solution.py:375
  34.9 0.0 collective-permute-start.7
  34.9 1.6 %own_kernel.1 = (bf16[6,64,512]{2,1,0:T(8,128)(2,1)S(1)}, bf16[6,64,512]{2,1,0:T(8,128)(2,1)S(1)}) custom-call(bf16[2,8,64,256]{3,2,1,0:T(8,128)(2,1)S(1)} %whiten_block.5.mine_p, bf16[2,8,64,256]{3,2,1,0:T(8,128)(2,1)S(1)} %get-tuple-element.18.got_p, bf16[2,8,64,256]{3,2,1,0:T(8,128)(2,1)S(1)} %whiten_block.7.rest_0_.down0, ...), custom_call_target="tpu_custom_call" | custom-call | flops 1000 | bytes 1000 | tf_op jit(solution)/shard_map/own_kernel/pallas_call | solution.py:242
  36.5 0.0 copy-start.1
  36.6 0.0 copy-start.2
  36.6 0.0 copy-start.3
  36.6 0.3 collective-permute-start.6
  36.8 0.0 collective-permute-done.8.up
  36.8 0.5 back_kernel.3
  37.3 1.3 %collective-permute-start.9 = (bf16[4,64,512]{2,1,0:T(8,128)(2,1)S(1)}, bf16[4,64,512]{2,1,0:T(8,128)(2,1)S(1)}, u32[]{:S(2)}, u32[]{:S(2)}) collective-permute-start(bf16[4,64,512]{2,1,0:T(8,128)(2,1)S(1)} %back_kernel.3), channel_id=1, source_target_pairs={{4,1},{5,0},{6,3},{7,2},{8,5},{9,4},{10,7},{11,6},{12,9},{13,8},{1... | collective-permute-start | bytes 786440 | tf_op jit(solution)/shard_map/ppermute | solution.py:378
  38.6 0.2 collective-permute-done.10.refs_3_
  38.9 2.2 %collective-permute-done.11.refs_4_ = bf16[4,64,512]{2,1,0:T(8,128)(2,1)S(1)} collective-permute-done((bf16[4,64,512]{2,1,0:T(8,128)(2,1)S(1)}, bf16[4,64,512]{2,1,0:T(8,128)(2,1)S(1)}, u32[]{:S(2)}, u32[]{:S(2)}) %collective-permute-start.11) | collective-permute-done | bytes 262176 | tf_op jit(solution)/shard_map/ppermute | solution.py:374
  41.0 0.0 copy-done.1
  41.0 0.0 copy-done.2
  41.1 0.0 copy-done.3
  41.1 1.8 %lags.2.earlier = bf16[1,4,256,512]{3,2,1,0:T(8,128)(2,1)} custom-call(s32[1,4]{1,0:T(1,128)S(1)} %copy-done.2, s32[1,4]{1,0:T(1,128)S(1)} %copy-done.3, bf16[6,64,512]{2,1,0:T(8,128)(2,1)S(1)} %get-tuple-element.25.refs_2_, bf16[2,64,512]{2,1,0:T(8,128)(2,1)S(1)} %collective-permute-done.10.refs_3_, ...), custom_call_target="tpu_custom_call" | custom-call | flops 10000000000 | bytes 40000000 | tf_op jit(solution)/shard_map/lags/pallas_call | solution.py:309
  42.8 0.0 collective-permute-done.7.side
  42.8 5.9 %collective-permute-done.9.back = bf16[4,64,512]{2,1,0:T(8,128)(2,1)S(1)} collective-permute-done((bf16[4,64,512]{2,1,0:T(8,128)(2,1)S(1)}, bf16[4,64,512]{2,1,0:T(8,128)(2,1)S(1)}, u32[]{:S(2)}, u32[]{:S(2)}) %collective-permute-start.9) | collective-permute-done | bytes 262176 | tf_op jit(solution)/shard_map/ppermute | solution.py:378
  48.7 0.0 collective-permute-done.6.own
  48.7 1.8 %lags.3 = bf16[1,4,256,512]{3,2,1,0:T(8,128)(2,1)} custom-call(s32[1,4]{1,0:T(1,128)S(1)} %copy-done.2, s32[1,4]{1,0:T(1,128)S(1)} %copy-done.3, bf16[6,64,512]{2,1,0:T(8,128)(2,1)S(1)} %collective-permute-done.6.own, bf16[2,64,512]{2,1,0:T(8,128)(2,1)S(1)} %collective-permute-done.7.side, ...), custom_call_target="tpu_custom_call", output_to_operand_aliasing={{}: (6, {})} | custom-call | flops 1000 | bytes 1000 | tf_op jit(solution)/shard_map/lags/pallas_call | solution.py:309
Async XLA Ops:
  0.0 1.6 %copy-start = (bf16[1,2,8,256,256]{4,3,2,1,0:T(8,128)(2,1)S(1)}, bf16[1,2,8,256,256]{4,3,2,1,0:T(8,128)(2,1)}, u32[]{:S(2)}) copy-start(bf16[1,2,8,256,256]{4,3,2,1,0:T(8,128)(2,1)} %spectra.1) | copy-start | bytes 6291460
  1.8 9.0 %collective-permute-start = (bf16[2,2,8,64,256]{4,3,2,1,0:T(8,128)(2,1)S(1)}, bf16[2,2,8,64,256]{4,3,2,1,0:T(8,128)(2,1)S(1)}, u32[]{:S(2)}, u32[]{:S(2)}) collective-permute-start(bf16[2,2,8,64,256]{4,3,2,1,0:T(8,128)(2,1)S(1)} %get-tuple-element.17), channel_id=1, source_target_pairs={{0,1},{1,0},{2,3},{3,2},{4,5},{5,4},{6,7},{7,6},{8,9},{9,8},{10,11... | collective-permute-start | bytes 3145736 | tf_op jit(solution)/shard_map/ppermute | solution.py:353
  2.3 17.3 %collective-permute-start.1 = (bf16[2,8,64,256]{3,2,1,0:T(8,128)(2,1)S(1)}, bf16[2,8,64,256]{3,2,1,0:T(8,128)(2,1)S(1)}, u32[]{:S(2)}, u32[]{:S(2)}) collective-permute-start(bf16[2,8,64,256]{3,2,1,0:T(8,128)(2,1)S(1)} %get-tuple-element.16.source), channel_id=1, source_target_pairs={{4,0},{5,1},{6,2},{7,3},{8,4},{9,5},{10,6},{11,7},{12,8},{13,9},{1... | collective-permute-start | bytes 1572872 | tf_op jit(solution)/shard_map/ppermute | solution.py:354
  3.6 23.0 %collective-permute-start.3 = (bf16[2,8,64,256]{3,2,1,0:T(8,128)(2,1)S(1)}, bf16[2,8,64,256]{3,2,1,0:T(8,128)(2,1)S(1)}, u32[]{:S(2)}, u32[]{:S(2)}) collective-permute-start(bf16[2,8,64,256]{3,2,1,0:T(8,128)(2,1)S(1)} %get-tuple-element.21), channel_id=1, source_target_pairs={{0,2},{1,3},{2,0},{3,1},{4,6},{5,7},{6,4},{7,5},{8,10},{9,11},{10,... | collective-permute-start | bytes 1572872 | tf_op jit(solution)/shard_map/ppermute | solution.py:355
  6.2 21.3 %collective-permute-start.5 = (bf16[2,8,64,256]{3,2,1,0:T(8,128)(2,1)S(1)}, bf16[2,8,64,256]{3,2,1,0:T(8,128)(2,1)S(1)}, u32[]{:S(2)}, u32[]{:S(2)}) collective-permute-start(bf16[2,8,64,256]{3,2,1,0:T(8,128)(2,1)S(1)} %get-tuple-element.19.source), channel_id=1, source_target_pairs={{0,4},{1,5},{2,6},{3,7},{4,8},{5,9},{6,10},{7,11},{8,12},{9,13},{1... | collective-permute-start | bytes 1572872 | tf_op jit(solution)/shard_map/ppermute | solution.py:356
  12.5 17.5 %collective-permute-start.4 = (bf16[2,8,64,256]{3,2,1,0:T(8,128)(2,1)S(1)}, bf16[2,8,64,256]{3,2,1,0:T(8,128)(2,1)S(1)}, u32[]{:S(2)}, u32[]{:S(2)}) collective-permute-start(bf16[2,8,64,256]{3,2,1,0:T(8,128)(2,1)S(1)} %get-tuple-element.22), channel_id=1, source_target_pairs={{0,2},{1,3},{2,0},{3,1},{4,6},{5,7},{6,4},{7,5},{8,10},{9,11},{10,... | collective-permute-start | bytes 1572872 | tf_op jit(solution)/shard_map/ppermute | solution.py:359
  12.6 19.2 %collective-permute-start.2 = (bf16[2,8,64,256]{3,2,1,0:T(8,128)(2,1)S(1)}, bf16[2,8,64,256]{3,2,1,0:T(8,128)(2,1)S(1)}, u32[]{:S(2)}, u32[]{:S(2)}) collective-permute-start(bf16[2,8,64,256]{3,2,1,0:T(8,128)(2,1)S(1)} %get-tuple-element.18.got_p), channel_id=1, source_target_pairs={{4,0},{5,1},{6,2},{7,3},{8,4},{9,5},{10,6},{11,7},{12,8},{13,9},{1... | collective-permute-start | bytes 1572872 | tf_op jit(solution)/shard_map/ppermute | solution.py:358
  19.6 17.2 %collective-permute-start.8 = (bf16[2,8,64,256]{3,2,1,0:T(8,128)(2,1)S(1)}, bf16[2,8,64,256]{3,2,1,0:T(8,128)(2,1)S(1)}, u32[]{:S(2)}, u32[]{:S(2)}) collective-permute-start(bf16[2,8,64,256]{3,2,1,0:T(8,128)(2,1)S(1)} %get-tuple-element.20.got_q), channel_id=1, source_target_pairs={{0,4},{1,5},{2,6},{3,7},{4,8},{5,9},{6,10},{7,11},{8,12},{9,13},{1... | collective-permute-start | bytes 1572872 | tf_op jit(solution)/shard_map/ppermute | solution.py:360
  30.5 10.5 %collective-permute-start.11 = (bf16[4,64,512]{2,1,0:T(8,128)(2,1)S(1)}, bf16[4,64,512]{2,1,0:T(8,128)(2,1)S(1)}, u32[]{:S(2)}, u32[]{:S(2)}) collective-permute-start(bf16[4,64,512]{2,1,0:T(8,128)(2,1)S(1)} %back_kernel.2.after), channel_id=1, source_target_pairs={{4,0},{5,1},{6,2},{7,3},{8,4},{9,5},{10,6},{11,7},{12,8},{13,9},{1... | collective-permute-start | bytes 786440 | tf_op jit(solution)/shard_map/ppermute | solution.py:374
  32.6 6.2 %collective-permute-start.10 = (bf16[2,64,512]{2,1,0:T(8,128)(2,1)S(1)}, bf16[2,64,512]{2,1,0:T(8,128)(2,1)S(1)}, u32[]{:S(2)}, u32[]{:S(2)}) collective-permute-start(bf16[2,64,512]{2,1,0:T(8,128)(2,1)S(1)} %get-tuple-element.26), channel_id=1, source_target_pairs={{0,2},{1,3},{2,0},{3,1},{4,6},{5,7},{6,4},{7,5},{8,10},{9,11},{10,... | collective-permute-start | bytes 393224 | tf_op jit(solution)/shard_map/ppermute | solution.py:375
  34.9 7.9 %collective-permute-start.7 = (bf16[2,64,512]{2,1,0:T(8,128)(2,1)S(1)}, bf16[2,64,512]{2,1,0:T(8,128)(2,1)S(1)}, u32[]{:S(2)}, u32[]{:S(2)}) collective-permute-start(bf16[2,64,512]{2,1,0:T(8,128)(2,1)S(1)} %get-tuple-element.23.after), channel_id=1, source_target_pairs={{0,3},{1,2},{2,1},{3,0},{4,7},{5,6},{6,5},{7,4},{8,11},{9,10},{10,... | collective-permute-start | bytes 393224 | tf_op jit(solution)/shard_map/ppermute | solution.py:376
  36.5 4.5 %copy-start.1 = (bf16[512,512]{1,0:T(8,128)(2,1)S(1)}, bf16[512,512]{1,0:T(8,128)(2,1)}, u32[]{:S(2)}) copy-start(bf16[512,512]{1,0:T(8,128)(2,1)} %constant.2.clone.refs_5_.table) | copy-start | bytes 1572868
  36.6 4.5 %copy-start.2 = (s32[1,4]{1,0:T(1,128)S(1)}, s32[1,4]{1,0:T(1,128)}, u32[]{:S(2)}) copy-start(s32[1,4]{1,0:T(1,128)} %offsets.1) | copy-start | bytes 52
  36.6 4.5 %copy-start.3 = (s32[1,4]{1,0:T(1,128)S(1)}, s32[1,4]{1,0:T(1,128)}, u32[]{:S(2)}) copy-start(s32[1,4]{1,0:T(1,128)} %limits.1) | copy-start | bytes 52
  36.6 12.2 %collective-permute-start.6 = (bf16[6,64,512]{2,1,0:T(8,128)(2,1)S(1)}, bf16[6,64,512]{2,1,0:T(8,128)(2,1)S(1)}, u32[]{:S(2)}, u32[]{:S(2)}) collective-permute-start(bf16[6,64,512]{2,1,0:T(8,128)(2,1)S(1)} %get-tuple-element.24.after), channel_id=1, source_target_pairs={{0,1},{1,0},{2,3},{3,2},{4,5},{5,4},{6,7},{7,6},{8,9},{9,8},{10,11... | collective-permute-start | bytes 1179656 | tf_op jit(solution)/shard_map/ppermute | solution.py:377
  37.3 11.4 %collective-permute-start.9 = (bf16[4,64,512]{2,1,0:T(8,128)(2,1)S(1)}, bf16[4,64,512]{2,1,0:T(8,128)(2,1)S(1)}, u32[]{:S(2)}, u32[]{:S(2)}) collective-permute-start(bf16[4,64,512]{2,1,0:T(8,128)(2,1)S(1)} %back_kernel.3), channel_id=1, source_target_pairs={{4,1},{5,0},{6,3},{7,2},{8,5},{9,4},{10,7},{11,6},{12,9},{13,8},{1... | collective-permute-start | bytes 786440 | tf_op jit(solution)/shard_map/ppermute | solution.py:378

commit v4 on v3

--- a/solution.py
+++ b/solution.py
@@ -13,7 +13,7 @@
 TILE = 16
 LANES = 128
 VMEM_LIMIT = 16 * 1024 * 1024
-VMEM_ALL = 16 * 1024 * 1024
+VMEM_ALL = 50 * 1024 * 1024
 WHITEN_TILE = 16
 
 SMALL = pl.CostEstimate(flops=1000, bytes_accessed=1000, transcendentals=0)
@@ -250,25 +250,22 @@
     )(*blocks, *extra)
 
 
-def lag_kernel(flip, offsets, limits, own, side, back, table, earlier, out, cand, lagged, sent):
+def lag_kernel(flip, classes, offsets, limits, own, side, back, table, out, cand, lagged, sent):
     core, x = place()
     half = core if flip == 0 else 1 - core
     rows, lags = own.shape[1], table.shape[1]
-    p_rows, q_rows = pl.ds(0, rows), pl.ds(rows, rows)
-    cand[0, p_rows, :] = own[4]
-    cand[0, q_rows, :] = own[5]
-    cand[3:5, p_rows, :] = own[2:4]
-    cand[3:5, q_rows, :] = back[2:4]
-
-    @pl.when(x == 0)
-    def _():
-        cand[1:3, p_rows, :] = own[0:2]
-        cand[1:3, q_rows, :] = side[...]
-
-    @pl.when(x == 1)
-    def _():
-        cand[1:3, p_rows, :] = side[...]
-        cand[1:3, q_rows, :] = back[0:2]
+    for spot, k in enumerate(classes):
+        part = pl.ds(spot * rows, rows)
+        cand[0, part, :] = own[4 + k]
+        cand[3:5, part, :] = own[2:4] if k == 0 else back[2:4]
+
+        @pl.when(x == 0)
+        def _():
+            cand[1:3, part, :] = own[0:2] if k == 0 else side[...]
+
+        @pl.when(x == 1)
+        def _():
+            cand[1:3, part, :] = side[...] if k == 0 else back[0:2]
 
     lag = lax.broadcasted_iota(jnp.int32, (1, lags), 1)
     distance = jnp.minimum(lag, lags - lag)
@@ -282,13 +279,13 @@
         )
         limit = jnp.where(offset > 0, limits[0, slot], 0)
         lagged[slot] = jnp.where(distance < limit, product, 0.0).astype(jnp.bfloat16)
-        for k in range(2):
+        for spot, k in enumerate(classes):
             target = pl.multiple_of((2 * k + half) * rows, rows)
             copies.append(
                 pltpu.make_async_copy(
-                    lagged.at[slot, pl.ds(k * rows, rows), :],
+                    lagged.at[slot, pl.ds(spot * rows, rows), :],
                     out.at[0, slot, pl.ds(target, rows), :],
-                    sent.at[slot, k],
+                    sent.at[slot, spot],
                 )
             )
             copies[-1].start()
@@ -296,31 +293,39 @@
         copy.wait()
 
 
-def lag_products(flip, cost, offsets, limits, pieces, table, earlier):
-    rows, width = pieces[0].shape[1:]
+def lag_products(flip, classes, cost, offsets, limits, own, side, back, table, earlier):
+    rows, width = own.shape[1:]
     slots, lags = offsets.shape[1], table.shape[1]
     vmem = pl.BlockSpec(memory_space=pltpu.VMEM)
     smem = pl.BlockSpec(memory_space=pltpu.SMEM)
-    kernel = functools.partial(lag_kernel, flip)
-    extra = [earlier]
-    if earlier is None:
-        kernel = lambda *refs: lag_kernel(flip, *refs[:6], None, *refs[6:])
-        extra = []
+    pieces = [own, side] + ([] if back is None else [back]) + [table]
+    extra = [] if earlier is None else [earlier]
+
+    def kernel(*refs):
+        refs = list(refs)
+        if earlier is not None:
+            del refs[2 + len(pieces)]
+        if back is None:
+            refs.insert(4, None)
+        lag_kernel(flip, classes, *refs)
+
     return pl.pallas_call(
         kernel,
         out_shape=jax.ShapeDtypeStruct((1, slots, 4 * rows, lags), jnp.bfloat16),
-        in_specs=[smem] * 2 + [vmem] * 4 + [pl.BlockSpec(memory_space=pl.ANY)] * len(extra),
+        in_specs=[smem] * 2
+        + [vmem] * len(pieces)
+        + [pl.BlockSpec(memory_space=pl.ANY)] * len(extra),
         out_specs=pl.BlockSpec(memory_space=pl.ANY),
         scratch_shapes=[
-            pltpu.VMEM((5, 2 * rows, width), jnp.bfloat16),
-            pltpu.VMEM((slots, 2 * rows, lags), jnp.bfloat16),
-            pltpu.SemaphoreType.DMA((slots, 2)),
+            pltpu.VMEM((5, len(classes) * rows, width), jnp.bfloat16),
+            pltpu.VMEM((slots, len(classes) * rows, lags), jnp.bfloat16),
+            pltpu.SemaphoreType.DMA((slots, len(classes))),
         ],
-        input_output_aliases={6: 0} if extra else {},
+        input_output_aliases={2 + len(pieces): 0} if extra else {},
         compiler_params=pltpu.CompilerParams(vmem_limit_bytes=VMEM_LIMIT),
         cost_estimate=cost,
         name="lags",
-    )(offsets, limits, *pieces, table, *extra)
+    )(offsets, limits, *pieces, *extra)
 
 
 def phase_table(bins, lag_count):
@@ -361,25 +366,25 @@
     mine_p = whiten_block(down_raw)
     mine_q = whiten_block(up_raw)
     (pair,) = cross(chip_kernel, (2,), mine_p, got_p, mine_q, got_q)
-    down0 = whiten_block(down0, after=pair)
-    side0 = whiten_block(side0, after=down0)
-    up0 = whiten_block(up0, after=side0)
+    side0 = whiten_block(side0, after=pair)
+    down0 = whiten_block(down0, after=side0)
+    up0 = whiten_block(up0, after=down0)
 
     (zs,) = cross(back_kernel, (4,), mine_q, got_q, up0, side0, side1, after=up0)
     xs, xd = cross(near_kernel, (2, 2), mine_q, got_q, down0, down1, side0, side1, after=zs)
+    (zd,) = cross(back_kernel, (4,), mine_q, got_q, up1, side0, side1, after=xd)
     own_here, own_chip = cross(
-        own_kernel, (6, 6), mine_p, got_p, down0, down1, side0, side1, pair, after=xd
+        own_kernel, (6, 6), mine_p, got_p, down0, down1, side0, side1, pair, after=zd
     )
-    (zd,) = cross(back_kernel, (4,), mine_q, got_q, up1, side0, side1, after=own_chip)
     zs = move["down"](zs)
     xs = move["xs"](xs)
     xd = move["xd"](xd)
     own_chip = move["chip"](own_chip)
     zd = move["crossed"](zd)
-    straight = (own_here, xs, zs)
-    crossed = (own_chip, xd, zd)
-    out = lag_products(0, LARGE, pair_offset, lag_limit, straight, table, None)
-    return lag_products(1, SMALL, pair_offset, lag_limit, crossed, table, out)
+    slots = (pair_offset, lag_limit)
+    out = lag_products(0, (0, 1), LARGE, *slots, own_here, xs, zs, table, None)
+    out = lag_products(1, (0,), LARGE, *slots, own_chip, xd, None, table, out)
+    return lag_products(1, (1,), SMALL, *slots, own_chip, xd, zd, table, out)
 
 
 def solution(mesh):

time: 50.8 us -> 46.9 us (0.923)
  waiting for transfers between devices: 15.7 us -> 10.3 us
  Pallas kernels: 13.6 us -> 16.8 us
  local copies, waits for them, and re-layouts: 1.61 us -> 0.02 us
    ppermute x1, waiting for transfers between devices: 5.68 us -> 0.01 us  [local(): down0 = move['down'](down_raw)]
    ppermute x1, waiting for transfers between devices: 0.01 us -> 3.78 us  [local(): side0 = move['xs'](side_raw)]
    ppermute x1, waiting for transfers between devices: 5.91 us -> 2.31 us  [local(): zd = move['crossed'](zd)]
    ppermute x1, waiting for transfers between devices: 2.19 us -> 0.01 us  [local(): zs = move['down'](zs)]
    pallas_call x2 -> x3, Pallas kernels: 3.51 us -> 5.2 us  [lag_products(): pl.pallas_call(kernel, out_shape=jax.ShapeDtypeStruct((1, slots, 4 * rows...]
    unnamed x8 -> x6, local copies, waits for them, and re-layouts: 1.61 us -> 0.02 us
    ppermute x1, waiting for transfers between devices: 0.01 us -> 1.56 us  [local(): down1 = move['down'](got_p)]
    pallas_call x1, Pallas kernels: 0.23 us -> 1.75 us  [quarters(): pl.pallas_call(quarters_kernel, out_shape=[jax.ShapeDtypeStruct((2,) + sh...]
  transfers between devices with their start and end apart: 12 -> 12, of which waited for: 5 -> 5; matrix products, arithmetic and copies ran while one was open for 0% -> 0% of each run, Pallas kernels for 23% -> 29%
where the time goes in v4:
time: 46.9 us; the launch traced here: 46.6 us
  starting transfers between devices  19.3 us (41%)
  Pallas kernels  16.8 us (36%)
  waiting for transfers between devices  10.3 us (22%)
    pallas_call x3, Pallas kernels, lag_products(): pl.pallas_call(kernel, out_shape=jax.ShapeDtypeStruct((1, slots, 4 * rows...  5.2 us
    ppermute x1, starting transfers between devices, local(): up0 = move['up'](up_raw)  4.58 us
    pallas_call x5, Pallas kernels, cross(): pl.pallas_call(kernel, out_shape=[jax.ShapeDtypeStruct((n, rows, 2 * bins...  4.09 us
    pallas_call x5, Pallas kernels, whiten_block(): pl.pallas_call(whiten_block_kernel, out_shape=jax.ShapeDtypeStruct(block....  4.06 us
    ppermute x1, starting transfers between devices, local(): up1 = move['up'](got_q)  3.95 us
    ppermute x1, waiting for transfers between devices, local(): side0 = move['xs'](side_raw)  3.78 us
    ppermute x1, starting transfers between devices, local(): side0 = move['xs'](side_raw)  2.61 us
    ppermute x1, waiting for transfers between devices, local(): zd = move['crossed'](zd)  2.31 us
  transfers between devices with their start and end apart: 12, of which 5 were waited for; matrix products, arithmetic and copies ran while one was open for 0% of the time, Pallas kernels for 29%

profile of v4, /device:TPU:0, one launch (start us, length us, event | category | flops | bytes accessed | tf_op | source)
XLA Modules:
  0.0 46.6 jit_solution(10602244159514761221)
XLA Ops:
  0.0 1.8 %quarters.1 = (bf16[2,2,8,64,256]{4,3,2,1,0:T(8,128)(2,1)S(1)}, bf16[2,8,64,256]{3,2,1,0:T(8,128)(2,1)S(1)}, bf16[2,8,64,256]{3,2,1,0:T(8,128)(2,1)S(1)}, bf16[2,8,64,256]{3,2,1,0:T(8,128)(2,1)S(1)}) custom-call(bf16[1,2,8,256,256]{4,3,2,1,0:T(8,128)(2,1)} %spectra.1), custom_call_target="tpu_custom_call" | custom-call | flops 1000 | bytes 1000 | tf_op jit(solution)/shard_map/quarters/pallas_call | solution.py:65
  1.8 0.5 %collective-permute-start = (bf16[2,2,8,64,256]{4,3,2,1,0:T(8,128)(2,1)S(1)}, bf16[2,2,8,64,256]{4,3,2,1,0:T(8,128)(2,1)S(1)}, u32[]{:S(2)}, u32[]{:S(2)}) collective-permute-start(bf16[2,2,8,64,256]{4,3,2,1,0:T(8,128)(2,1)S(1)} %get-tuple-element.17), channel_id=1, source_target_pairs={{0,1},{1,0},{2,3},{3,2},{4,5},{5,4},{6,7},{7,6},{8,9},{9,8},{10,11... | collective-permute-start | bytes 3145736 | tf_op jit(solution)/shard_map/ppermute | solution.py:358
  2.2 2.6 %collective-permute-start.2 = (bf16[2,8,64,256]{3,2,1,0:T(8,128)(2,1)S(1)}, bf16[2,8,64,256]{3,2,1,0:T(8,128)(2,1)S(1)}, u32[]{:S(2)}, u32[]{:S(2)}) collective-permute-start(bf16[2,8,64,256]{3,2,1,0:T(8,128)(2,1)S(1)} %get-tuple-element.19), channel_id=1, source_target_pairs={{0,2},{1,3},{2,0},{3,1},{4,6},{5,7},{6,4},{7,5},{8,10},{9,11},{10,... | collective-permute-start | bytes 1572872 | tf_op jit(solution)/shard_map/ppermute | solution.py:360
  4.9 1.3 %collective-permute-start.1 = (bf16[2,8,64,256]{3,2,1,0:T(8,128)(2,1)S(1)}, bf16[2,8,64,256]{3,2,1,0:T(8,128)(2,1)S(1)}, u32[]{:S(2)}, u32[]{:S(2)}) collective-permute-start(bf16[2,8,64,256]{3,2,1,0:T(8,128)(2,1)S(1)} %get-tuple-element.16.source), channel_id=1, source_target_pairs={{4,0},{5,1},{6,2},{7,3},{8,4},{9,5},{10,6},{11,7},{12,8},{13,9},{1... | collective-permute-start | bytes 1572872 | tf_op jit(solution)/shard_map/ppermute | solution.py:359
  6.1 4.6 %collective-permute-start.6 = (bf16[2,8,64,256]{3,2,1,0:T(8,128)(2,1)S(1)}, bf16[2,8,64,256]{3,2,1,0:T(8,128)(2,1)S(1)}, u32[]{:S(2)}, u32[]{:S(2)}) collective-permute-start(bf16[2,8,64,256]{3,2,1,0:T(8,128)(2,1)S(1)} %get-tuple-element.20.source), channel_id=1, source_target_pairs={{0,4},{1,5},{2,6},{3,7},{4,8},{5,9},{6,10},{7,11},{8,12},{9,13},{1... | collective-permute-start | bytes 1572872 | tf_op jit(solution)/shard_map/ppermute | solution.py:361
  10.7 0.0 collective-permute-done.got
  10.7 1.7 %whiten_got.1 = (bf16[2,8,64,256]{3,2,1,0:T(8,128)(2,1)S(1)}, bf16[2,8,64,256]{3,2,1,0:T(8,128)(2,1)S(1)}, bf16[2,8,64,256]{3,2,1,0:T(8,128)(2,1)S(1)}) custom-call(bf16[2,2,8,64,256]{4,3,2,1,0:T(8,128)(2,1)S(1)} %collective-permute-done.got), custom_call_target="tpu_custom_call" | custom-call | flops 1000 | bytes 1000 | tf_op jit(solution)/shard_map/whiten_got/pallas_call | solution.py:102
  12.4 0.1 collective-permute-start.4
  12.6 1.3 %collective-permute-start.3 = (bf16[2,8,64,256]{3,2,1,0:T(8,128)(2,1)S(1)}, bf16[2,8,64,256]{3,2,1,0:T(8,128)(2,1)S(1)}, u32[]{:S(2)}, u32[]{:S(2)}) collective-permute-start(bf16[2,8,64,256]{3,2,1,0:T(8,128)(2,1)S(1)} %get-tuple-element.18.got_p), channel_id=1, source_target_pairs={{4,0},{5,1},{6,2},{7,3},{8,4},{9,5},{10,6},{11,7},{12,8},{13,9},{1... | collective-permute-start | bytes 1572872 | tf_op jit(solution)/shard_map/ppermute | solution.py:363
  13.9 3.8 %collective-permute-done.2.source = bf16[2,8,64,256]{3,2,1,0:T(8,128)(2,1)S(1)} collective-permute-done((bf16[2,8,64,256]{3,2,1,0:T(8,128)(2,1)S(1)}, bf16[2,8,64,256]{3,2,1,0:T(8,128)(2,1)S(1)}, u32[]{:S(2)}, u32[]{:S(2)}) %collective-permute-start.2) | collective-permute-done | bytes 524320 | tf_op jit(solution)/shard_map/ppermute | solution.py:360
  17.6 3.9 %collective-permute-start.5 = (bf16[2,8,64,256]{3,2,1,0:T(8,128)(2,1)S(1)}, bf16[2,8,64,256]{3,2,1,0:T(8,128)(2,1)S(1)}, u32[]{:S(2)}, u32[]{:S(2)}) collective-permute-start(bf16[2,8,64,256]{3,2,1,0:T(8,128)(2,1)S(1)} %get-tuple-element.21.got_q), channel_id=1, source_target_pairs={{0,4},{1,5},{2,6},{3,7},{4,8},{5,9},{6,10},{7,11},{8,12},{9,13},{1... | collective-permute-start | bytes 1572872 | tf_op jit(solution)/shard_map/ppermute | solution.py:365
  21.6 0.8 %whiten_block.6.mine_q = bf16[2,8,64,256]{3,2,1,0:T(8,128)(2,1)S(1)} custom-call(bf16[2,8,64,256]{3,2,1,0:T(8,128)(2,1)S(1)} %get-tuple-element.20.source), custom_call_target="tpu_custom_call" | custom-call | flops 1000 | bytes 1000 | tf_op jit(solution)/shard_map/whiten_block/pallas_call | solution.py:128
  22.4 0.8 %whiten_block.5.mine_p = bf16[2,8,64,256]{3,2,1,0:T(8,128)(2,1)S(1)} custom-call(bf16[2,8,64,256]{3,2,1,0:T(8,128)(2,1)S(1)} %get-tuple-element.16.source), custom_call_target="tpu_custom_call" | custom-call | flops 1000 | bytes 1000 | tf_op jit(solution)/shard_map/whiten_block/pallas_call | solution.py:128
  23.2 0.7 %chip_kernel.1.rest_0_.pair = bf16[2,64,512]{2,1,0:T(8,128)(2,1)S(1)} custom-call(bf16[2,8,64,256]{3,2,1,0:T(8,128)(2,1)S(1)} %whiten_block.5.mine_p, bf16[2,8,64,256]{3,2,1,0:T(8,128)(2,1)S(1)} %get-tuple-element.18.got_p, bf16[2,8,64,256]{3,2,1,0:T(8,128)(2,1)S(1)} %whiten_block.6.mine_q, bf16[2,8,64,256]{3,2,1,0:T(8,128)(2,1)S(1)} %get-tuple-element.21.got_q), custom_call_target="tpu_custom_call" | custom-call | flops 1000 | bytes 1000 | tf_op jit(solution)/shard_map/chip_kernel/pallas_call | solution.py:242
  23.9 0.8 %whiten_block.7.rest_0_.side0 = bf16[2,8,64,256]{3,2,1,0:T(8,128)(2,1)S(1)} custom-call(bf16[2,8,64,256]{3,2,1,0:T(8,128)(2,1)S(1)} %collective-permute-done.2.source, bf16[2,64,512]{2,1,0:T(8,128)(2,1)S(1)} %chip_kernel.1.rest_0_.pair), custom_call_target="tpu_custom_call" | custom-call | flops 1000 | bytes 1000 | tf_op jit(solution)/shard_map/whiten_block/pallas_call | solution.py:128
  24.8 0.0 collective-permute-done.1.source
  24.8 0.8 %whiten_block.8.rest_0_.down0 = bf16[2,8,64,256]{3,2,1,0:T(8,128)(2,1)S(1)} custom-call(bf16[2,8,64,256]{3,2,1,0:T(8,128)(2,1)S(1)} %collective-permute-done.1.source, bf16[2,8,64,256]{3,2,1,0:T(8,128)(2,1)S(1)} %whiten_block.7.rest_0_.side0), custom_call_target="tpu_custom_call" | custom-call | flops 1000 | bytes 1000 | tf_op jit(solution)/shard_map/whiten_block/pallas_call | solution.py:128
  25.6 0.0 collective-permute-done.6.source
  25.6 0.8 %whiten_block.9.up.after = bf16[2,8,64,256]{3,2,1,0:T(8,128)(2,1)S(1)} custom-call(bf16[2,8,64,256]{3,2,1,0:T(8,128)(2,1)S(1)} %collective-permute-done.6.source, bf16[2,8,64,256]{3,2,1,0:T(8,128)(2,1)S(1)} %whiten_block.8.rest_0_.down0), custom_call_target="tpu_custom_call" | custom-call | flops 1000 | bytes 1000 | tf_op jit(solution)/shard_map/whiten_block/pallas_call | solution.py:128
  26.4 2.2 %collective-permute-done.4.side1 = bf16[2,8,64,256]{3,2,1,0:T(8,128)(2,1)S(1)} collective-permute-done((bf16[2,8,64,256]{3,2,1,0:T(8,128)(2,1)S(1)}, bf16[2,8,64,256]{3,2,1,0:T(8,128)(2,1)S(1)}, u32[]{:S(2)}, u32[]{:S(2)}) %collective-permute-start.4) | collective-permute-done | bytes 524320 | tf_op jit(solution)/shard_map/ppermute | solution.py:364
  28.6 0.5 %back_kernel.2.after = bf16[4,64,512]{2,1,0:T(8,128)(2,1)S(1)} custom-call(bf16[2,8,64,256]{3,2,1,0:T(8,128)(2,1)S(1)} %whiten_block.6.mine_q, bf16[2,8,64,256]{3,2,1,0:T(8,128)(2,1)S(1)} %get-tuple-element.21.got_q, bf16[2,8,64,256]{3,2,1,0:T(8,128)(2,1)S(1)} %whiten_block.9.up.after, bf16[2,8,64,256]{3,2,1,0:T(8,128)(2,1)S(1)} %whiten_block.7.rest_0_.side0, ...), custom_call_target="tpu_custom_call" | custom-call | flops 1000 | bytes 1000 | tf_op jit(solution)/shard_map/back_kernel/pallas_call | solution.py:242
  29.1 1.3 %collective-permute-start.11 = (bf16[4,64,512]{2,1,0:T(8,128)(2,1)S(1)}, bf16[4,64,512]{2,1,0:T(8,128)(2,1)S(1)}, u32[]{:S(2)}, u32[]{:S(2)}) collective-permute-start(bf16[4,64,512]{2,1,0:T(8,128)(2,1)S(1)} %back_kernel.2.after), channel_id=1, source_target_pairs={{4,0},{5,1},{6,2},{7,3},{8,4},{9,5},{10,6},{11,7},{12,8},{13,9},{1... | collective-permute-start | bytes 786440 | tf_op jit(solution)/shard_map/ppermute | solution.py:379
  30.4 1.6 %collective-permute-done.3.down1 = bf16[2,8,64,256]{3,2,1,0:T(8,128)(2,1)S(1)} collective-permute-done((bf16[2,8,64,256]{3,2,1,0:T(8,128)(2,1)S(1)}, bf16[2,8,64,256]{3,2,1,0:T(8,128)(2,1)S(1)}, u32[]{:S(2)}, u32[]{:S(2)}) %collective-permute-start.3) | collective-permute-done | bytes 524320 | tf_op jit(solution)/shard_map/ppermute | solution.py:363
  32.0 0.8 %near_kernel.1 = (bf16[2,64,512]{2,1,0:T(8,128)(2,1)S(1)}, bf16[2,64,512]{2,1,0:T(8,128)(2,1)S(1)}) custom-call(bf16[2,8,64,256]{3,2,1,0:T(8,128)(2,1)S(1)} %whiten_block.6.mine_q, bf16[2,8,64,256]{3,2,1,0:T(8,128)(2,1)S(1)} %get-tuple-element.21.got_q, bf16[2,8,64,256]{3,2,1,0:T(8,128)(2,1)S(1)} %whiten_block.8.rest_0_.down0, ...), custom_call_target="tpu_custom_call" | custom-call | flops 1000 | bytes 1000 | tf_op jit(solution)/shard_map/near_kernel/pallas_call | solution.py:242
  32.8 0.8 %collective-permute-start.10 = (bf16[2,64,512]{2,1,0:T(8,128)(2,1)S(1)}, bf16[2,64,512]{2,1,0:T(8,128)(2,1)S(1)}, u32[]{:S(2)}, u32[]{:S(2)}) collective-permute-start(bf16[2,64,512]{2,1,0:T(8,128)(2,1)S(1)} %get-tuple-element.26), channel_id=1, source_target_pairs={{0,2},{1,3},{2,0},{3,1},{4,6},{5,7},{6,4},{7,5},{8,10},{9,11},{10,... | collective-permute-start | bytes 393224 | tf_op jit(solution)/shard_map/ppermute | solution.py:380
  33.6 0.0 collective-permute-start.8
  33.6 0.0 collective-permute-done.5.up
  33.6 0.5 %back_kernel.3.after = bf16[4,64,512]{2,1,0:T(8,128)(2,1)S(1)} custom-call(bf16[2,8,64,256]{3,2,1,0:T(8,128)(2,1)S(1)} %whiten_block.6.mine_q, bf16[2,8,64,256]{3,2,1,0:T(8,128)(2,1)S(1)} %get-tuple-element.21.got_q, bf16[2,8,64,256]{3,2,1,0:T(8,128)(2,1)S(1)} %collective-permute-done.5.up, bf16[2,8,64,256]{3,2,1,0:T(8,128)(2,1)S(1)} %whiten_block.7.rest_0_.side0, ...), custom_call_target="tpu_custom_call" | custom-call | flops 1000 | bytes 1000 | tf_op jit(solution)/shard_map/back_kernel/pallas_call | solution.py:242
  34.1 0.0 copy-start
  34.1 0.0 copy-start.1
  34.1 0.0 copy-start.2
  34.1 1.4 %collective-permute-start.9 = (bf16[4,64,512]{2,1,0:T(8,128)(2,1)S(1)}, bf16[4,64,512]{2,1,0:T(8,128)(2,1)S(1)}, u32[]{:S(2)}, u32[]{:S(2)}) collective-permute-start(bf16[4,64,512]{2,1,0:T(8,128)(2,1)S(1)} %back_kernel.3.after), channel_id=1, source_target_pairs={{4,1},{5,0},{6,3},{7,2},{8,5},{9,4},{10,7},{11,6},{12,9},{13,8},{1... | collective-permute-start | bytes 786440 | tf_op jit(solution)/shard_map/ppermute | solution.py:383
  35.5 1.6 %own_kernel.1 = (bf16[6,64,512]{2,1,0:T(8,128)(2,1)S(1)}, bf16[6,64,512]{2,1,0:T(8,128)(2,1)S(1)}) custom-call(bf16[2,8,64,256]{3,2,1,0:T(8,128)(2,1)S(1)} %whiten_block.5.mine_p, bf16[2,8,64,256]{3,2,1,0:T(8,128)(2,1)S(1)} %get-tuple-element.18.got_p, bf16[2,8,64,256]{3,2,1,0:T(8,128)(2,1)S(1)} %whiten_block.8.rest_0_.down0, ...), custom_call_target="tpu_custom_call" | custom-call | flops 1000 | bytes 1000 | tf_op jit(solution)/shard_map/own_kernel/pallas_call | solution.py:242
  37.1 1.5 %collective-permute-start.7 = (bf16[6,64,512]{2,1,0:T(8,128)(2,1)S(1)}, bf16[6,64,512]{2,1,0:T(8,128)(2,1)S(1)}, u32[]{:S(2)}, u32[]{:S(2)}) collective-permute-start(bf16[6,64,512]{2,1,0:T(8,128)(2,1)S(1)} %get-tuple-element.24), channel_id=1, source_target_pairs={{0,1},{1,0},{2,3},{3,2},{4,5},{5,4},{6,7},{7,6},{8,9},{9,8},{10,11... | collective-permute-start | bytes 1179656 | tf_op jit(solution)/shard_map/ppermute | solution.py:382
  38.6 0.4 collective-permute-done.10.refs_3_
  39.0 0.0 collective-permute-done.11.refs_4_
  39.1 0.0 copy-done
  39.1 0.0 copy-done.1
  39.1 0.0 copy-done.2
  39.1 1.8 %lags.3.refs_5_ = bf16[1,4,256,512]{3,2,1,0:T(8,128)(2,1)} custom-call(s32[1,4]{1,0:T(1,128)S(1)} %copy-done.1, s32[1,4]{1,0:T(1,128)S(1)} %copy-done.2, bf16[6,64,512]{2,1,0:T(8,128)(2,1)S(1)} %get-tuple-element.25.refs_2_, bf16[2,64,512]{2,1,0:T(8,128)(2,1)S(1)} %collective-permute-done.10.refs_3_, ...), custom_call_target="tpu_custom_call" | custom-call | flops 10000000000 | bytes 40000000 | tf_op jit(solution)/shard_map/lags/pallas_call | solution.py:312
  40.8 0.0 collective-permute-done.8.refs_3_
  40.9 0.0 collective-permute-done.7.refs_2_
  40.9 1.7 %lags.4.refs_6_ = bf16[1,4,256,512]{3,2,1,0:T(8,128)(2,1)} custom-call(s32[1,4]{1,0:T(1,128)S(1)} %copy-done.1, s32[1,4]{1,0:T(1,128)S(1)} %copy-done.2, bf16[6,64,512]{2,1,0:T(8,128)(2,1)S(1)} %collective-permute-done.7.refs_2_, bf16[2,64,512]{2,1,0:T(8,128)(2,1)S(1)} %collective-permute-done.8.refs_3_, ...), custom_call_target="tpu_custom_call", output_to_operand_aliasing={{}: (5, {})} | custom-call | flops 10000000000 | bytes 40000000 | tf_op jit(solution)/shard_map/lags/pallas_call | solution.py:312
  42.6 2.3 %collective-permute-done.9.refs_4_ = bf16[4,64,512]{2,1,0:T(8,128)(2,1)S(1)} collective-permute-done((bf16[4,64,512]{2,1,0:T(8,128)(2,1)S(1)}, bf16[4,64,512]{2,1,0:T(8,128)(2,1)S(1)}, u32[]{:S(2)}, u32[]{:S(2)}) %collective-permute-start.9) | collective-permute-done | bytes 262176 | tf_op jit(solution)/shard_map/ppermute | solution.py:383
  44.9 1.7 %lags.5 = bf16[1,4,256,512]{3,2,1,0:T(8,128)(2,1)} custom-call(s32[1,4]{1,0:T(1,128)S(1)} %copy-done.1, s32[1,4]{1,0:T(1,128)S(1)} %copy-done.2, bf16[6,64,512]{2,1,0:T(8,128)(2,1)S(1)} %collective-permute-done.7.refs_2_, bf16[2,64,512]{2,1,0:T(8,128)(2,1)S(1)} %collective-permute-done.8.refs_3_, ...), custom_call_target="tpu_custom_call", output_to_operand_aliasing={{}: (6, {})} | custom-call | flops 1000 | bytes 1000 | tf_op jit(solution)/shard_map/lags/pallas_call | solution.py:312
Async XLA Ops:
  1.8 9.0 %collective-permute-start = (bf16[2,2,8,64,256]{4,3,2,1,0:T(8,128)(2,1)S(1)}, bf16[2,2,8,64,256]{4,3,2,1,0:T(8,128)(2,1)S(1)}, u32[]{:S(2)}, u32[]{:S(2)}) collective-permute-start(bf16[2,2,8,64,256]{4,3,2,1,0:T(8,128)(2,1)S(1)} %get-tuple-element.17), channel_id=1, source_target_pairs={{0,1},{1,0},{2,3},{3,2},{4,5},{5,4},{6,7},{7,6},{8,9},{9,8},{10,11... | collective-permute-start | bytes 3145736 | tf_op jit(solution)/shard_map/ppermute | solution.py:358
  2.2 15.4 %collective-permute-start.2 = (bf16[2,8,64,256]{3,2,1,0:T(8,128)(2,1)S(1)}, bf16[2,8,64,256]{3,2,1,0:T(8,128)(2,1)S(1)}, u32[]{:S(2)}, u32[]{:S(2)}) collective-permute-start(bf16[2,8,64,256]{3,2,1,0:T(8,128)(2,1)S(1)} %get-tuple-element.19), channel_id=1, source_target_pairs={{0,2},{1,3},{2,0},{3,1},{4,6},{5,7},{6,4},{7,5},{8,10},{9,11},{10,... | collective-permute-start | bytes 1572872 | tf_op jit(solution)/shard_map/ppermute | solution.py:360
  4.9 19.9 %collective-permute-start.1 = (bf16[2,8,64,256]{3,2,1,0:T(8,128)(2,1)S(1)}, bf16[2,8,64,256]{3,2,1,0:T(8,128)(2,1)S(1)}, u32[]{:S(2)}, u32[]{:S(2)}) collective-permute-start(bf16[2,8,64,256]{3,2,1,0:T(8,128)(2,1)S(1)} %get-tuple-element.16.source), channel_id=1, source_target_pairs={{4,0},{5,1},{6,2},{7,3},{8,4},{9,5},{10,6},{11,7},{12,8},{13,9},{1... | collective-permute-start | bytes 1572872 | tf_op jit(solution)/shard_map/ppermute | solution.py:359
  6.1 19.4 %collective-permute-start.6 = (bf16[2,8,64,256]{3,2,1,0:T(8,128)(2,1)S(1)}, bf16[2,8,64,256]{3,2,1,0:T(8,128)(2,1)S(1)}, u32[]{:S(2)}, u32[]{:S(2)}) collective-permute-start(bf16[2,8,64,256]{3,2,1,0:T(8,128)(2,1)S(1)} %get-tuple-element.20.source), channel_id=1, source_target_pairs={{0,4},{1,5},{2,6},{3,7},{4,8},{5,9},{6,10},{7,11},{8,12},{9,13},{1... | collective-permute-start | bytes 1572872 | tf_op jit(solution)/shard_map/ppermute | solution.py:361
  12.4 16.2 %collective-permute-start.4 = (bf16[2,8,64,256]{3,2,1,0:T(8,128)(2,1)S(1)}, bf16[2,8,64,256]{3,2,1,0:T(8,128)(2,1)S(1)}, u32[]{:S(2)}, u32[]{:S(2)}) collective-permute-start(bf16[2,8,64,256]{3,2,1,0:T(8,128)(2,1)S(1)} %get-tuple-element.22), channel_id=1, source_target_pairs={{0,2},{1,3},{2,0},{3,1},{4,6},{5,7},{6,4},{7,5},{8,10},{9,11},{10,... | collective-permute-start | bytes 1572872 | tf_op jit(solution)/shard_map/ppermute | solution.py:364
  12.6 19.4 %collective-permute-start.3 = (bf16[2,8,64,256]{3,2,1,0:T(8,128)(2,1)S(1)}, bf16[2,8,64,256]{3,2,1,0:T(8,128)(2,1)S(1)}, u32[]{:S(2)}, u32[]{:S(2)}) collective-permute-start(bf16[2,8,64,256]{3,2,1,0:T(8,128)(2,1)S(1)} %get-tuple-element.18.got_p), channel_id=1, source_target_pairs={{4,0},{5,1},{6,2},{7,3},{8,4},{9,5},{10,6},{11,7},{12,8},{13,9},{1... | collective-permute-start | bytes 1572872 | tf_op jit(solution)/shard_map/ppermute | solution.py:363
  17.6 15.9 %collective-permute-start.5 = (bf16[2,8,64,256]{3,2,1,0:T(8,128)(2,1)S(1)}, bf16[2,8,64,256]{3,2,1,0:T(8,128)(2,1)S(1)}, u32[]{:S(2)}, u32[]{:S(2)}) collective-permute-start(bf16[2,8,64,256]{3,2,1,0:T(8,128)(2,1)S(1)} %get-tuple-element.21.got_q), channel_id=1, source_target_pairs={{0,4},{1,5},{2,6},{3,7},{4,8},{5,9},{6,10},{7,11},{8,12},{9,13},{1... | collective-permute-start | bytes 1572872 | tf_op jit(solution)/shard_map/ppermute | solution.py:365
  29.1 10.0 %collective-permute-start.11 = (bf16[4,64,512]{2,1,0:T(8,128)(2,1)S(1)}, bf16[4,64,512]{2,1,0:T(8,128)(2,1)S(1)}, u32[]{:S(2)}, u32[]{:S(2)}) collective-permute-start(bf16[4,64,512]{2,1,0:T(8,128)(2,1)S(1)} %back_kernel.2.after), channel_id=1, source_target_pairs={{4,0},{5,1},{6,2},{7,3},{8,4},{9,5},{10,6},{11,7},{12,8},{13,9},{1... | collective-permute-start | bytes 786440 | tf_op jit(solution)/shard_map/ppermute | solution.py:379
  32.8 6.3 %collective-permute-start.10 = (bf16[2,64,512]{2,1,0:T(8,128)(2,1)S(1)}, bf16[2,64,512]{2,1,0:T(8,128)(2,1)S(1)}, u32[]{:S(2)}, u32[]{:S(2)}) collective-permute-start(bf16[2,64,512]{2,1,0:T(8,128)(2,1)S(1)} %get-tuple-element.26), channel_id=1, source_target_pairs={{0,2},{1,3},{2,0},{3,1},{4,6},{5,7},{6,4},{7,5},{8,10},{9,11},{10,... | collective-permute-start | bytes 393224 | tf_op jit(solution)/shard_map/ppermute | solution.py:380
  33.6 7.3 %collective-permute-start.8 = (bf16[2,64,512]{2,1,0:T(8,128)(2,1)S(1)}, bf16[2,64,512]{2,1,0:T(8,128)(2,1)S(1)}, u32[]{:S(2)}, u32[]{:S(2)}) collective-permute-start(bf16[2,64,512]{2,1,0:T(8,128)(2,1)S(1)} %get-tuple-element.23.after), channel_id=1, source_target_pairs={{0,3},{1,2},{2,1},{3,0},{4,7},{5,6},{6,5},{7,4},{8,11},{9,10},{10,... | collective-permute-start | bytes 393224 | tf_op jit(solution)/shard_map/ppermute | solution.py:381
  34.1 5.0 %copy-start = (bf16[512,512]{1,0:T(8,128)(2,1)S(1)}, bf16[512,512]{1,0:T(8,128)(2,1)}, u32[]{:S(2)}) copy-start(bf16[512,512]{1,0:T(8,128)(2,1)} %constant.2.clone.refs_5_.refs_4_) | copy-start | bytes 1572868
  34.1 5.0 %copy-start.1 = (s32[1,4]{1,0:T(1,128)S(1)}, s32[1,4]{1,0:T(1,128)}, u32[]{:S(2)}) copy-start(s32[1,4]{1,0:T(1,128)} %refs_0_.5) | copy-start | bytes 52
  34.1 5.0 %copy-start.2 = (s32[1,4]{1,0:T(1,128)S(1)}, s32[1,4]{1,0:T(1,128)}, u32[]{:S(2)}) copy-start(s32[1,4]{1,0:T(1,128)} %refs_1_.5) | copy-start | bytes 52
  34.1 10.8 %collective-permute-start.9 = (bf16[4,64,512]{2,1,0:T(8,128)(2,1)S(1)}, bf16[4,64,512]{2,1,0:T(8,128)(2,1)S(1)}, u32[]{:S(2)}, u32[]{:S(2)}) collective-permute-start(bf16[4,64,512]{2,1,0:T(8,128)(2,1)S(1)} %back_kernel.3.after), channel_id=1, source_target_pairs={{4,1},{5,0},{6,3},{7,2},{8,5},{9,4},{10,7},{11,6},{12,9},{13,8},{1... | collective-permute-start | bytes 786440 | tf_op jit(solution)/shard_map/ppermute | solution.py:383
  37.1 3.7 %collective-permute-start.7 = (bf16[6,64,512]{2,1,0:T(8,128)(2,1)S(1)}, bf16[6,64,512]{2,1,0:T(8,128)(2,1)S(1)}, u32[]{:S(2)}, u32[]{:S(2)}) collective-permute-start(bf16[6,64,512]{2,1,0:T(8,128)(2,1)S(1)} %get-tuple-element.24), channel_id=1, source_target_pairs={{0,1},{1,0},{2,3},{3,2},{4,5},{5,4},{6,7},{7,6},{8,9},{9,8},{10,11... | collective-permute-start | bytes 1179656 | tf_op jit(solution)/shard_map/ppermute | solution.py:382

commit v5 on v4

--- a/solution.py
+++ b/solution.py
@@ -205,12 +205,11 @@
         run([reader(side0), reader(side1)], [spots(core, back, 0)])
 
 
-def near_kernel(mine_q, got_q, down0, down1, side0, side1, after, xs, xd):
+def near_kernel(mine_q, got_q, down0, down1, side, after, near):
     windows, rows, bins = mine_q.shape[1:]
     core, x = place()
-    side = [reader(side0), reader(side1)]
-    stores = [spots(core, xs, 0), spots(core, xd, 0)]
-    run = functools.partial(products, side, rows=rows, bins=bins, windows=windows)
+    stores = [spots(core, near, 0)]
+    run = functools.partial(products, [reader(side)], rows=rows, bins=bins, windows=windows)
 
     @pl.when(x == 0)
     def _():
@@ -250,7 +249,7 @@
     )(*blocks, *extra)
 
 
-def lag_kernel(flip, classes, offsets, limits, own, side, back, table, out, cand, lagged, sent):
+def lag_kernel(flip, classes, offsets, limits, own, side, back, table, out, cand, chosen, lagged, sent):
     core, x = place()
     half = core if flip == 0 else 1 - core
     rows, lags = own.shape[1], table.shape[1]
@@ -269,16 +268,16 @@
 
     lag = lax.broadcasted_iota(jnp.int32, (1, lags), 1)
     distance = jnp.minimum(lag, lags - lag)
+    height = len(classes) * rows
+    for slot in range(out.shape[1]):
+        offset = offsets[0, slot]
+        chosen[pl.ds(slot * height, height), :] = cand[jnp.clip(offset - 1 + core, 0, 4)]
+    product = jnp.dot(chosen[...], table[...], preferred_element_type=jnp.float32)
     copies = []
     for slot in range(out.shape[1]):
-        offset = offsets[0, slot]
-        product = jnp.dot(
-            cand[jnp.clip(offset - 1 + core, 0, 4)],
-            table[...],
-            preferred_element_type=jnp.float32,
-        )
-        limit = jnp.where(offset > 0, limits[0, slot], 0)
-        lagged[slot] = jnp.where(distance < limit, product, 0.0).astype(jnp.bfloat16)
+        limit = jnp.where(offsets[0, slot] > 0, limits[0, slot], 0)
+        kept = jnp.where(distance < limit, product[slot * height : (slot + 1) * height], 0.0)
+        lagged[slot] = kept.astype(jnp.bfloat16)
         for spot, k in enumerate(classes):
             target = pl.multiple_of((2 * k + half) * rows, rows)
             copies.append(
@@ -318,6 +317,7 @@
         out_specs=pl.BlockSpec(memory_space=pl.ANY),
         scratch_shapes=[
             pltpu.VMEM((5, len(classes) * rows, width), jnp.bfloat16),
+            pltpu.VMEM((slots * len(classes) * rows, width), jnp.bfloat16),
             pltpu.VMEM((slots, len(classes) * rows, lags), jnp.bfloat16),
             pltpu.SemaphoreType.DMA((slots, len(classes))),
         ],
@@ -371,10 +371,11 @@
     up0 = whiten_block(up0, after=down0)
 
     (zs,) = cross(back_kernel, (4,), mine_q, got_q, up0, side0, side1, after=up0)
-    xs, xd = cross(near_kernel, (2, 2), mine_q, got_q, down0, down1, side0, side1, after=zs)
-    (zd,) = cross(back_kernel, (4,), mine_q, got_q, up1, side0, side1, after=xd)
+    (xs,) = cross(near_kernel, (2,), mine_q, got_q, down0, down1, side0, after=zs)
+    (zd,) = cross(back_kernel, (4,), mine_q, got_q, up1, side0, side1, after=xs)
+    (xd,) = cross(near_kernel, (2,), mine_q, got_q, down0, down1, side1, after=zd)
     own_here, own_chip = cross(
-        own_kernel, (6, 6), mine_p, got_p, down0, down1, side0, side1, pair, after=zd
+        own_kernel, (6, 6), mine_p, got_p, down0, down1, side0, side1, pair, after=xd
     )
     zs = move["down"](zs)
     xs = move["xs"](xs)

time: 46.9 us -> 45.9 us (0.979)
  waiting for transfers between devices: 10.3 us -> 8.8 us
    ppermute x1, waiting for transfers between devices: 2.31 us -> 1.07 us  [local(): zd = move['crossed'](zd)]
    ppermute x1, starting transfers between devices: 0.01 us -> 0.53 us  [local(): xd = move['xd'](xd)]
    pallas_call x5 -> x6, Pallas kernels: 4.09 us -> 4.3 us  [cross(): pl.pallas_call(kernel, out_shape=[jax.ShapeDtypeStruct((n, rows, 2 * bins...]
where the time goes in v5:
time: 45.9 us; the launch traced here: 45.4 us
  starting transfers between devices  19.7 us (43%)
  Pallas kernels  16.7 us (36%)
  waiting for transfers between devices  8.8 us (19%)
    pallas_call x3, Pallas kernels, lag_products(): pl.pallas_call(kernel, out_shape=jax.ShapeDtypeStruct((1, slots, 4 * rows...  4.88 us
    ppermute x1, starting transfers between devices, local(): up0 = move['up'](up_raw)  4.58 us
    pallas_call x6, Pallas kernels, cross(): pl.pallas_call(kernel, out_shape=[jax.ShapeDtypeStruct((n, rows, 2 * bins...  4.3 us
    pallas_call x5, Pallas kernels, whiten_block(): pl.pallas_call(whiten_block_kernel, out_shape=jax.ShapeDtypeStruct(block....  4.06 us
    ppermute x1, starting transfers between devices, local(): up1 = move['up'](got_q)  3.95 us
    ppermute x1, waiting for transfers between devices, local(): side0 = move['xs'](side_raw)  3.78 us
    ppermute x1, starting transfers between devices, local(): side0 = move['xs'](side_raw)  2.61 us
    ppermute x1, waiting for transfers between devices, local(): side1 = move['xs'](got_side)  2.19 us
  transfers between devices with their start and end apart: 12, of which 5 were waited for; matrix products, arithmetic and copies ran while one was open for 0% of the time, Pallas kernels for 29%

profile of v5, /device:TPU:0, one launch (start us, length us, event | category | flops | bytes accessed | tf_op | source)
XLA Modules:
  0.0 45.4 jit_solution(8240944902821308394)
XLA Ops:
  0.0 1.8 %quarters.1 = (bf16[2,2,8,64,256]{4,3,2,1,0:T(8,128)(2,1)S(1)}, bf16[2,8,64,256]{3,2,1,0:T(8,128)(2,1)S(1)}, bf16[2,8,64,256]{3,2,1,0:T(8,128)(2,1)S(1)}, bf16[2,8,64,256]{3,2,1,0:T(8,128)(2,1)S(1)}) custom-call(bf16[1,2,8,256,256]{4,3,2,1,0:T(8,128)(2,1)} %spectra.1), custom_call_target="tpu_custom_call" | custom-call | flops 1000 | bytes 1000 | tf_op jit(solution)/shard_map/quarters/pallas_call | solution.py:65
  1.8 0.5 %collective-permute-start = (bf16[2,2,8,64,256]{4,3,2,1,0:T(8,128)(2,1)S(1)}, bf16[2,2,8,64,256]{4,3,2,1,0:T(8,128)(2,1)S(1)}, u32[]{:S(2)}, u32[]{:S(2)}) collective-permute-start(bf16[2,2,8,64,256]{4,3,2,1,0:T(8,128)(2,1)S(1)} %get-tuple-element.15), channel_id=1, source_target_pairs={{0,1},{1,0},{2,3},{3,2},{4,5},{5,4},{6,7},{7,6},{8,9},{9,8},{10,11... | collective-permute-start | bytes 3145736 | tf_op jit(solution)/shard_map/ppermute | solution.py:358
  2.2 2.6 %collective-permute-start.2 = (bf16[2,8,64,256]{3,2,1,0:T(8,128)(2,1)S(1)}, bf16[2,8,64,256]{3,2,1,0:T(8,128)(2,1)S(1)}, u32[]{:S(2)}, u32[]{:S(2)}) collective-permute-start(bf16[2,8,64,256]{3,2,1,0:T(8,128)(2,1)S(1)} %get-tuple-element.17), channel_id=1, source_target_pairs={{0,2},{1,3},{2,0},{3,1},{4,6},{5,7},{6,4},{7,5},{8,10},{9,11},{10,... | collective-permute-start | bytes 1572872 | tf_op jit(solution)/shard_map/ppermute | solution.py:360
  4.9 1.3 %collective-permute-start.1 = (bf16[2,8,64,256]{3,2,1,0:T(8,128)(2,1)S(1)}, bf16[2,8,64,256]{3,2,1,0:T(8,128)(2,1)S(1)}, u32[]{:S(2)}, u32[]{:S(2)}) collective-permute-start(bf16[2,8,64,256]{3,2,1,0:T(8,128)(2,1)S(1)} %get-tuple-element.14.source), channel_id=1, source_target_pairs={{4,0},{5,1},{6,2},{7,3},{8,4},{9,5},{10,6},{11,7},{12,8},{13,9},{1... | collective-permute-start | bytes 1572872 | tf_op jit(solution)/shard_map/ppermute | solution.py:359
  6.1 4.6 %collective-permute-start.6 = (bf16[2,8,64,256]{3,2,1,0:T(8,128)(2,1)S(1)}, bf16[2,8,64,256]{3,2,1,0:T(8,128)(2,1)S(1)}, u32[]{:S(2)}, u32[]{:S(2)}) collective-permute-start(bf16[2,8,64,256]{3,2,1,0:T(8,128)(2,1)S(1)} %get-tuple-element.18.source), channel_id=1, source_target_pairs={{0,4},{1,5},{2,6},{3,7},{4,8},{5,9},{6,10},{7,11},{8,12},{9,13},{1... | collective-permute-start | bytes 1572872 | tf_op jit(solution)/shard_map/ppermute | solution.py:361
  10.7 0.0 collective-permute-done.got
  10.7 1.7 %whiten_got.1 = (bf16[2,8,64,256]{3,2,1,0:T(8,128)(2,1)S(1)}, bf16[2,8,64,256]{3,2,1,0:T(8,128)(2,1)S(1)}, bf16[2,8,64,256]{3,2,1,0:T(8,128)(2,1)S(1)}) custom-call(bf16[2,2,8,64,256]{4,3,2,1,0:T(8,128)(2,1)S(1)} %collective-permute-done.got), custom_call_target="tpu_custom_call" | custom-call | flops 1000 | bytes 1000 | tf_op jit(solution)/shard_map/whiten_got/pallas_call | solution.py:102
  12.4 0.1 collective-permute-start.4
  12.6 1.3 %collective-permute-start.3 = (bf16[2,8,64,256]{3,2,1,0:T(8,128)(2,1)S(1)}, bf16[2,8,64,256]{3,2,1,0:T(8,128)(2,1)S(1)}, u32[]{:S(2)}, u32[]{:S(2)}) collective-permute-start(bf16[2,8,64,256]{3,2,1,0:T(8,128)(2,1)S(1)} %get-tuple-element.16.got_p), channel_id=1, source_target_pairs={{4,0},{5,1},{6,2},{7,3},{8,4},{9,5},{10,6},{11,7},{12,8},{13,9},{1... | collective-permute-start | bytes 1572872 | tf_op jit(solution)/shard_map/ppermute | solution.py:363
  13.9 3.8 %collective-permute-done.2.source = bf16[2,8,64,256]{3,2,1,0:T(8,128)(2,1)S(1)} collective-permute-done((bf16[2,8,64,256]{3,2,1,0:T(8,128)(2,1)S(1)}, bf16[2,8,64,256]{3,2,1,0:T(8,128)(2,1)S(1)}, u32[]{:S(2)}, u32[]{:S(2)}) %collective-permute-start.2) | collective-permute-done | bytes 524320 | tf_op jit(solution)/shard_map/ppermute | solution.py:360
  17.6 3.9 %collective-permute-start.5 = (bf16[2,8,64,256]{3,2,1,0:T(8,128)(2,1)S(1)}, bf16[2,8,64,256]{3,2,1,0:T(8,128)(2,1)S(1)}, u32[]{:S(2)}, u32[]{:S(2)}) collective-permute-start(bf16[2,8,64,256]{3,2,1,0:T(8,128)(2,1)S(1)} %get-tuple-element.19.got_q), channel_id=1, source_target_pairs={{0,4},{1,5},{2,6},{3,7},{4,8},{5,9},{6,10},{7,11},{8,12},{9,13},{1... | collective-permute-start | bytes 1572872 | tf_op jit(solution)/shard_map/ppermute | solution.py:365
  21.6 0.8 %whiten_block.6.mine_q = bf16[2,8,64,256]{3,2,1,0:T(8,128)(2,1)S(1)} custom-call(bf16[2,8,64,256]{3,2,1,0:T(8,128)(2,1)S(1)} %get-tuple-element.18.source), custom_call_target="tpu_custom_call" | custom-call | flops 1000 | bytes 1000 | tf_op jit(solution)/shard_map/whiten_block/pallas_call | solution.py:128
  22.4 0.8 %whiten_block.5.mine_p = bf16[2,8,64,256]{3,2,1,0:T(8,128)(2,1)S(1)} custom-call(bf16[2,8,64,256]{3,2,1,0:T(8,128)(2,1)S(1)} %get-tuple-element.14.source), custom_call_target="tpu_custom_call" | custom-call | flops 1000 | bytes 1000 | tf_op jit(solution)/shard_map/whiten_block/pallas_call | solution.py:128
  23.2 0.7 %chip_kernel.1.rest_0_.pair = bf16[2,64,512]{2,1,0:T(8,128)(2,1)S(1)} custom-call(bf16[2,8,64,256]{3,2,1,0:T(8,128)(2,1)S(1)} %whiten_block.5.mine_p, bf16[2,8,64,256]{3,2,1,0:T(8,128)(2,1)S(1)} %get-tuple-element.16.got_p, bf16[2,8,64,256]{3,2,1,0:T(8,128)(2,1)S(1)} %whiten_block.6.mine_q, bf16[2,8,64,256]{3,2,1,0:T(8,128)(2,1)S(1)} %get-tuple-element.19.got_q), custom_call_target="tpu_custom_call" | custom-call | flops 1000 | bytes 1000 | tf_op jit(solution)/shard_map/chip_kernel/pallas_call | solution.py:241
  23.9 0.8 %whiten_block.7.rest_0_.side0.side = bf16[2,8,64,256]{3,2,1,0:T(8,128)(2,1)S(1)} custom-call(bf16[2,8,64,256]{3,2,1,0:T(8,128)(2,1)S(1)} %collective-permute-done.2.source, bf16[2,64,512]{2,1,0:T(8,128)(2,1)S(1)} %chip_kernel.1.rest_0_.pair), custom_call_target="tpu_custom_call" | custom-call | flops 1000 | bytes 1000 | tf_op jit(solution)/shard_map/whiten_block/pallas_call | solution.py:128
  24.8 0.0 collective-permute-done.1.source
  24.8 0.8 %whiten_block.8.rest_0_.down0 = bf16[2,8,64,256]{3,2,1,0:T(8,128)(2,1)S(1)} custom-call(bf16[2,8,64,256]{3,2,1,0:T(8,128)(2,1)S(1)} %collective-permute-done.1.source, bf16[2,8,64,256]{3,2,1,0:T(8,128)(2,1)S(1)} %whiten_block.7.rest_0_.side0.side), custom_call_target="tpu_custom_call" | custom-call | flops 1000 | bytes 1000 | tf_op jit(solution)/shard_map/whiten_block/pallas_call | solution.py:128
  25.6 0.0 collective-permute-done.6.source
  25.6 0.8 %whiten_block.9.up.after = bf16[2,8,64,256]{3,2,1,0:T(8,128)(2,1)S(1)} custom-call(bf16[2,8,64,256]{3,2,1,0:T(8,128)(2,1)S(1)} %collective-permute-done.6.source, bf16[2,8,64,256]{3,2,1,0:T(8,128)(2,1)S(1)} %whiten_block.8.rest_0_.down0), custom_call_target="tpu_custom_call" | custom-call | flops 1000 | bytes 1000 | tf_op jit(solution)/shard_map/whiten_block/pallas_call | solution.py:128
  26.4 2.2 %collective-permute-done.4.side1.side = bf16[2,8,64,256]{3,2,1,0:T(8,128)(2,1)S(1)} collective-permute-done((bf16[2,8,64,256]{3,2,1,0:T(8,128)(2,1)S(1)}, bf16[2,8,64,256]{3,2,1,0:T(8,128)(2,1)S(1)}, u32[]{:S(2)}, u32[]{:S(2)}) %collective-permute-start.4) | collective-permute-done | bytes 524320 | tf_op jit(solution)/shard_map/ppermute | solution.py:364
  28.6 0.5 %back_kernel.2.after = bf16[4,64,512]{2,1,0:T(8,128)(2,1)S(1)} custom-call(bf16[2,8,64,256]{3,2,1,0:T(8,128)(2,1)S(1)} %whiten_block.6.mine_q, bf16[2,8,64,256]{3,2,1,0:T(8,128)(2,1)S(1)} %get-tuple-element.19.got_q, bf16[2,8,64,256]{3,2,1,0:T(8,128)(2,1)S(1)} %whiten_block.9.up.after, bf16[2,8,64,256]{3,2,1,0:T(8,128)(2,1)S(1)} %whiten_block.7.rest_0_.side0.side, ...), custom_call_target="tpu_custom_call" | custom-call | flops 1000 | bytes 1000 | tf_op jit(solution)/shard_map/back_kernel/pallas_call | solution.py:241
  29.1 1.3 %collective-permute-start.11 = (bf16[4,64,512]{2,1,0:T(8,128)(2,1)S(1)}, bf16[4,64,512]{2,1,0:T(8,128)(2,1)S(1)}, u32[]{:S(2)}, u32[]{:S(2)}) collective-permute-start(bf16[4,64,512]{2,1,0:T(8,128)(2,1)S(1)} %back_kernel.2.after), channel_id=1, source_target_pairs={{4,0},{5,1},{6,2},{7,3},{8,4},{9,5},{10,6},{11,7},{12,8},{13,9},{1... | collective-permute-start | bytes 786440 | tf_op jit(solution)/shard_map/ppermute | solution.py:380
  30.4 1.6 %collective-permute-done.3.down1 = bf16[2,8,64,256]{3,2,1,0:T(8,128)(2,1)S(1)} collective-permute-done((bf16[2,8,64,256]{3,2,1,0:T(8,128)(2,1)S(1)}, bf16[2,8,64,256]{3,2,1,0:T(8,128)(2,1)S(1)}, u32[]{:S(2)}, u32[]{:S(2)}) %collective-permute-start.3) | collective-permute-done | bytes 524320 | tf_op jit(solution)/shard_map/ppermute | solution.py:363
  32.0 0.5 %near_kernel.2.after = bf16[2,64,512]{2,1,0:T(8,128)(2,1)S(1)} custom-call(bf16[2,8,64,256]{3,2,1,0:T(8,128)(2,1)S(1)} %whiten_block.6.mine_q, bf16[2,8,64,256]{3,2,1,0:T(8,128)(2,1)S(1)} %get-tuple-element.19.got_q, bf16[2,8,64,256]{3,2,1,0:T(8,128)(2,1)S(1)} %whiten_block.8.rest_0_.down0, bf16[2,8,64,256]{3,2,1,0:T(8,128)(2,1)S(1)} %collective-permute-done.3.down1, ...), custom_call_target="tpu_custom_call" | custom-call | flops 1000 | bytes 1000 | tf_op jit(solution)/shard_map/near_kernel/pallas_call | solution.py:241
  32.5 0.8 %collective-permute-start.10 = (bf16[2,64,512]{2,1,0:T(8,128)(2,1)S(1)}, bf16[2,64,512]{2,1,0:T(8,128)(2,1)S(1)}, u32[]{:S(2)}, u32[]{:S(2)}) collective-permute-start(bf16[2,64,512]{2,1,0:T(8,128)(2,1)S(1)} %near_kernel.2.after), channel_id=1, source_target_pairs={{0,2},{1,3},{2,0},{3,1},{4,6},{5,7},{6,4},{7,5},{8,10},{9,11},{10,... | collective-permute-start | bytes 393224 | tf_op jit(solution)/shard_map/ppermute | solution.py:381
  33.2 0.0 collective-permute-done.5.up
  33.2 0.5 %back_kernel.3.after = bf16[4,64,512]{2,1,0:T(8,128)(2,1)S(1)} custom-call(bf16[2,8,64,256]{3,2,1,0:T(8,128)(2,1)S(1)} %whiten_block.6.mine_q, bf16[2,8,64,256]{3,2,1,0:T(8,128)(2,1)S(1)} %get-tuple-element.19.got_q, bf16[2,8,64,256]{3,2,1,0:T(8,128)(2,1)S(1)} %collective-permute-done.5.up, bf16[2,8,64,256]{3,2,1,0:T(8,128)(2,1)S(1)} %whiten_block.7.rest_0_.side0.side, ...), custom_call_target="tpu_custom_call" | custom-call | flops 1000 | bytes 1000 | tf_op jit(solution)/shard_map/back_kernel/pallas_call | solution.py:241
  33.7 1.3 %collective-permute-start.9 = (bf16[4,64,512]{2,1,0:T(8,128)(2,1)S(1)}, bf16[4,64,512]{2,1,0:T(8,128)(2,1)S(1)}, u32[]{:S(2)}, u32[]{:S(2)}) collective-permute-start(bf16[4,64,512]{2,1,0:T(8,128)(2,1)S(1)} %back_kernel.3.after), channel_id=1, source_target_pairs={{4,1},{5,0},{6,3},{7,2},{8,5},{9,4},{10,7},{11,6},{12,9},{13,8},{1... | collective-permute-start | bytes 786440 | tf_op jit(solution)/shard_map/ppermute | solution.py:384
  35.0 0.5 %near_kernel.3.after = bf16[2,64,512]{2,1,0:T(8,128)(2,1)S(1)} custom-call(bf16[2,8,64,256]{3,2,1,0:T(8,128)(2,1)S(1)} %whiten_block.6.mine_q, bf16[2,8,64,256]{3,2,1,0:T(8,128)(2,1)S(1)} %get-tuple-element.19.got_q, bf16[2,8,64,256]{3,2,1,0:T(8,128)(2,1)S(1)} %whiten_block.8.rest_0_.down0, bf16[2,8,64,256]{3,2,1,0:T(8,128)(2,1)S(1)} %collective-permute-done.3.down1, ...), custom_call_target="tpu_custom_call" | custom-call | flops 1000 | bytes 1000 | tf_op jit(solution)/shard_map/near_kernel/pallas_call | solution.py:241
  35.6 0.0 copy-start
  35.6 0.0 copy-start.1
  35.6 0.0 copy-start.2
  35.6 0.5 %collective-permute-start.8 = (bf16[2,64,512]{2,1,0:T(8,128)(2,1)S(1)}, bf16[2,64,512]{2,1,0:T(8,128)(2,1)S(1)}, u32[]{:S(2)}, u32[]{:S(2)}) collective-permute-start(bf16[2,64,512]{2,1,0:T(8,128)(2,1)S(1)} %near_kernel.3.after), channel_id=1, source_target_pairs={{0,3},{1,2},{2,1},{3,0},{4,7},{5,6},{6,5},{7,4},{8,11},{9,10},{10,... | collective-permute-start | bytes 393224 | tf_op jit(solution)/shard_map/ppermute | solution.py:382
  36.1 1.6 %own_kernel.1 = (bf16[6,64,512]{2,1,0:T(8,128)(2,1)S(1)}, bf16[6,64,512]{2,1,0:T(8,128)(2,1)S(1)}) custom-call(bf16[2,8,64,256]{3,2,1,0:T(8,128)(2,1)S(1)} %whiten_block.5.mine_p, bf16[2,8,64,256]{3,2,1,0:T(8,128)(2,1)S(1)} %get-tuple-element.16.got_p, bf16[2,8,64,256]{3,2,1,0:T(8,128)(2,1)S(1)} %whiten_block.8.rest_0_.down0, ...), custom_call_target="tpu_custom_call" | custom-call | flops 1000 | bytes 1000 | tf_op jit(solution)/shard_map/own_kernel/pallas_call | solution.py:241
  37.7 1.5 %collective-permute-start.7 = (bf16[6,64,512]{2,1,0:T(8,128)(2,1)S(1)}, bf16[6,64,512]{2,1,0:T(8,128)(2,1)S(1)}, u32[]{:S(2)}, u32[]{:S(2)}) collective-permute-start(bf16[6,64,512]{2,1,0:T(8,128)(2,1)S(1)} %get-tuple-element.21), channel_id=1, source_target_pairs={{0,1},{1,0},{2,3},{3,2},{4,5},{5,4},{6,7},{7,6},{8,9},{9,8},{10,11... | collective-permute-start | bytes 1179656 | tf_op jit(solution)/shard_map/ppermute | solution.py:383
  39.2 0.0 collective-permute-done.10.refs_3_
  39.2 0.2 collective-permute-done.11.refs_4_
  39.4 0.0 copy-done
  39.4 0.0 copy-done.1
  39.4 0.0 copy-done.2
  39.4 1.8 %lags.3.refs_5_ = bf16[1,4,256,512]{3,2,1,0:T(8,128)(2,1)} custom-call(s32[1,4]{1,0:T(1,128)S(1)} %copy-done.1, s32[1,4]{1,0:T(1,128)S(1)} %copy-done.2, bf16[6,64,512]{2,1,0:T(8,128)(2,1)S(1)} %get-tuple-element.22.refs_2_, bf16[2,64,512]{2,1,0:T(8,128)(2,1)S(1)} %collective-permute-done.10.refs_3_, ...), custom_call_target="tpu_custom_call" | custom-call | flops 10000000000 | bytes 40000000 | tf_op jit(solution)/shard_map/lags/pallas_call | solution.py:311
  41.2 0.0 collective-permute-done.8.refs_3_
  41.2 0.0 collective-permute-done.7.refs_2_
  41.2 1.6 %lags.4.refs_6_ = bf16[1,4,256,512]{3,2,1,0:T(8,128)(2,1)} custom-call(s32[1,4]{1,0:T(1,128)S(1)} %copy-done.1, s32[1,4]{1,0:T(1,128)S(1)} %copy-done.2, bf16[6,64,512]{2,1,0:T(8,128)(2,1)S(1)} %collective-permute-done.7.refs_2_, bf16[2,64,512]{2,1,0:T(8,128)(2,1)S(1)} %collective-permute-done.8.refs_3_, ...), custom_call_target="tpu_custom_call", output_to_operand_aliasing={{}: (5, {})} | custom-call | flops 10000000000 | bytes 40000000 | tf_op jit(solution)/shard_map/lags/pallas_call | solution.py:311
  42.8 1.1 %collective-permute-done.9.refs_4_ = bf16[4,64,512]{2,1,0:T(8,128)(2,1)S(1)} collective-permute-done((bf16[4,64,512]{2,1,0:T(8,128)(2,1)S(1)}, bf16[4,64,512]{2,1,0:T(8,128)(2,1)S(1)}, u32[]{:S(2)}, u32[]{:S(2)}) %collective-permute-start.9) | collective-permute-done | bytes 262176 | tf_op jit(solution)/shard_map/ppermute | solution.py:384
  43.9 1.5 %lags.5 = bf16[1,4,256,512]{3,2,1,0:T(8,128)(2,1)} custom-call(s32[1,4]{1,0:T(1,128)S(1)} %copy-done.1, s32[1,4]{1,0:T(1,128)S(1)} %copy-done.2, bf16[6,64,512]{2,1,0:T(8,128)(2,1)S(1)} %collective-permute-done.7.refs_2_, bf16[2,64,512]{2,1,0:T(8,128)(2,1)S(1)} %collective-permute-done.8.refs_3_, ...), custom_call_target="tpu_custom_call", output_to_operand_aliasing={{}: (6, {})} | custom-call | flops 1000 | bytes 1000 | tf_op jit(solution)/shard_map/lags/pallas_call | solution.py:311
Async XLA Ops:
  1.8 9.0 %collective-permute-start = (bf16[2,2,8,64,256]{4,3,2,1,0:T(8,128)(2,1)S(1)}, bf16[2,2,8,64,256]{4,3,2,1,0:T(8,128)(2,1)S(1)}, u32[]{:S(2)}, u32[]{:S(2)}) collective-permute-start(bf16[2,2,8,64,256]{4,3,2,1,0:T(8,128)(2,1)S(1)} %get-tuple-element.15), channel_id=1, source_target_pairs={{0,1},{1,0},{2,3},{3,2},{4,5},{5,4},{6,7},{7,6},{8,9},{9,8},{10,11... | collective-permute-start | bytes 3145736 | tf_op jit(solution)/shard_map/ppermute | solution.py:358
  2.2 15.4 %collective-permute-start.2 = (bf16[2,8,64,256]{3,2,1,0:T(8,128)(2,1)S(1)}, bf16[2,8,64,256]{3,2,1,0:T(8,128)(2,1)S(1)}, u32[]{:S(2)}, u32[]{:S(2)}) collective-permute-start(bf16[2,8,64,256]{3,2,1,0:T(8,128)(2,1)S(1)} %get-tuple-element.17), channel_id=1, source_target_pairs={{0,2},{1,3},{2,0},{3,1},{4,6},{5,7},{6,4},{7,5},{8,10},{9,11},{10,... | collective-permute-start | bytes 1572872 | tf_op jit(solution)/shard_map/ppermute | solution.py:360
  4.9 19.9 %collective-permute-start.1 = (bf16[2,8,64,256]{3,2,1,0:T(8,128)(2,1)S(1)}, bf16[2,8,64,256]{3,2,1,0:T(8,128)(2,1)S(1)}, u32[]{:S(2)}, u32[]{:S(2)}) collective-permute-start(bf16[2,8,64,256]{3,2,1,0:T(8,128)(2,1)S(1)} %get-tuple-element.14.source), channel_id=1, source_target_pairs={{4,0},{5,1},{6,2},{7,3},{8,4},{9,5},{10,6},{11,7},{12,8},{13,9},{1... | collective-permute-start | bytes 1572872 | tf_op jit(solution)/shard_map/ppermute | solution.py:359
  6.1 19.4 %collective-permute-start.6 = (bf16[2,8,64,256]{3,2,1,0:T(8,128)(2,1)S(1)}, bf16[2,8,64,256]{3,2,1,0:T(8,128)(2,1)S(1)}, u32[]{:S(2)}, u32[]{:S(2)}) collective-permute-start(bf16[2,8,64,256]{3,2,1,0:T(8,128)(2,1)S(1)} %get-tuple-element.18.source), channel_id=1, source_target_pairs={{0,4},{1,5},{2,6},{3,7},{4,8},{5,9},{6,10},{7,11},{8,12},{9,13},{1... | collective-permute-start | bytes 1572872 | tf_op jit(solution)/shard_map/ppermute | solution.py:361
  12.4 16.2 %collective-permute-start.4 = (bf16[2,8,64,256]{3,2,1,0:T(8,128)(2,1)S(1)}, bf16[2,8,64,256]{3,2,1,0:T(8,128)(2,1)S(1)}, u32[]{:S(2)}, u32[]{:S(2)}) collective-permute-start(bf16[2,8,64,256]{3,2,1,0:T(8,128)(2,1)S(1)} %get-tuple-element.20), channel_id=1, source_target_pairs={{0,2},{1,3},{2,0},{3,1},{4,6},{5,7},{6,4},{7,5},{8,10},{9,11},{10,... | collective-permute-start | bytes 1572872 | tf_op jit(solution)/shard_map/ppermute | solution.py:364
  12.6 19.4 %collective-permute-start.3 = (bf16[2,8,64,256]{3,2,1,0:T(8,128)(2,1)S(1)}, bf16[2,8,64,256]{3,2,1,0:T(8,128)(2,1)S(1)}, u32[]{:S(2)}, u32[]{:S(2)}) collective-permute-start(bf16[2,8,64,256]{3,2,1,0:T(8,128)(2,1)S(1)} %get-tuple-element.16.got_p), channel_id=1, source_target_pairs={{4,0},{5,1},{6,2},{7,3},{8,4},{9,5},{10,6},{11,7},{12,8},{13,9},{1... | collective-permute-start | bytes 1572872 | tf_op jit(solution)/shard_map/ppermute | solution.py:363
  17.6 15.6 %collective-permute-start.5 = (bf16[2,8,64,256]{3,2,1,0:T(8,128)(2,1)S(1)}, bf16[2,8,64,256]{3,2,1,0:T(8,128)(2,1)S(1)}, u32[]{:S(2)}, u32[]{:S(2)}) collective-permute-start(bf16[2,8,64,256]{3,2,1,0:T(8,128)(2,1)S(1)} %get-tuple-element.19.got_q), channel_id=1, source_target_pairs={{0,4},{1,5},{2,6},{3,7},{4,8},{5,9},{6,10},{7,11},{8,12},{9,13},{1... | collective-permute-start | bytes 1572872 | tf_op jit(solution)/shard_map/ppermute | solution.py:365
  29.1 10.3 %collective-permute-start.11 = (bf16[4,64,512]{2,1,0:T(8,128)(2,1)S(1)}, bf16[4,64,512]{2,1,0:T(8,128)(2,1)S(1)}, u32[]{:S(2)}, u32[]{:S(2)}) collective-permute-start(bf16[4,64,512]{2,1,0:T(8,128)(2,1)S(1)} %back_kernel.2.after), channel_id=1, source_target_pairs={{4,0},{5,1},{6,2},{7,3},{8,4},{9,5},{10,6},{11,7},{12,8},{13,9},{1... | collective-permute-start | bytes 786440 | tf_op jit(solution)/shard_map/ppermute | solution.py:380
  32.5 6.8 %collective-permute-start.10 = (bf16[2,64,512]{2,1,0:T(8,128)(2,1)S(1)}, bf16[2,64,512]{2,1,0:T(8,128)(2,1)S(1)}, u32[]{:S(2)}, u32[]{:S(2)}) collective-permute-start(bf16[2,64,512]{2,1,0:T(8,128)(2,1)S(1)} %near_kernel.2.after), channel_id=1, source_target_pairs={{0,2},{1,3},{2,0},{3,1},{4,6},{5,7},{6,4},{7,5},{8,10},{9,11},{10,... | collective-permute-start | bytes 393224 | tf_op jit(solution)/shard_map/ppermute | solution.py:381
  33.7 10.1 %collective-permute-start.9 = (bf16[4,64,512]{2,1,0:T(8,128)(2,1)S(1)}, bf16[4,64,512]{2,1,0:T(8,128)(2,1)S(1)}, u32[]{:S(2)}, u32[]{:S(2)}) collective-permute-start(bf16[4,64,512]{2,1,0:T(8,128)(2,1)S(1)} %back_kernel.3.after), channel_id=1, source_target_pairs={{4,1},{5,0},{6,3},{7,2},{8,5},{9,4},{10,7},{11,6},{12,9},{13,8},{1... | collective-permute-start | bytes 786440 | tf_op jit(solution)/shard_map/ppermute | solution.py:384
  35.6 3.9 %copy-start = (bf16[512,512]{1,0:T(8,128)(2,1)S(1)}, bf16[512,512]{1,0:T(8,128)(2,1)}, u32[]{:S(2)}) copy-start(bf16[512,512]{1,0:T(8,128)(2,1)} %constant.2.clone.refs_5_.refs_4_) | copy-start | bytes 1572868
  35.6 3.9 %copy-start.1 = (s32[1,4]{1,0:T(1,128)S(1)}, s32[1,4]{1,0:T(1,128)}, u32[]{:S(2)}) copy-start(s32[1,4]{1,0:T(1,128)} %refs_0_.5) | copy-start | bytes 52
  35.6 3.9 %copy-start.2 = (s32[1,4]{1,0:T(1,128)S(1)}, s32[1,4]{1,0:T(1,128)}, u32[]{:S(2)}) copy-start(s32[1,4]{1,0:T(1,128)} %refs_1_.5) | copy-start | bytes 52
  35.6 5.6 %collective-permute-start.8 = (bf16[2,64,512]{2,1,0:T(8,128)(2,1)S(1)}, bf16[2,64,512]{2,1,0:T(8,128)(2,1)S(1)}, u32[]{:S(2)}, u32[]{:S(2)}) collective-permute-start(bf16[2,64,512]{2,1,0:T(8,128)(2,1)S(1)} %near_kernel.3.after), channel_id=1, source_target_pairs={{0,3},{1,2},{2,1},{3,0},{4,7},{5,6},{6,5},{7,4},{8,11},{9,10},{10,... | collective-permute-start | bytes 393224 | tf_op jit(solution)/shard_map/ppermute | solution.py:382
  37.7 3.5 %collective-permute-start.7 = (bf16[6,64,512]{2,1,0:T(8,128)(2,1)S(1)}, bf16[6,64,512]{2,1,0:T(8,128)(2,1)S(1)}, u32[]{:S(2)}, u32[]{:S(2)}) collective-permute-start(bf16[6,64,512]{2,1,0:T(8,128)(2,1)S(1)} %get-tuple-element.21), channel_id=1, source_target_pairs={{0,1},{1,0},{2,3},{3,2},{4,5},{5,4},{6,7},{7,6},{8,9},{9,8},{10,11... | collective-permute-start | bytes 1179656 | tf_op jit(solution)/shard_map/ppermute | solution.py:383

commit v6 on v5

--- a/solution.py
+++ b/solution.py
@@ -249,9 +249,8 @@
     )(*blocks, *extra)
 
 
-def lag_kernel(flip, classes, offsets, limits, own, side, back, table, out, cand, chosen, lagged, sent):
-    core, x = place()
-    half = core if flip == 0 else 1 - core
+def lag_rows(classes, offsets, limits, own, side, back, table, lagged, cand, chosen):
+    core, x = place()
     rows, lags = own.shape[1], table.shape[1]
     for spot, k in enumerate(classes):
         part = pl.ds(spot * rows, rows)
@@ -268,64 +267,121 @@
 
     lag = lax.broadcasted_iota(jnp.int32, (1, lags), 1)
     distance = jnp.minimum(lag, lags - lag)
-    height = len(classes) * rows
-    for slot in range(out.shape[1]):
+    height, slots = len(classes) * rows, lagged.shape[0]
+    for slot in range(slots):
         offset = offsets[0, slot]
         chosen[pl.ds(slot * height, height), :] = cand[jnp.clip(offset - 1 + core, 0, 4)]
     product = jnp.dot(chosen[...], table[...], preferred_element_type=jnp.float32)
-    copies = []
-    for slot in range(out.shape[1]):
+    for slot in range(slots):
         limit = jnp.where(offsets[0, slot] > 0, limits[0, slot], 0)
         kept = jnp.where(distance < limit, product[slot * height : (slot + 1) * height], 0.0)
         lagged[slot] = kept.astype(jnp.bfloat16)
-        for spot, k in enumerate(classes):
-            target = pl.multiple_of((2 * k + half) * rows, rows)
-            copies.append(
-                pltpu.make_async_copy(
-                    lagged.at[slot, pl.ds(spot * rows, rows), :],
-                    out.at[0, slot, pl.ds(target, rows), :],
-                    sent.at[slot, spot],
+
+
+def lag_part(classes, offsets, limits, *pieces, choose=False):
+    rows, width = pieces[0].shape[1:]
+    slots, lags = offsets.shape[1], pieces[-1].shape[1]
+    height = len(classes) * rows
+    vmem = pl.BlockSpec(memory_space=pltpu.VMEM)
+    smem = pl.BlockSpec(memory_space=pltpu.SMEM)
+
+    def kernel(*refs):
+        refs = list(refs)
+        if 1 not in classes:
+            refs.insert(4, None)
+        if choose:
+            choice, kept = refs.pop(7), refs.pop(7)
+            core, _ = place()
+            row = lax.broadcasted_iota(jnp.int32, (rows, 6 * rows), 0)
+            column = lax.broadcasted_iota(jnp.int32, (rows, 6 * rows), 1)
+            lag = lax.broadcasted_iota(jnp.int32, (1, lags), 1)
+            distance = jnp.minimum(lag, lags - lag)
+            for slot in range(slots):
+                offset = refs[0][0, slot]
+                spot = jnp.clip(offset - 1 + core, 0, 4) * rows
+                choice[pl.ds(slot * rows, rows), :] = jnp.where(column == row + spot, 1.0, 0.0).astype(
+                    jnp.bfloat16
                 )
-            )
-            copies[-1].start()
+                limit = jnp.where(offset > 0, refs[1][0, slot], 0)
+                kept[pl.ds(slot, 1), :] = jnp.where(distance < limit, 1.0, 0.0)
+        lag_rows(classes, *refs)
+
+    out_shape = [jax.ShapeDtypeStruct((slots, height, lags), jnp.bfloat16)]
+    if choose:
+        out_shape.append(jax.ShapeDtypeStruct((slots * rows, 6 * rows), jnp.bfloat16))
+        out_shape.append(jax.ShapeDtypeStruct((slots, lags), jnp.float32))
+    return pl.pallas_call(
+        kernel,
+        out_shape=out_shape,
+        in_specs=[smem] * 2 + [vmem] * len(pieces),
+        out_specs=[vmem] * len(out_shape),
+        scratch_shapes=[
+            pltpu.VMEM((5, height, width), jnp.bfloat16),
+            pltpu.VMEM((slots * height, width), jnp.bfloat16),
+        ],
+        compiler_params=pltpu.CompilerParams(vmem_limit_bytes=VMEM_LIMIT),
+        cost_estimate=LARGE,
+        name="lags",
+    )(offsets, limits, *pieces)
+
+
+def last_kernel(own, side, back, table, straight, crossed, choice, kept, out, lagged, cand, sent):
+    core, x = place()
+    slots, rows = lagged.shape[:2]
+    copies = []
+
+    def leave(source, k, half):
+        target = pl.multiple_of((2 * k + half) * rows, rows)
+        target = out.at[0, :, pl.ds(target, rows), :]
+        copies.append(pltpu.make_async_copy(source, target, sent.at[len(copies)]))
+        copies[-1].start()
+
+    leave(straight.at[:, pl.ds(0, rows), :], 0, core)
+    leave(straight.at[:, pl.ds(rows, rows), :], 1, core)
+    leave(crossed, 0, 1 - core)
+    cand[0] = own[5]
+    cand[3:5] = back[2:4]
+    cand[5] = jnp.zeros(cand.shape[1:], cand.dtype)
+
+    @pl.when(x == 0)
+    def _():
+        cand[1:3] = side[...]
+
+    @pl.when(x == 1)
+    def _():
+        cand[1:3] = back[0:2]
+
+    spectrum = jnp.dot(
+        choice[...], cand[...].reshape(6 * rows, -1), preferred_element_type=jnp.float32
+    ).astype(jnp.bfloat16)
+    product = jnp.dot(spectrum, table[...], preferred_element_type=jnp.float32)
+    for slot in range(slots):
+        keep = kept[pl.ds(slot, 1), :] > 0.0
+        part = jnp.where(keep, product[slot * rows : (slot + 1) * rows], 0.0)
+        lagged[slot] = part.astype(jnp.bfloat16)
+    leave(lagged, 1, 1 - core)
     for copy in copies:
         copy.wait()
 
 
-def lag_products(flip, classes, cost, offsets, limits, own, side, back, table, earlier):
-    rows, width = own.shape[1:]
-    slots, lags = offsets.shape[1], table.shape[1]
+def last_part(*pieces):
+    rows, width = pieces[0].shape[1:]
+    slots, _, lags = pieces[4].shape
     vmem = pl.BlockSpec(memory_space=pltpu.VMEM)
-    smem = pl.BlockSpec(memory_space=pltpu.SMEM)
-    pieces = [own, side] + ([] if back is None else [back]) + [table]
-    extra = [] if earlier is None else [earlier]
-
-    def kernel(*refs):
-        refs = list(refs)
-        if earlier is not None:
-            del refs[2 + len(pieces)]
-        if back is None:
-            refs.insert(4, None)
-        lag_kernel(flip, classes, *refs)
-
-    return pl.pallas_call(
-        kernel,
+    return pl.pallas_call(
+        last_kernel,
         out_shape=jax.ShapeDtypeStruct((1, slots, 4 * rows, lags), jnp.bfloat16),
-        in_specs=[smem] * 2
-        + [vmem] * len(pieces)
-        + [pl.BlockSpec(memory_space=pl.ANY)] * len(extra),
+        in_specs=[vmem] * len(pieces),
         out_specs=pl.BlockSpec(memory_space=pl.ANY),
         scratch_shapes=[
-            pltpu.VMEM((5, len(classes) * rows, width), jnp.bfloat16),
-            pltpu.VMEM((slots * len(classes) * rows, width), jnp.bfloat16),
-            pltpu.VMEM((slots, len(classes) * rows, lags), jnp.bfloat16),
-            pltpu.SemaphoreType.DMA((slots, len(classes))),
+            pltpu.VMEM((slots, rows, lags), jnp.bfloat16),
+            pltpu.VMEM((6, rows, width), jnp.bfloat16),
+            pltpu.SemaphoreType.DMA((4,)),
         ],
-        input_output_aliases={2 + len(pieces): 0} if extra else {},
         compiler_params=pltpu.CompilerParams(vmem_limit_bytes=VMEM_LIMIT),
-        cost_estimate=cost,
-        name="lags",
-    )(offsets, limits, *pieces, *extra)
+        cost_estimate=SMALL,
+        name="last",
+    )(*pieces)
 
 
 def phase_table(bins, lag_count):
@@ -379,13 +435,13 @@
     )
     zs = move["down"](zs)
     xs = move["xs"](xs)
+    zd = move["crossed"](zd)
     xd = move["xd"](xd)
     own_chip = move["chip"](own_chip)
-    zd = move["crossed"](zd)
     slots = (pair_offset, lag_limit)
-    out = lag_products(0, (0, 1), LARGE, *slots, own_here, xs, zs, table, None)
-    out = lag_products(1, (0,), LARGE, *slots, own_chip, xd, None, table, out)
-    return lag_products(1, (1,), SMALL, *slots, own_chip, xd, zd, table, out)
+    (straight,) = lag_part((0, 1), *slots, own_here, xs, zs, table)
+    crossed, choice, kept = lag_part((0,), *slots, own_chip, xd, table, choose=True)
+    return last_part(own_chip, xd, zd, table, straight, crossed, choice, kept)
 
 
 def solution(mesh):

time: 45.9 us -> 45.6 us (level)
  Pallas kernels: 16.7 us -> 15 us
  waiting for transfers between devices: 8.8 us -> 10.2 us
    pallas_call x3, Pallas kernels: 4.88 us -> 3.21 us  [the longest x2 1.94 us: lag_part(): pl.pallas_call(kernel, out_shape=out_shape, in_specs=[smem] * 2 + [vmem]...]
    ppermute x1, waiting for transfers between devices: 0.01 us -> 0.72 us  [local(): xd = move['xd'](xd)]
    ppermute x1, waiting for transfers between devices: 1.07 us -> 1.77 us  [local(): zd = move['crossed'](zd)]
  transfers between devices with their start and end apart: 12 -> 12, of which waited for: 5 -> 6; matrix products, arithmetic and copies ran while one was open for 0% -> 0% of each run, Pallas kernels for 29% -> 26%
where the time goes in v6:
time: 45.6 us; the launch traced here: 45.2 us
  starting transfers between devices  19.7 us (43%)
  Pallas kernels  15 us (33%)
  waiting for transfers between devices  10.2 us (22%)
    ppermute x1, starting transfers between devices, local(): up0 = move['up'](up_raw)  4.58 us
    pallas_call x6, Pallas kernels, cross(): pl.pallas_call(kernel, out_shape=[jax.ShapeDtypeStruct((n, rows, 2 * bins...  4.3 us
    pallas_call x5, Pallas kernels, whiten_block(): pl.pallas_call(whiten_block_kernel, out_shape=jax.ShapeDtypeStruct(block....  4.06 us
    ppermute x1, starting transfers between devices, local(): up1 = move['up'](got_q)  3.95 us
    ppermute x1, waiting for transfers between devices, local(): side0 = move['xs'](side_raw)  3.78 us
    ppermute x1, starting transfers between devices, local(): side0 = move['xs'](side_raw)  2.61 us
    ppermute x1, waiting for transfers between devices, local(): side1 = move['xs'](got_side)  2.19 us
    pallas_call x2, Pallas kernels, lag_part(): pl.pallas_call(kernel, out_shape=out_shape, in_specs=[smem] * 2 + [vmem]...  1.94 us
  transfers between devices with their start and end apart: 12, of which 6 were waited for; matrix products, arithmetic and copies ran while one was open for 0% of the time, Pallas kernels for 26%

profile of v6, /device:TPU:0, one launch (start us, length us, event | category | flops | bytes accessed | tf_op | source)
XLA Modules:
  0.0 45.2 jit_solution(15116118254453772185)
XLA Ops:
  0.0 1.8 %quarters.1 = (bf16[2,2,8,64,256]{4,3,2,1,0:T(8,128)(2,1)S(1)}, bf16[2,8,64,256]{3,2,1,0:T(8,128)(2,1)S(1)}, bf16[2,8,64,256]{3,2,1,0:T(8,128)(2,1)S(1)}, bf16[2,8,64,256]{3,2,1,0:T(8,128)(2,1)S(1)}) custom-call(bf16[1,2,8,256,256]{4,3,2,1,0:T(8,128)(2,1)} %spectra.1), custom_call_target="tpu_custom_call" | custom-call | flops 1000 | bytes 1000 | tf_op jit(solution)/shard_map/quarters/pallas_call | solution.py:65
  1.8 0.5 %collective-permute-start = (bf16[2,2,8,64,256]{4,3,2,1,0:T(8,128)(2,1)S(1)}, bf16[2,2,8,64,256]{4,3,2,1,0:T(8,128)(2,1)S(1)}, u32[]{:S(2)}, u32[]{:S(2)}) collective-permute-start(bf16[2,2,8,64,256]{4,3,2,1,0:T(8,128)(2,1)S(1)} %get-tuple-element.18), channel_id=1, source_target_pairs={{0,1},{1,0},{2,3},{3,2},{4,5},{5,4},{6,7},{7,6},{8,9},{9,8},{10,11... | collective-permute-start | bytes 3145736 | tf_op jit(solution)/shard_map/ppermute | solution.py:414
  2.2 2.6 %collective-permute-start.2 = (bf16[2,8,64,256]{3,2,1,0:T(8,128)(2,1)S(1)}, bf16[2,8,64,256]{3,2,1,0:T(8,128)(2,1)S(1)}, u32[]{:S(2)}, u32[]{:S(2)}) collective-permute-start(bf16[2,8,64,256]{3,2,1,0:T(8,128)(2,1)S(1)} %get-tuple-element.20), channel_id=1, source_target_pairs={{0,2},{1,3},{2,0},{3,1},{4,6},{5,7},{6,4},{7,5},{8,10},{9,11},{10,... | collective-permute-start | bytes 1572872 | tf_op jit(solution)/shard_map/ppermute | solution.py:416
  4.9 1.3 %collective-permute-start.1 = (bf16[2,8,64,256]{3,2,1,0:T(8,128)(2,1)S(1)}, bf16[2,8,64,256]{3,2,1,0:T(8,128)(2,1)S(1)}, u32[]{:S(2)}, u32[]{:S(2)}) collective-permute-start(bf16[2,8,64,256]{3,2,1,0:T(8,128)(2,1)S(1)} %get-tuple-element.17.source), channel_id=1, source_target_pairs={{4,0},{5,1},{6,2},{7,3},{8,4},{9,5},{10,6},{11,7},{12,8},{13,9},{1... | collective-permute-start | bytes 1572872 | tf_op jit(solution)/shard_map/ppermute | solution.py:415
  6.1 4.6 %collective-permute-start.6 = (bf16[2,8,64,256]{3,2,1,0:T(8,128)(2,1)S(1)}, bf16[2,8,64,256]{3,2,1,0:T(8,128)(2,1)S(1)}, u32[]{:S(2)}, u32[]{:S(2)}) collective-permute-start(bf16[2,8,64,256]{3,2,1,0:T(8,128)(2,1)S(1)} %get-tuple-element.21.source), channel_id=1, source_target_pairs={{0,4},{1,5},{2,6},{3,7},{4,8},{5,9},{6,10},{7,11},{8,12},{9,13},{1... | collective-permute-start | bytes 1572872 | tf_op jit(solution)/shard_map/ppermute | solution.py:417
  10.7 0.0 collective-permute-done.got
  10.7 1.7 %whiten_got.1 = (bf16[2,8,64,256]{3,2,1,0:T(8,128)(2,1)S(1)}, bf16[2,8,64,256]{3,2,1,0:T(8,128)(2,1)S(1)}, bf16[2,8,64,256]{3,2,1,0:T(8,128)(2,1)S(1)}) custom-call(bf16[2,2,8,64,256]{4,3,2,1,0:T(8,128)(2,1)S(1)} %collective-permute-done.got), custom_call_target="tpu_custom_call" | custom-call | flops 1000 | bytes 1000 | tf_op jit(solution)/shard_map/whiten_got/pallas_call | solution.py:102
  12.4 0.1 collective-permute-start.4
  12.6 1.3 %collective-permute-start.3 = (bf16[2,8,64,256]{3,2,1,0:T(8,128)(2,1)S(1)}, bf16[2,8,64,256]{3,2,1,0:T(8,128)(2,1)S(1)}, u32[]{:S(2)}, u32[]{:S(2)}) collective-permute-start(bf16[2,8,64,256]{3,2,1,0:T(8,128)(2,1)S(1)} %get-tuple-element.19.got_p), channel_id=1, source_target_pairs={{4,0},{5,1},{6,2},{7,3},{8,4},{9,5},{10,6},{11,7},{12,8},{13,9},{1... | collective-permute-start | bytes 1572872 | tf_op jit(solution)/shard_map/ppermute | solution.py:419
  13.9 3.8 %collective-permute-done.2.source = bf16[2,8,64,256]{3,2,1,0:T(8,128)(2,1)S(1)} collective-permute-done((bf16[2,8,64,256]{3,2,1,0:T(8,128)(2,1)S(1)}, bf16[2,8,64,256]{3,2,1,0:T(8,128)(2,1)S(1)}, u32[]{:S(2)}, u32[]{:S(2)}) %collective-permute-start.2) | collective-permute-done | bytes 524320 | tf_op jit(solution)/shard_map/ppermute | solution.py:416
  17.6 3.9 %collective-permute-start.5 = (bf16[2,8,64,256]{3,2,1,0:T(8,128)(2,1)S(1)}, bf16[2,8,64,256]{3,2,1,0:T(8,128)(2,1)S(1)}, u32[]{:S(2)}, u32[]{:S(2)}) collective-permute-start(bf16[2,8,64,256]{3,2,1,0:T(8,128)(2,1)S(1)} %get-tuple-element.22.got_q), channel_id=1, source_target_pairs={{0,4},{1,5},{2,6},{3,7},{4,8},{5,9},{6,10},{7,11},{8,12},{9,13},{1... | collective-permute-start | bytes 1572872 | tf_op jit(solution)/shard_map/ppermute | solution.py:421
  21.6 0.8 %whiten_block.6.mine_q = bf16[2,8,64,256]{3,2,1,0:T(8,128)(2,1)S(1)} custom-call(bf16[2,8,64,256]{3,2,1,0:T(8,128)(2,1)S(1)} %get-tuple-element.21.source), custom_call_target="tpu_custom_call" | custom-call | flops 1000 | bytes 1000 | tf_op jit(solution)/shard_map/whiten_block/pallas_call | solution.py:128
  22.4 0.8 %whiten_block.5.mine_p = bf16[2,8,64,256]{3,2,1,0:T(8,128)(2,1)S(1)} custom-call(bf16[2,8,64,256]{3,2,1,0:T(8,128)(2,1)S(1)} %get-tuple-element.17.source), custom_call_target="tpu_custom_call" | custom-call | flops 1000 | bytes 1000 | tf_op jit(solution)/shard_map/whiten_block/pallas_call | solution.py:128
  23.2 0.7 %chip_kernel.1.rest_0_.pair = bf16[2,64,512]{2,1,0:T(8,128)(2,1)S(1)} custom-call(bf16[2,8,64,256]{3,2,1,0:T(8,128)(2,1)S(1)} %whiten_block.5.mine_p, bf16[2,8,64,256]{3,2,1,0:T(8,128)(2,1)S(1)} %get-tuple-element.19.got_p, bf16[2,8,64,256]{3,2,1,0:T(8,128)(2,1)S(1)} %whiten_block.6.mine_q, bf16[2,8,64,256]{3,2,1,0:T(8,128)(2,1)S(1)} %get-tuple-element.22.got_q), custom_call_target="tpu_custom_call" | custom-call | flops 1000 | bytes 1000 | tf_op jit(solution)/shard_map/chip_kernel/pallas_call | solution.py:241
  23.9 0.8 %whiten_block.7.rest_0_.side0.side = bf16[2,8,64,256]{3,2,1,0:T(8,128)(2,1)S(1)} custom-call(bf16[2,8,64,256]{3,2,1,0:T(8,128)(2,1)S(1)} %collective-permute-done.2.source, bf16[2,64,512]{2,1,0:T(8,128)(2,1)S(1)} %chip_kernel.1.rest_0_.pair), custom_call_target="tpu_custom_call" | custom-call | flops 1000 | bytes 1000 | tf_op jit(solution)/shard_map/whiten_block/pallas_call | solution.py:128
  24.8 0.0 collective-permute-done.1.source
  24.8 0.8 %whiten_block.8.rest_0_.down0 = bf16[2,8,64,256]{3,2,1,0:T(8,128)(2,1)S(1)} custom-call(bf16[2,8,64,256]{3,2,1,0:T(8,128)(2,1)S(1)} %collective-permute-done.1.source, bf16[2,8,64,256]{3,2,1,0:T(8,128)(2,1)S(1)} %whiten_block.7.rest_0_.side0.side), custom_call_target="tpu_custom_call" | custom-call | flops 1000 | bytes 1000 | tf_op jit(solution)/shard_map/whiten_block/pallas_call | solution.py:128
  25.6 0.0 collective-permute-done.6.source
  25.6 0.8 %whiten_block.9.up.after = bf16[2,8,64,256]{3,2,1,0:T(8,128)(2,1)S(1)} custom-call(bf16[2,8,64,256]{3,2,1,0:T(8,128)(2,1)S(1)} %collective-permute-done.6.source, bf16[2,8,64,256]{3,2,1,0:T(8,128)(2,1)S(1)} %whiten_block.8.rest_0_.down0), custom_call_target="tpu_custom_call" | custom-call | flops 1000 | bytes 1000 | tf_op jit(solution)/shard_map/whiten_block/pallas_call | solution.py:128
  26.4 2.2 %collective-permute-done.4.side1.side = bf16[2,8,64,256]{3,2,1,0:T(8,128)(2,1)S(1)} collective-permute-done((bf16[2,8,64,256]{3,2,1,0:T(8,128)(2,1)S(1)}, bf16[2,8,64,256]{3,2,1,0:T(8,128)(2,1)S(1)}, u32[]{:S(2)}, u32[]{:S(2)}) %collective-permute-start.4) | collective-permute-done | bytes 524320 | tf_op jit(solution)/shard_map/ppermute | solution.py:420
  28.6 0.5 %back_kernel.2.after = bf16[4,64,512]{2,1,0:T(8,128)(2,1)S(1)} custom-call(bf16[2,8,64,256]{3,2,1,0:T(8,128)(2,1)S(1)} %whiten_block.6.mine_q, bf16[2,8,64,256]{3,2,1,0:T(8,128)(2,1)S(1)} %get-tuple-element.22.got_q, bf16[2,8,64,256]{3,2,1,0:T(8,128)(2,1)S(1)} %whiten_block.9.up.after, bf16[2,8,64,256]{3,2,1,0:T(8,128)(2,1)S(1)} %whiten_block.7.rest_0_.side0.side, ...), custom_call_target="tpu_custom_call" | custom-call | flops 1000 | bytes 1000 | tf_op jit(solution)/shard_map/back_kernel/pallas_call | solution.py:241
  29.1 1.3 %collective-permute-start.11 = (bf16[4,64,512]{2,1,0:T(8,128)(2,1)S(1)}, bf16[4,64,512]{2,1,0:T(8,128)(2,1)S(1)}, u32[]{:S(2)}, u32[]{:S(2)}) collective-permute-start(bf16[4,64,512]{2,1,0:T(8,128)(2,1)S(1)} %back_kernel.2.after), channel_id=1, source_target_pairs={{4,0},{5,1},{6,2},{7,3},{8,4},{9,5},{10,6},{11,7},{12,8},{13,9},{1... | collective-permute-start | bytes 786440 | tf_op jit(solution)/shard_map/ppermute | solution.py:436
  30.4 1.6 %collective-permute-done.3.down1 = bf16[2,8,64,256]{3,2,1,0:T(8,128)(2,1)S(1)} collective-permute-done((bf16[2,8,64,256]{3,2,1,0:T(8,128)(2,1)S(1)}, bf16[2,8,64,256]{3,2,1,0:T(8,128)(2,1)S(1)}, u32[]{:S(2)}, u32[]{:S(2)}) %collective-permute-start.3) | collective-permute-done | bytes 524320 | tf_op jit(solution)/shard_map/ppermute | solution.py:419
  32.0 0.5 %near_kernel.2.after = bf16[2,64,512]{2,1,0:T(8,128)(2,1)S(1)} custom-call(bf16[2,8,64,256]{3,2,1,0:T(8,128)(2,1)S(1)} %whiten_block.6.mine_q, bf16[2,8,64,256]{3,2,1,0:T(8,128)(2,1)S(1)} %get-tuple-element.22.got_q, bf16[2,8,64,256]{3,2,1,0:T(8,128)(2,1)S(1)} %whiten_block.8.rest_0_.down0, bf16[2,8,64,256]{3,2,1,0:T(8,128)(2,1)S(1)} %collective-permute-done.3.down1, ...), custom_call_target="tpu_custom_call" | custom-call | flops 1000 | bytes 1000 | tf_op jit(solution)/shard_map/near_kernel/pallas_call | solution.py:241
  32.5 0.8 %collective-permute-start.10 = (bf16[2,64,512]{2,1,0:T(8,128)(2,1)S(1)}, bf16[2,64,512]{2,1,0:T(8,128)(2,1)S(1)}, u32[]{:S(2)}, u32[]{:S(2)}) collective-permute-start(bf16[2,64,512]{2,1,0:T(8,128)(2,1)S(1)} %near_kernel.2.after), channel_id=1, source_target_pairs={{0,2},{1,3},{2,0},{3,1},{4,6},{5,7},{6,4},{7,5},{8,10},{9,11},{10,... | collective-permute-start | bytes 393224 | tf_op jit(solution)/shard_map/ppermute | solution.py:437
  33.2 0.0 collective-permute-done.5.up
  33.2 0.5 %back_kernel.3.after = bf16[4,64,512]{2,1,0:T(8,128)(2,1)S(1)} custom-call(bf16[2,8,64,256]{3,2,1,0:T(8,128)(2,1)S(1)} %whiten_block.6.mine_q, bf16[2,8,64,256]{3,2,1,0:T(8,128)(2,1)S(1)} %get-tuple-element.22.got_q, bf16[2,8,64,256]{3,2,1,0:T(8,128)(2,1)S(1)} %collective-permute-done.5.up, bf16[2,8,64,256]{3,2,1,0:T(8,128)(2,1)S(1)} %whiten_block.7.rest_0_.side0.side, ...), custom_call_target="tpu_custom_call" | custom-call | flops 1000 | bytes 1000 | tf_op jit(solution)/shard_map/back_kernel/pallas_call | solution.py:241
  33.7 1.3 %collective-permute-start.9 = (bf16[4,64,512]{2,1,0:T(8,128)(2,1)S(1)}, bf16[4,64,512]{2,1,0:T(8,128)(2,1)S(1)}, u32[]{:S(2)}, u32[]{:S(2)}) collective-permute-start(bf16[4,64,512]{2,1,0:T(8,128)(2,1)S(1)} %back_kernel.3.after), channel_id=1, source_target_pairs={{4,1},{5,0},{6,3},{7,2},{8,5},{9,4},{10,7},{11,6},{12,9},{13,8},{1... | collective-permute-start | bytes 786440 | tf_op jit(solution)/shard_map/ppermute | solution.py:438
  35.0 0.5 %near_kernel.3.after = bf16[2,64,512]{2,1,0:T(8,128)(2,1)S(1)} custom-call(bf16[2,8,64,256]{3,2,1,0:T(8,128)(2,1)S(1)} %whiten_block.6.mine_q, bf16[2,8,64,256]{3,2,1,0:T(8,128)(2,1)S(1)} %get-tuple-element.22.got_q, bf16[2,8,64,256]{3,2,1,0:T(8,128)(2,1)S(1)} %whiten_block.8.rest_0_.down0, bf16[2,8,64,256]{3,2,1,0:T(8,128)(2,1)S(1)} %collective-permute-done.3.down1, ...), custom_call_target="tpu_custom_call" | custom-call | flops 1000 | bytes 1000 | tf_op jit(solution)/shard_map/near_kernel/pallas_call | solution.py:241
  35.6 0.0 copy-start
  35.6 0.0 copy-start.1
  35.6 0.0 copy-start.2
  35.6 0.5 %collective-permute-start.8 = (bf16[2,64,512]{2,1,0:T(8,128)(2,1)S(1)}, bf16[2,64,512]{2,1,0:T(8,128)(2,1)S(1)}, u32[]{:S(2)}, u32[]{:S(2)}) collective-permute-start(bf16[2,64,512]{2,1,0:T(8,128)(2,1)S(1)} %near_kernel.3.after), channel_id=1, source_target_pairs={{0,3},{1,2},{2,1},{3,0},{4,7},{5,6},{6,5},{7,4},{8,11},{9,10},{10,... | collective-permute-start | bytes 393224 | tf_op jit(solution)/shard_map/ppermute | solution.py:439
  36.1 1.6 %own_kernel.1 = (bf16[6,64,512]{2,1,0:T(8,128)(2,1)S(1)}, bf16[6,64,512]{2,1,0:T(8,128)(2,1)S(1)}) custom-call(bf16[2,8,64,256]{3,2,1,0:T(8,128)(2,1)S(1)} %whiten_block.5.mine_p, bf16[2,8,64,256]{3,2,1,0:T(8,128)(2,1)S(1)} %get-tuple-element.19.got_p, bf16[2,8,64,256]{3,2,1,0:T(8,128)(2,1)S(1)} %whiten_block.8.rest_0_.down0, ...), custom_call_target="tpu_custom_call" | custom-call | flops 1000 | bytes 1000 | tf_op jit(solution)/shard_map/own_kernel/pallas_call | solution.py:241
  37.7 1.5 %collective-permute-start.7 = (bf16[6,64,512]{2,1,0:T(8,128)(2,1)S(1)}, bf16[6,64,512]{2,1,0:T(8,128)(2,1)S(1)}, u32[]{:S(2)}, u32[]{:S(2)}) collective-permute-start(bf16[6,64,512]{2,1,0:T(8,128)(2,1)S(1)} %get-tuple-element.24), channel_id=1, source_target_pairs={{0,1},{1,0},{2,3},{3,2},{4,5},{5,4},{6,7},{7,6},{8,9},{9,8},{10,11... | collective-permute-start | bytes 1179656 | tf_op jit(solution)/shard_map/ppermute | solution.py:440
  39.2 0.0 collective-permute-done.10.refs_3_
  39.2 0.2 collective-permute-done.11.refs_4_
  39.4 0.0 copy-done
  39.4 0.0 copy-done.1
  39.4 0.0 copy-done.2
  39.4 1.0 %lags.2.straight = bf16[4,128,512]{2,1,0:T(8,128)(2,1)S(1)} custom-call(s32[1,4]{1,0:T(1,128)S(1)} %copy-done.1, s32[1,4]{1,0:T(1,128)S(1)} %copy-done.2, bf16[6,64,512]{2,1,0:T(8,128)(2,1)S(1)} %get-tuple-element.25.refs_2_, bf16[2,64,512]{2,1,0:T(8,128)(2,1)S(1)} %collective-permute-done.10.refs_3_, ...), custom_call_target="tpu_custom_call" | custom-call | flops 10000000000 | bytes 40000000 | tf_op jit(solution)/shard_map/lags/pallas_call | solution.py:313
  40.5 0.7 %collective-permute-done.8.refs_3_.side = bf16[2,64,512]{2,1,0:T(8,128)(2,1)S(1)} collective-permute-done((bf16[2,64,512]{2,1,0:T(8,128)(2,1)S(1)}, bf16[2,64,512]{2,1,0:T(8,128)(2,1)S(1)}, u32[]{:S(2)}, u32[]{:S(2)}) %collective-permute-start.8) | collective-permute-done | bytes 131104 | tf_op jit(solution)/shard_map/ppermute | solution.py:439
  41.2 0.0 collective-permute-done.7.refs_2_.own
  41.2 0.9 %lags.3 = (bf16[4,64,512]{2,1,0:T(8,128)(2,1)S(1)}, bf16[256,384]{1,0:T(8,128)(2,1)S(1)}, f32[4,512]{1,0:T(4,128)S(1)}) custom-call(s32[1,4]{1,0:T(1,128)S(1)} %copy-done.1, s32[1,4]{1,0:T(1,128)S(1)} %copy-done.2, bf16[6,64,512]{2,1,0:T(8,128)(2,1)S(1)} %collective-permute-done.7.refs_2_.own, bf16[2,64,512]{2,1,0:T(8,128)(2,1)S(1)} %collective-permute-done.8.refs_3_.side, ...), custom_call_target="tpu_custom_call" | custom-call | flops 10000000000 | bytes 40000000 | tf_op jit(solution)/shard_map/lags/pallas_call | solution.py:313
  42.1 1.8 %collective-permute-done.9.back = bf16[4,64,512]{2,1,0:T(8,128)(2,1)S(1)} collective-permute-done((bf16[4,64,512]{2,1,0:T(8,128)(2,1)S(1)}, bf16[4,64,512]{2,1,0:T(8,128)(2,1)S(1)}, u32[]{:S(2)}, u32[]{:S(2)}) %collective-permute-start.9) | collective-permute-done | bytes 262176 | tf_op jit(solution)/shard_map/ppermute | solution.py:438
  43.9 1.3 %last.1 = bf16[1,4,256,512]{3,2,1,0:T(8,128)(2,1)} custom-call(bf16[6,64,512]{2,1,0:T(8,128)(2,1)S(1)} %collective-permute-done.7.refs_2_.own, bf16[2,64,512]{2,1,0:T(8,128)(2,1)S(1)} %collective-permute-done.8.refs_3_.side, bf16[4,64,512]{2,1,0:T(8,128)(2,1)S(1)} %collective-permute-done.9.back, bf16[512,512]{1,0:T(8,128)(2,1)S(1)} %copy-done, ...), custom_call_target="tpu_custom_call" | custom-call | flops 1000 | bytes 1000 | tf_op jit(solution)/shard_map/last/pallas_call | solution.py:371
Async XLA Ops:
  1.8 9.0 %collective-permute-start = (bf16[2,2,8,64,256]{4,3,2,1,0:T(8,128)(2,1)S(1)}, bf16[2,2,8,64,256]{4,3,2,1,0:T(8,128)(2,1)S(1)}, u32[]{:S(2)}, u32[]{:S(2)}) collective-permute-start(bf16[2,2,8,64,256]{4,3,2,1,0:T(8,128)(2,1)S(1)} %get-tuple-element.18), channel_id=1, source_target_pairs={{0,1},{1,0},{2,3},{3,2},{4,5},{5,4},{6,7},{7,6},{8,9},{9,8},{10,11... | collective-permute-start | bytes 3145736 | tf_op jit(solution)/shard_map/ppermute | solution.py:414
  2.2 15.4 %collective-permute-start.2 = (bf16[2,8,64,256]{3,2,1,0:T(8,128)(2,1)S(1)}, bf16[2,8,64,256]{3,2,1,0:T(8,128)(2,1)S(1)}, u32[]{:S(2)}, u32[]{:S(2)}) collective-permute-start(bf16[2,8,64,256]{3,2,1,0:T(8,128)(2,1)S(1)} %get-tuple-element.20), channel_id=1, source_target_pairs={{0,2},{1,3},{2,0},{3,1},{4,6},{5,7},{6,4},{7,5},{8,10},{9,11},{10,... | collective-permute-start | bytes 1572872 | tf_op jit(solution)/shard_map/ppermute | solution.py:416
  4.9 19.9 %collective-permute-start.1 = (bf16[2,8,64,256]{3,2,1,0:T(8,128)(2,1)S(1)}, bf16[2,8,64,256]{3,2,1,0:T(8,128)(2,1)S(1)}, u32[]{:S(2)}, u32[]{:S(2)}) collective-permute-start(bf16[2,8,64,256]{3,2,1,0:T(8,128)(2,1)S(1)} %get-tuple-element.17.source), channel_id=1, source_target_pairs={{4,0},{5,1},{6,2},{7,3},{8,4},{9,5},{10,6},{11,7},{12,8},{13,9},{1... | collective-permute-start | bytes 1572872 | tf_op jit(solution)/shard_map/ppermute | solution.py:415
  6.1 19.4 %collective-permute-start.6 = (bf16[2,8,64,256]{3,2,1,0:T(8,128)(2,1)S(1)}, bf16[2,8,64,256]{3,2,1,0:T(8,128)(2,1)S(1)}, u32[]{:S(2)}, u32[]{:S(2)}) collective-permute-start(bf16[2,8,64,256]{3,2,1,0:T(8,128)(2,1)S(1)} %get-tuple-element.21.source), channel_id=1, source_target_pairs={{0,4},{1,5},{2,6},{3,7},{4,8},{5,9},{6,10},{7,11},{8,12},{9,13},{1... | collective-permute-start | bytes 1572872 | tf_op jit(solution)/shard_map/ppermute | solution.py:417
  12.4 16.2 %collective-permute-start.4 = (bf16[2,8,64,256]{3,2,1,0:T(8,128)(2,1)S(1)}, bf16[2,8,64,256]{3,2,1,0:T(8,128)(2,1)S(1)}, u32[]{:S(2)}, u32[]{:S(2)}) collective-permute-start(bf16[2,8,64,256]{3,2,1,0:T(8,128)(2,1)S(1)} %get-tuple-element.23), channel_id=1, source_target_pairs={{0,2},{1,3},{2,0},{3,1},{4,6},{5,7},{6,4},{7,5},{8,10},{9,11},{10,... | collective-permute-start | bytes 1572872 | tf_op jit(solution)/shard_map/ppermute | solution.py:420
  12.6 19.4 %collective-permute-start.3 = (bf16[2,8,64,256]{3,2,1,0:T(8,128)(2,1)S(1)}, bf16[2,8,64,256]{3,2,1,0:T(8,128)(2,1)S(1)}, u32[]{:S(2)}, u32[]{:S(2)}) collective-permute-start(bf16[2,8,64,256]{3,2,1,0:T(8,128)(2,1)S(1)} %get-tuple-element.19.got_p), channel_id=1, source_target_pairs={{4,0},{5,1},{6,2},{7,3},{8,4},{9,5},{10,6},{11,7},{12,8},{13,9},{1... | collective-permute-start | bytes 1572872 | tf_op jit(solution)/shard_map/ppermute | solution.py:419
  17.6 15.6 %collective-permute-start.5 = (bf16[2,8,64,256]{3,2,1,0:T(8,128)(2,1)S(1)}, bf16[2,8,64,256]{3,2,1,0:T(8,128)(2,1)S(1)}, u32[]{:S(2)}, u32[]{:S(2)}) collective-permute-start(bf16[2,8,64,256]{3,2,1,0:T(8,128)(2,1)S(1)} %get-tuple-element.22.got_q), channel_id=1, source_target_pairs={{0,4},{1,5},{2,6},{3,7},{4,8},{5,9},{6,10},{7,11},{8,12},{9,13},{1... | collective-permute-start | bytes 1572872 | tf_op jit(solution)/shard_map/ppermute | solution.py:421
  29.1 10.3 %collective-permute-start.11 = (bf16[4,64,512]{2,1,0:T(8,128)(2,1)S(1)}, bf16[4,64,512]{2,1,0:T(8,128)(2,1)S(1)}, u32[]{:S(2)}, u32[]{:S(2)}) collective-permute-start(bf16[4,64,512]{2,1,0:T(8,128)(2,1)S(1)} %back_kernel.2.after), channel_id=1, source_target_pairs={{4,0},{5,1},{6,2},{7,3},{8,4},{9,5},{10,6},{11,7},{12,8},{13,9},{1... | collective-permute-start | bytes 786440 | tf_op jit(solution)/shard_map/ppermute | solution.py:436
  32.5 6.8 %collective-permute-start.10 = (bf16[2,64,512]{2,1,0:T(8,128)(2,1)S(1)}, bf16[2,64,512]{2,1,0:T(8,128)(2,1)S(1)}, u32[]{:S(2)}, u32[]{:S(2)}) collective-permute-start(bf16[2,64,512]{2,1,0:T(8,128)(2,1)S(1)} %near_kernel.2.after), channel_id=1, source_target_pairs={{0,2},{1,3},{2,0},{3,1},{4,6},{5,7},{6,4},{7,5},{8,10},{9,11},{10,... | collective-permute-start | bytes 393224 | tf_op jit(solution)/shard_map/ppermute | solution.py:437
  33.7 10.1 %collective-permute-start.9 = (bf16[4,64,512]{2,1,0:T(8,128)(2,1)S(1)}, bf16[4,64,512]{2,1,0:T(8,128)(2,1)S(1)}, u32[]{:S(2)}, u32[]{:S(2)}) collective-permute-start(bf16[4,64,512]{2,1,0:T(8,128)(2,1)S(1)} %back_kernel.3.after), channel_id=1, source_target_pairs={{4,1},{5,0},{6,3},{7,2},{8,5},{9,4},{10,7},{11,6},{12,9},{13,8},{1... | collective-permute-start | bytes 786440 | tf_op jit(solution)/shard_map/ppermute | solution.py:438
  35.6 3.9 %copy-start = (bf16[512,512]{1,0:T(8,128)(2,1)S(1)}, bf16[512,512]{1,0:T(8,128)(2,1)}, u32[]{:S(2)}) copy-start(bf16[512,512]{1,0:T(8,128)(2,1)} %constant.2.clone.refs_5_.refs_4_.table) | copy-start | bytes 1572868
  35.6 3.9 %copy-start.1 = (s32[1,4]{1,0:T(1,128)S(1)}, s32[1,4]{1,0:T(1,128)}, u32[]{:S(2)}) copy-start(s32[1,4]{1,0:T(1,128)} %refs_0_.3) | copy-start | bytes 52
  35.6 3.9 %copy-start.2 = (s32[1,4]{1,0:T(1,128)S(1)}, s32[1,4]{1,0:T(1,128)}, u32[]{:S(2)}) copy-start(s32[1,4]{1,0:T(1,128)} %refs_1_.3) | copy-start | bytes 52
  35.6 5.6 %collective-permute-start.8 = (bf16[2,64,512]{2,1,0:T(8,128)(2,1)S(1)}, bf16[2,64,512]{2,1,0:T(8,128)(2,1)S(1)}, u32[]{:S(2)}, u32[]{:S(2)}) collective-permute-start(bf16[2,64,512]{2,1,0:T(8,128)(2,1)S(1)} %near_kernel.3.after), channel_id=1, source_target_pairs={{0,3},{1,2},{2,1},{3,0},{4,7},{5,6},{6,5},{7,4},{8,11},{9,10},{10,... | collective-permute-start | bytes 393224 | tf_op jit(solution)/shard_map/ppermute | solution.py:439
  37.7 3.5 %collective-permute-start.7 = (bf16[6,64,512]{2,1,0:T(8,128)(2,1)S(1)}, bf16[6,64,512]{2,1,0:T(8,128)(2,1)S(1)}, u32[]{:S(2)}, u32[]{:S(2)}) collective-permute-start(bf16[6,64,512]{2,1,0:T(8,128)(2,1)S(1)} %get-tuple-element.24), channel_id=1, source_target_pairs={{0,1},{1,0},{2,3},{3,2},{4,5},{5,4},{6,7},{7,6},{8,9},{9,8},{10,11... | collective-permute-start | bytes 1179656 | tf_op jit(solution)/shard_map/ppermute | solution.py:440

commit v7 on v6

--- a/solution.py
+++ b/solution.py
@@ -194,6 +194,44 @@
             run([reader(own[1])], [reader(own[0])], [both])
 
 
+def early_kernel(mine_q, got_q, up0, side0, down0, after, far, near):
+    windows, rows, bins = mine_q.shape[1:]
+    core, x = place()
+    run = functools.partial(products, rows=rows, bins=bins, windows=windows)
+    own_q = [reader(mine_q), reader(got_q)]
+    run([reader(up0)], own_q, [spots(core, far, 0)])
+
+    @pl.when(x == 0)
+    def _():
+        run([reader(side0)], [reader(down0)], [spots(core, near, 0)[:1]])
+
+    @pl.when(x == 1)
+    def _():
+        run([reader(side0)], own_q, [spots(core, near, 0)])
+
+
+def back_straight_kernel(up, side0, side1, far, back):
+    windows, rows, bins = up.shape[1:]
+    core, x = place()
+    back[2:4] = far[...]
+
+    @pl.when(x == 1)
+    def _():
+        side = [reader(side0), reader(side1)]
+        products([reader(up)], side, [spots(core, back, 0)], rows, bins, windows)
+
+
+def near_straight_kernel(side, down1, early, after, near):
+    windows, rows, bins = side.shape[1:]
+    core, x = place()
+    near[...] = early[...]
+
+    @pl.when(x == 0)
+    def _():
+        stores = [spots(core, near, 0)[1:]]
+        products([reader(side)], [reader(down1)], stores, rows, bins, windows)
+
+
 def back_kernel(mine_q, got_q, up, side0, side1, after, back):
     windows, rows, bins = mine_q.shape[1:]
     core, x = place()
@@ -426,8 +464,9 @@
     down0 = whiten_block(down0, after=side0)
     up0 = whiten_block(up0, after=down0)
 
-    (zs,) = cross(back_kernel, (4,), mine_q, got_q, up0, side0, side1, after=up0)
-    (xs,) = cross(near_kernel, (2,), mine_q, got_q, down0, down1, side0, after=zs)
+    far, near = cross(early_kernel, (2, 2), mine_q, got_q, up0, side0, down0, after=up0)
+    (zs,) = cross(back_straight_kernel, (4,), up0, side0, side1, far)
+    (xs,) = cross(near_straight_kernel, (2,), side0, down1, near, after=zs)
     (zd,) = cross(back_kernel, (4,), mine_q, got_q, up1, side0, side1, after=xs)
     (xd,) = cross(near_kernel, (2,), mine_q, got_q, down0, down1, side1, after=zd)
     own_here, own_chip = cross(

time: 45.6 us -> 45.3 us (level)
  starting transfers between devices: 19.7 us -> 19 us
    ppermute x1, waiting for transfers between devices: 2.19 us -> 1.32 us  [local(): side1 = move['xs'](got_side)]
    ppermute x1, waiting for transfers between devices: 0.01 us -> 0.73 us  [local(): up1 = move['up'](got_q)]
    ppermute x1, starting transfers between devices: 0.78 us -> 0.09 us  [local(): xs = move['xs'](xs)]
    ppermute x1, waiting for transfers between devices: 1.77 us -> 1.25 us  [local(): zd = move['crossed'](zd)]
    ppermute x1, waiting for transfers between devices: 1.56 us -> 2.04 us  [local(): down1 = move['down'](got_p)]
    pallas_call x6 -> x7, Pallas kernels: 4.3 us -> 4.55 us  [cross(): pl.pallas_call(kernel, out_shape=[jax.ShapeDtypeStruct((n, rows, 2 * bins...]
  transfers between devices with their start and end apart: 12 -> 12, of which waited for: 6 -> 6; matrix products, arithmetic and copies ran while one was open for 0% -> 0% of each run, Pallas kernels for 26% -> 27%
where the time goes in v7:
time: 45.3 us; the launch traced here: 44.5 us
  starting transfers between devices  19 us (42%)
  Pallas kernels  15.2 us (34%)
  waiting for transfers between devices  9.99 us (22%)
    ppermute x1, starting transfers between devices, local(): up0 = move['up'](up_raw)  4.58 us
    pallas_call x7, Pallas kernels, cross(): pl.pallas_call(kernel, out_shape=[jax.ShapeDtypeStruct((n, rows, 2 * bins...  4.55 us
    pallas_call x5, Pallas kernels, whiten_block(): pl.pallas_call(whiten_block_kernel, out_shape=jax.ShapeDtypeStruct(block....  4.06 us
    ppermute x1, starting transfers between devices, local(): up1 = move['up'](got_q)  3.95 us
    ppermute x1, waiting for transfers between devices, local(): side0 = move['xs'](side_raw)  3.78 us
    ppermute x1, starting transfers between devices, local(): side0 = move['xs'](side_raw)  2.61 us
    ppermute x1, waiting for transfers between devices, local(): down1 = move['down'](got_p)  2.04 us
    pallas_call x2, Pallas kernels, lag_part(): pl.pallas_call(kernel, out_shape=out_shape, in_specs=[smem] * 2 + [vmem]...  1.94 us
  transfers between devices with their start and end apart: 12, of which 6 were waited for; matrix products, arithmetic and copies ran while one was open for 0% of the time, Pallas kernels for 27%

profile of v7, /device:TPU:0, one launch (start us, length us, event | category | flops | bytes accessed | tf_op | source)
XLA Modules:
  0.0 44.5 jit_solution(11544553030112983708)
XLA Ops:
  0.0 1.8 %quarters.1 = (bf16[2,2,8,64,256]{4,3,2,1,0:T(8,128)(2,1)S(1)}, bf16[2,8,64,256]{3,2,1,0:T(8,128)(2,1)S(1)}, bf16[2,8,64,256]{3,2,1,0:T(8,128)(2,1)S(1)}, bf16[2,8,64,256]{3,2,1,0:T(8,128)(2,1)S(1)}) custom-call(bf16[1,2,8,256,256]{4,3,2,1,0:T(8,128)(2,1)} %spectra.1), custom_call_target="tpu_custom_call" | custom-call | flops 1000 | bytes 1000 | tf_op jit(solution)/shard_map/quarters/pallas_call | solution.py:65
  1.8 0.5 %collective-permute-start = (bf16[2,2,8,64,256]{4,3,2,1,0:T(8,128)(2,1)S(1)}, bf16[2,2,8,64,256]{4,3,2,1,0:T(8,128)(2,1)S(1)}, u32[]{:S(2)}, u32[]{:S(2)}) collective-permute-start(bf16[2,2,8,64,256]{4,3,2,1,0:T(8,128)(2,1)S(1)} %get-tuple-element.20), channel_id=1, source_target_pairs={{0,1},{1,0},{2,3},{3,2},{4,5},{5,4},{6,7},{7,6},{8,9},{9,8},{10,11... | collective-permute-start | bytes 3145736 | tf_op jit(solution)/shard_map/ppermute | solution.py:452
  2.2 2.6 %collective-permute-start.2 = (bf16[2,8,64,256]{3,2,1,0:T(8,128)(2,1)S(1)}, bf16[2,8,64,256]{3,2,1,0:T(8,128)(2,1)S(1)}, u32[]{:S(2)}, u32[]{:S(2)}) collective-permute-start(bf16[2,8,64,256]{3,2,1,0:T(8,128)(2,1)S(1)} %get-tuple-element.22), channel_id=1, source_target_pairs={{0,2},{1,3},{2,0},{3,1},{4,6},{5,7},{6,4},{7,5},{8,10},{9,11},{10,... | collective-permute-start | bytes 1572872 | tf_op jit(solution)/shard_map/ppermute | solution.py:454
  4.9 1.3 %collective-permute-start.1 = (bf16[2,8,64,256]{3,2,1,0:T(8,128)(2,1)S(1)}, bf16[2,8,64,256]{3,2,1,0:T(8,128)(2,1)S(1)}, u32[]{:S(2)}, u32[]{:S(2)}) collective-permute-start(bf16[2,8,64,256]{3,2,1,0:T(8,128)(2,1)S(1)} %get-tuple-element.19.source), channel_id=1, source_target_pairs={{4,0},{5,1},{6,2},{7,3},{8,4},{9,5},{10,6},{11,7},{12,8},{13,9},{1... | collective-permute-start | bytes 1572872 | tf_op jit(solution)/shard_map/ppermute | solution.py:453
  6.1 4.6 %collective-permute-start.6 = (bf16[2,8,64,256]{3,2,1,0:T(8,128)(2,1)S(1)}, bf16[2,8,64,256]{3,2,1,0:T(8,128)(2,1)S(1)}, u32[]{:S(2)}, u32[]{:S(2)}) collective-permute-start(bf16[2,8,64,256]{3,2,1,0:T(8,128)(2,1)S(1)} %get-tuple-element.23.source), channel_id=1, source_target_pairs={{0,4},{1,5},{2,6},{3,7},{4,8},{5,9},{6,10},{7,11},{8,12},{9,13},{1... | collective-permute-start | bytes 1572872 | tf_op jit(solution)/shard_map/ppermute | solution.py:455
  10.7 0.0 collective-permute-done.got
  10.7 1.7 %whiten_got.1 = (bf16[2,8,64,256]{3,2,1,0:T(8,128)(2,1)S(1)}, bf16[2,8,64,256]{3,2,1,0:T(8,128)(2,1)S(1)}, bf16[2,8,64,256]{3,2,1,0:T(8,128)(2,1)S(1)}) custom-call(bf16[2,2,8,64,256]{4,3,2,1,0:T(8,128)(2,1)S(1)} %collective-permute-done.got), custom_call_target="tpu_custom_call" | custom-call | flops 1000 | bytes 1000 | tf_op jit(solution)/shard_map/whiten_got/pallas_call | solution.py:102
  12.4 0.1 collective-permute-start.4
  12.6 1.3 %collective-permute-start.3 = (bf16[2,8,64,256]{3,2,1,0:T(8,128)(2,1)S(1)}, bf16[2,8,64,256]{3,2,1,0:T(8,128)(2,1)S(1)}, u32[]{:S(2)}, u32[]{:S(2)}) collective-permute-start(bf16[2,8,64,256]{3,2,1,0:T(8,128)(2,1)S(1)} %get-tuple-element.21.got_p), channel_id=1, source_target_pairs={{4,0},{5,1},{6,2},{7,3},{8,4},{9,5},{10,6},{11,7},{12,8},{13,9},{1... | collective-permute-start | bytes 1572872 | tf_op jit(solution)/shard_map/ppermute | solution.py:457
  13.9 3.8 %collective-permute-done.2.source = bf16[2,8,64,256]{3,2,1,0:T(8,128)(2,1)S(1)} collective-permute-done((bf16[2,8,64,256]{3,2,1,0:T(8,128)(2,1)S(1)}, bf16[2,8,64,256]{3,2,1,0:T(8,128)(2,1)S(1)}, u32[]{:S(2)}, u32[]{:S(2)}) %collective-permute-start.2) | collective-permute-done | bytes 524320 | tf_op jit(solution)/shard_map/ppermute | solution.py:454
  17.6 3.9 %collective-permute-start.5 = (bf16[2,8,64,256]{3,2,1,0:T(8,128)(2,1)S(1)}, bf16[2,8,64,256]{3,2,1,0:T(8,128)(2,1)S(1)}, u32[]{:S(2)}, u32[]{:S(2)}) collective-permute-start(bf16[2,8,64,256]{3,2,1,0:T(8,128)(2,1)S(1)} %get-tuple-element.24.got_q), channel_id=1, source_target_pairs={{0,4},{1,5},{2,6},{3,7},{4,8},{5,9},{6,10},{7,11},{8,12},{9,13},{1... | collective-permute-start | bytes 1572872 | tf_op jit(solution)/shard_map/ppermute | solution.py:459
  21.6 0.8 %whiten_block.6.mine_q = bf16[2,8,64,256]{3,2,1,0:T(8,128)(2,1)S(1)} custom-call(bf16[2,8,64,256]{3,2,1,0:T(8,128)(2,1)S(1)} %get-tuple-element.23.source), custom_call_target="tpu_custom_call" | custom-call | flops 1000 | bytes 1000 | tf_op jit(solution)/shard_map/whiten_block/pallas_call | solution.py:128
  22.4 0.8 %whiten_block.5.mine_p = bf16[2,8,64,256]{3,2,1,0:T(8,128)(2,1)S(1)} custom-call(bf16[2,8,64,256]{3,2,1,0:T(8,128)(2,1)S(1)} %get-tuple-element.19.source), custom_call_target="tpu_custom_call" | custom-call | flops 1000 | bytes 1000 | tf_op jit(solution)/shard_map/whiten_block/pallas_call | solution.py:128
  23.2 0.7 %chip_kernel.1.rest_0_.pair = bf16[2,64,512]{2,1,0:T(8,128)(2,1)S(1)} custom-call(bf16[2,8,64,256]{3,2,1,0:T(8,128)(2,1)S(1)} %whiten_block.5.mine_p, bf16[2,8,64,256]{3,2,1,0:T(8,128)(2,1)S(1)} %get-tuple-element.21.got_p, bf16[2,8,64,256]{3,2,1,0:T(8,128)(2,1)S(1)} %whiten_block.6.mine_q, bf16[2,8,64,256]{3,2,1,0:T(8,128)(2,1)S(1)} %get-tuple-element.24.got_q), custom_call_target="tpu_custom_call" | custom-call | flops 1000 | bytes 1000 | tf_op jit(solution)/shard_map/chip_kernel/pallas_call | solution.py:279
  23.9 0.8 %whiten_block.7.rest_0_.side0.side = bf16[2,8,64,256]{3,2,1,0:T(8,128)(2,1)S(1)} custom-call(bf16[2,8,64,256]{3,2,1,0:T(8,128)(2,1)S(1)} %collective-permute-done.2.source, bf16[2,64,512]{2,1,0:T(8,128)(2,1)S(1)} %chip_kernel.1.rest_0_.pair), custom_call_target="tpu_custom_call" | custom-call | flops 1000 | bytes 1000 | tf_op jit(solution)/shard_map/whiten_block/pallas_call | solution.py:128
  24.8 0.0 collective-permute-done.1.source
  24.8 0.8 %whiten_block.8.rest_0_.down0 = bf16[2,8,64,256]{3,2,1,0:T(8,128)(2,1)S(1)} custom-call(bf16[2,8,64,256]{3,2,1,0:T(8,128)(2,1)S(1)} %collective-permute-done.1.source, bf16[2,8,64,256]{3,2,1,0:T(8,128)(2,1)S(1)} %whiten_block.7.rest_0_.side0.side), custom_call_target="tpu_custom_call" | custom-call | flops 1000 | bytes 1000 | tf_op jit(solution)/shard_map/whiten_block/pallas_call | solution.py:128
  25.6 0.0 collective-permute-done.6.source
  25.6 0.8 %whiten_block.9.up0.after.up = bf16[2,8,64,256]{3,2,1,0:T(8,128)(2,1)S(1)} custom-call(bf16[2,8,64,256]{3,2,1,0:T(8,128)(2,1)S(1)} %collective-permute-done.6.source, bf16[2,8,64,256]{3,2,1,0:T(8,128)(2,1)S(1)} %whiten_block.8.rest_0_.down0), custom_call_target="tpu_custom_call" | custom-call | flops 1000 | bytes 1000 | tf_op jit(solution)/shard_map/whiten_block/pallas_call | solution.py:128
  26.4 0.9 %early_kernel.1 = (bf16[2,64,512]{2,1,0:T(8,128)(2,1)S(1)}, bf16[2,64,512]{2,1,0:T(8,128)(2,1)S(1)}) custom-call(bf16[2,8,64,256]{3,2,1,0:T(8,128)(2,1)S(1)} %whiten_block.6.mine_q, bf16[2,8,64,256]{3,2,1,0:T(8,128)(2,1)S(1)} %get-tuple-element.24.got_q, bf16[2,8,64,256]{3,2,1,0:T(8,128)(2,1)S(1)} %whiten_block.9.up0.after.up, ...), custom_call_target="tpu_custom_call" | custom-call | flops 1000 | bytes 1000 | tf_op jit(solution)/shard_map/early_kernel/pallas_call | solution.py:279
  27.3 1.3 %collective-permute-done.4.side1.side = bf16[2,8,64,256]{3,2,1,0:T(8,128)(2,1)S(1)} collective-permute-done((bf16[2,8,64,256]{3,2,1,0:T(8,128)(2,1)S(1)}, bf16[2,8,64,256]{3,2,1,0:T(8,128)(2,1)S(1)}, u32[]{:S(2)}, u32[]{:S(2)}) %collective-permute-start.4) | collective-permute-done | bytes 524320 | tf_op jit(solution)/shard_map/ppermute | solution.py:458
  28.6 1.3 %collective-permute-start.11 = (bf16[4,64,512]{2,1,0:T(8,128)(2,1)S(1)}, bf16[4,64,512]{2,1,0:T(8,128)(2,1)S(1)}, u32[]{:S(2)}, u32[]{:S(2)}) collective-permute-start(bf16[4,64,512]{2,1,0:T(8,128)(2,1)S(1)} %back_straight_kernel.1.after), channel_id=1, source_target_pairs={{4,0},{5,1},{6,2},{7,3},{8,4},{9,5},{10,6},{11,7},{12,8},{13,9},{1... | collective-permute-start | bytes 786440 | tf_op jit(solution)/shard_map/ppermute | solution.py:475
  29.9 2.0 %collective-permute-done.3.down1 = bf16[2,8,64,256]{3,2,1,0:T(8,128)(2,1)S(1)} collective-permute-done((bf16[2,8,64,256]{3,2,1,0:T(8,128)(2,1)S(1)}, bf16[2,8,64,256]{3,2,1,0:T(8,128)(2,1)S(1)}, u32[]{:S(2)}, u32[]{:S(2)}) %collective-permute-start.3) | collective-permute-done | bytes 524320 | tf_op jit(solution)/shard_map/ppermute | solution.py:457
  32.0 0.4 near_straight_kernel.1.after
  32.3 0.1 collective-permute-start.10
  32.4 0.7 %collective-permute-done.5.up = bf16[2,8,64,256]{3,2,1,0:T(8,128)(2,1)S(1)} collective-permute-done((bf16[2,8,64,256]{3,2,1,0:T(8,128)(2,1)S(1)}, bf16[2,8,64,256]{3,2,1,0:T(8,128)(2,1)S(1)}, u32[]{:S(2)}, u32[]{:S(2)}) %collective-permute-start.5) | collective-permute-done | bytes 524320 | tf_op jit(solution)/shard_map/ppermute | solution.py:459
  33.1 0.5 %back_kernel.1.after = bf16[4,64,512]{2,1,0:T(8,128)(2,1)S(1)} custom-call(bf16[2,8,64,256]{3,2,1,0:T(8,128)(2,1)S(1)} %whiten_block.6.mine_q, bf16[2,8,64,256]{3,2,1,0:T(8,128)(2,1)S(1)} %get-tuple-element.24.got_q, bf16[2,8,64,256]{3,2,1,0:T(8,128)(2,1)S(1)} %collective-permute-done.5.up, bf16[2,8,64,256]{3,2,1,0:T(8,128)(2,1)S(1)} %whiten_block.7.rest_0_.side0.side, ...), custom_call_target="tpu_custom_call" | custom-call | flops 1000 | bytes 1000 | tf_op jit(solution)/shard_map/back_kernel/pallas_call | solution.py:279
  33.6 1.3 %collective-permute-start.9 = (bf16[4,64,512]{2,1,0:T(8,128)(2,1)S(1)}, bf16[4,64,512]{2,1,0:T(8,128)(2,1)S(1)}, u32[]{:S(2)}, u32[]{:S(2)}) collective-permute-start(bf16[4,64,512]{2,1,0:T(8,128)(2,1)S(1)} %back_kernel.1.after), channel_id=1, source_target_pairs={{4,1},{5,0},{6,3},{7,2},{8,5},{9,4},{10,7},{11,6},{12,9},{13,8},{1... | collective-permute-start | bytes 786440 | tf_op jit(solution)/shard_map/ppermute | solution.py:477
  34.9 0.5 %near_kernel.1.after = bf16[2,64,512]{2,1,0:T(8,128)(2,1)S(1)} custom-call(bf16[2,8,64,256]{3,2,1,0:T(8,128)(2,1)S(1)} %whiten_block.6.mine_q, bf16[2,8,64,256]{3,2,1,0:T(8,128)(2,1)S(1)} %get-tuple-element.24.got_q, bf16[2,8,64,256]{3,2,1,0:T(8,128)(2,1)S(1)} %whiten_block.8.rest_0_.down0, bf16[2,8,64,256]{3,2,1,0:T(8,128)(2,1)S(1)} %collective-permute-done.3.down1, ...), custom_call_target="tpu_custom_call" | custom-call | flops 1000 | bytes 1000 | tf_op jit(solution)/shard_map/near_kernel/pallas_call | solution.py:279
  35.5 0.0 copy-start
  35.5 0.0 copy-start.1
  35.5 0.0 copy-start.2
  35.5 0.5 %collective-permute-start.8 = (bf16[2,64,512]{2,1,0:T(8,128)(2,1)S(1)}, bf16[2,64,512]{2,1,0:T(8,128)(2,1)S(1)}, u32[]{:S(2)}, u32[]{:S(2)}) collective-permute-start(bf16[2,64,512]{2,1,0:T(8,128)(2,1)S(1)} %near_kernel.1.after), channel_id=1, source_target_pairs={{0,3},{1,2},{2,1},{3,0},{4,7},{5,6},{6,5},{7,4},{8,11},{9,10},{10,... | collective-permute-start | bytes 393224 | tf_op jit(solution)/shard_map/ppermute | solution.py:478
  36.0 1.6 %own_kernel.1 = (bf16[6,64,512]{2,1,0:T(8,128)(2,1)S(1)}, bf16[6,64,512]{2,1,0:T(8,128)(2,1)S(1)}) custom-call(bf16[2,8,64,256]{3,2,1,0:T(8,128)(2,1)S(1)} %whiten_block.5.mine_p, bf16[2,8,64,256]{3,2,1,0:T(8,128)(2,1)S(1)} %get-tuple-element.21.got_p, bf16[2,8,64,256]{3,2,1,0:T(8,128)(2,1)S(1)} %whiten_block.8.rest_0_.down0, ...), custom_call_target="tpu_custom_call" | custom-call | flops 1000 | bytes 1000 | tf_op jit(solution)/shard_map/own_kernel/pallas_call | solution.py:279
  37.6 1.5 %collective-permute-start.7 = (bf16[6,64,512]{2,1,0:T(8,128)(2,1)S(1)}, bf16[6,64,512]{2,1,0:T(8,128)(2,1)S(1)}, u32[]{:S(2)}, u32[]{:S(2)}) collective-permute-start(bf16[6,64,512]{2,1,0:T(8,128)(2,1)S(1)} %get-tuple-element.28), channel_id=1, source_target_pairs={{0,1},{1,0},{2,3},{3,2},{4,5},{5,4},{6,7},{7,6},{8,9},{9,8},{10,11... | collective-permute-start | bytes 1179656 | tf_op jit(solution)/shard_map/ppermute | solution.py:479
  39.1 0.0 collective-permute-done.10.refs_3_
  39.1 0.0 collective-permute-done.11.refs_4_
  39.1 0.0 copy-done
  39.1 0.0 copy-done.1
  39.1 0.0 copy-done.2
  39.1 1.0 %lags.2.straight = bf16[4,128,512]{2,1,0:T(8,128)(2,1)S(1)} custom-call(s32[1,4]{1,0:T(1,128)S(1)} %copy-done.1, s32[1,4]{1,0:T(1,128)S(1)} %copy-done.2, bf16[6,64,512]{2,1,0:T(8,128)(2,1)S(1)} %get-tuple-element.29.refs_2_, bf16[2,64,512]{2,1,0:T(8,128)(2,1)S(1)} %collective-permute-done.10.refs_3_, ...), custom_call_target="tpu_custom_call" | custom-call | flops 10000000000 | bytes 40000000 | tf_op jit(solution)/shard_map/lags/pallas_call | solution.py:351
  40.2 0.9 %collective-permute-done.8.refs_3_.side = bf16[2,64,512]{2,1,0:T(8,128)(2,1)S(1)} collective-permute-done((bf16[2,64,512]{2,1,0:T(8,128)(2,1)S(1)}, bf16[2,64,512]{2,1,0:T(8,128)(2,1)S(1)}, u32[]{:S(2)}, u32[]{:S(2)}) %collective-permute-start.8) | collective-permute-done | bytes 131104 | tf_op jit(solution)/shard_map/ppermute | solution.py:478
  41.0 0.0 collective-permute-done.7.refs_2_.own
  41.0 0.9 %lags.3 = (bf16[4,64,512]{2,1,0:T(8,128)(2,1)S(1)}, bf16[256,384]{1,0:T(8,128)(2,1)S(1)}, f32[4,512]{1,0:T(4,128)S(1)}) custom-call(s32[1,4]{1,0:T(1,128)S(1)} %copy-done.1, s32[1,4]{1,0:T(1,128)S(1)} %copy-done.2, bf16[6,64,512]{2,1,0:T(8,128)(2,1)S(1)} %collective-permute-done.7.refs_2_.own, bf16[2,64,512]{2,1,0:T(8,128)(2,1)S(1)} %collective-permute-done.8.refs_3_.side, ...), custom_call_target="tpu_custom_call" | custom-call | flops 10000000000 | bytes 40000000 | tf_op jit(solution)/shard_map/lags/pallas_call | solution.py:351
  42.0 1.3 %collective-permute-done.9.back = bf16[4,64,512]{2,1,0:T(8,128)(2,1)S(1)} collective-permute-done((bf16[4,64,512]{2,1,0:T(8,128)(2,1)S(1)}, bf16[4,64,512]{2,1,0:T(8,128)(2,1)S(1)}, u32[]{:S(2)}, u32[]{:S(2)}) %collective-permute-start.9) | collective-permute-done | bytes 262176 | tf_op jit(solution)/shard_map/ppermute | solution.py:477
  43.2 1.3 %last.1 = bf16[1,4,256,512]{3,2,1,0:T(8,128)(2,1)} custom-call(bf16[6,64,512]{2,1,0:T(8,128)(2,1)S(1)} %collective-permute-done.7.refs_2_.own, bf16[2,64,512]{2,1,0:T(8,128)(2,1)S(1)} %collective-permute-done.8.refs_3_.side, bf16[4,64,512]{2,1,0:T(8,128)(2,1)S(1)} %collective-permute-done.9.back, bf16[512,512]{1,0:T(8,128)(2,1)S(1)} %copy-done, ...), custom_call_target="tpu_custom_call" | custom-call | flops 1000 | bytes 1000 | tf_op jit(solution)/shard_map/last/pallas_call | solution.py:409
  (1 shorter events, 0.0 us)
Async XLA Ops:
  1.8 9.0 %collective-permute-start = (bf16[2,2,8,64,256]{4,3,2,1,0:T(8,128)(2,1)S(1)}, bf16[2,2,8,64,256]{4,3,2,1,0:T(8,128)(2,1)S(1)}, u32[]{:S(2)}, u32[]{:S(2)}) collective-permute-start(bf16[2,2,8,64,256]{4,3,2,1,0:T(8,128)(2,1)S(1)} %get-tuple-element.20), channel_id=1, source_target_pairs={{0,1},{1,0},{2,3},{3,2},{4,5},{5,4},{6,7},{7,6},{8,9},{9,8},{10,11... | collective-permute-start | bytes 3145736 | tf_op jit(solution)/shard_map/ppermute | solution.py:452
  2.2 15.4 %collective-permute-start.2 = (bf16[2,8,64,256]{3,2,1,0:T(8,128)(2,1)S(1)}, bf16[2,8,64,256]{3,2,1,0:T(8,128)(2,1)S(1)}, u32[]{:S(2)}, u32[]{:S(2)}) collective-permute-start(bf16[2,8,64,256]{3,2,1,0:T(8,128)(2,1)S(1)} %get-tuple-element.22), channel_id=1, source_target_pairs={{0,2},{1,3},{2,0},{3,1},{4,6},{5,7},{6,4},{7,5},{8,10},{9,11},{10,... | collective-permute-start | bytes 1572872 | tf_op jit(solution)/shard_map/ppermute | solution.py:454
  4.9 19.9 %collective-permute-start.1 = (bf16[2,8,64,256]{3,2,1,0:T(8,128)(2,1)S(1)}, bf16[2,8,64,256]{3,2,1,0:T(8,128)(2,1)S(1)}, u32[]{:S(2)}, u32[]{:S(2)}) collective-permute-start(bf16[2,8,64,256]{3,2,1,0:T(8,128)(2,1)S(1)} %get-tuple-element.19.source), channel_id=1, source_target_pairs={{4,0},{5,1},{6,2},{7,3},{8,4},{9,5},{10,6},{11,7},{12,8},{13,9},{1... | collective-permute-start | bytes 1572872 | tf_op jit(solution)/shard_map/ppermute | solution.py:453
  6.1 19.4 %collective-permute-start.6 = (bf16[2,8,64,256]{3,2,1,0:T(8,128)(2,1)S(1)}, bf16[2,8,64,256]{3,2,1,0:T(8,128)(2,1)S(1)}, u32[]{:S(2)}, u32[]{:S(2)}) collective-permute-start(bf16[2,8,64,256]{3,2,1,0:T(8,128)(2,1)S(1)} %get-tuple-element.23.source), channel_id=1, source_target_pairs={{0,4},{1,5},{2,6},{3,7},{4,8},{5,9},{6,10},{7,11},{8,12},{9,13},{1... | collective-permute-start | bytes 1572872 | tf_op jit(solution)/shard_map/ppermute | solution.py:455
  12.4 16.2 %collective-permute-start.4 = (bf16[2,8,64,256]{3,2,1,0:T(8,128)(2,1)S(1)}, bf16[2,8,64,256]{3,2,1,0:T(8,128)(2,1)S(1)}, u32[]{:S(2)}, u32[]{:S(2)}) collective-permute-start(bf16[2,8,64,256]{3,2,1,0:T(8,128)(2,1)S(1)} %get-tuple-element.25), channel_id=1, source_target_pairs={{0,2},{1,3},{2,0},{3,1},{4,6},{5,7},{6,4},{7,5},{8,10},{9,11},{10,... | collective-permute-start | bytes 1572872 | tf_op jit(solution)/shard_map/ppermute | solution.py:458
  12.6 19.4 %collective-permute-start.3 = (bf16[2,8,64,256]{3,2,1,0:T(8,128)(2,1)S(1)}, bf16[2,8,64,256]{3,2,1,0:T(8,128)(2,1)S(1)}, u32[]{:S(2)}, u32[]{:S(2)}) collective-permute-start(bf16[2,8,64,256]{3,2,1,0:T(8,128)(2,1)S(1)} %get-tuple-element.21.got_p), channel_id=1, source_target_pairs={{4,0},{5,1},{6,2},{7,3},{8,4},{9,5},{10,6},{11,7},{12,8},{13,9},{1... | collective-permute-start | bytes 1572872 | tf_op jit(solution)/shard_map/ppermute | solution.py:457
  17.6 15.5 %collective-permute-start.5 = (bf16[2,8,64,256]{3,2,1,0:T(8,128)(2,1)S(1)}, bf16[2,8,64,256]{3,2,1,0:T(8,128)(2,1)S(1)}, u32[]{:S(2)}, u32[]{:S(2)}) collective-permute-start(bf16[2,8,64,256]{3,2,1,0:T(8,128)(2,1)S(1)} %get-tuple-element.24.got_q), channel_id=1, source_target_pairs={{0,4},{1,5},{2,6},{3,7},{4,8},{5,9},{6,10},{7,11},{8,12},{9,13},{1... | collective-permute-start | bytes 1572872 | tf_op jit(solution)/shard_map/ppermute | solution.py:459
  28.6 10.5 %collective-permute-start.11 = (bf16[4,64,512]{2,1,0:T(8,128)(2,1)S(1)}, bf16[4,64,512]{2,1,0:T(8,128)(2,1)S(1)}, u32[]{:S(2)}, u32[]{:S(2)}) collective-permute-start(bf16[4,64,512]{2,1,0:T(8,128)(2,1)S(1)} %back_straight_kernel.1.after), channel_id=1, source_target_pairs={{4,0},{5,1},{6,2},{7,3},{8,4},{9,5},{10,6},{11,7},{12,8},{13,9},{1... | collective-permute-start | bytes 786440 | tf_op jit(solution)/shard_map/ppermute | solution.py:475
  32.3 6.8 %collective-permute-start.10 = (bf16[2,64,512]{2,1,0:T(8,128)(2,1)S(1)}, bf16[2,64,512]{2,1,0:T(8,128)(2,1)S(1)}, u32[]{:S(2)}, u32[]{:S(2)}) collective-permute-start(bf16[2,64,512]{2,1,0:T(8,128)(2,1)S(1)} %near_straight_kernel.1.after), channel_id=1, source_target_pairs={{0,2},{1,3},{2,0},{3,1},{4,6},{5,7},{6,4},{7,5},{8,10},{9,11},{10,... | collective-permute-start | bytes 393224 | tf_op jit(solution)/shard_map/ppermute | solution.py:476
  33.6 9.6 %collective-permute-start.9 = (bf16[4,64,512]{2,1,0:T(8,128)(2,1)S(1)}, bf16[4,64,512]{2,1,0:T(8,128)(2,1)S(1)}, u32[]{:S(2)}, u32[]{:S(2)}) collective-permute-start(bf16[4,64,512]{2,1,0:T(8,128)(2,1)S(1)} %back_kernel.1.after), channel_id=1, source_target_pairs={{4,1},{5,0},{6,3},{7,2},{8,5},{9,4},{10,7},{11,6},{12,9},{13,8},{1... | collective-permute-start | bytes 786440 | tf_op jit(solution)/shard_map/ppermute | solution.py:477
  35.5 3.7 %copy-start = (bf16[512,512]{1,0:T(8,128)(2,1)S(1)}, bf16[512,512]{1,0:T(8,128)(2,1)}, u32[]{:S(2)}) copy-start(bf16[512,512]{1,0:T(8,128)(2,1)} %constant.2.clone.refs_5_.refs_4_.table) | copy-start | bytes 1572868
  35.5 3.7 %copy-start.1 = (s32[1,4]{1,0:T(1,128)S(1)}, s32[1,4]{1,0:T(1,128)}, u32[]{:S(2)}) copy-start(s32[1,4]{1,0:T(1,128)} %refs_0_.3) | copy-start | bytes 52
  35.5 3.7 %copy-start.2 = (s32[1,4]{1,0:T(1,128)S(1)}, s32[1,4]{1,0:T(1,128)}, u32[]{:S(2)}) copy-start(s32[1,4]{1,0:T(1,128)} %refs_1_.3) | copy-start | bytes 52
  35.5 5.5 %collective-permute-start.8 = (bf16[2,64,512]{2,1,0:T(8,128)(2,1)S(1)}, bf16[2,64,512]{2,1,0:T(8,128)(2,1)S(1)}, u32[]{:S(2)}, u32[]{:S(2)}) collective-permute-start(bf16[2,64,512]{2,1,0:T(8,128)(2,1)S(1)} %near_kernel.1.after), channel_id=1, source_target_pairs={{0,3},{1,2},{2,1},{3,0},{4,7},{5,6},{6,5},{7,4},{8,11},{9,10},{10,... | collective-permute-start | bytes 393224 | tf_op jit(solution)/shard_map/ppermute | solution.py:478
  37.6 3.4 %collective-permute-start.7 = (bf16[6,64,512]{2,1,0:T(8,128)(2,1)S(1)}, bf16[6,64,512]{2,1,0:T(8,128)(2,1)S(1)}, u32[]{:S(2)}, u32[]{:S(2)}) collective-permute-start(bf16[6,64,512]{2,1,0:T(8,128)(2,1)S(1)} %get-tuple-element.28), channel_id=1, source_target_pairs={{0,1},{1,0},{2,3},{3,2},{4,5},{5,4},{6,7},{7,6},{8,9},{9,8},{10,11... | collective-permute-start | bytes 1179656 | tf_op jit(solution)/shard_map/ppermute | solution.py:479

commit v8 on v7

--- a/solution.py
+++ b/solution.py
@@ -13,7 +13,7 @@
 TILE = 16
 LANES = 128
 VMEM_LIMIT = 16 * 1024 * 1024
-VMEM_ALL = 50 * 1024 * 1024
+VMEM_ALL = 51 * 1024 * 1024
 WHITEN_TILE = 16
 
 SMALL = pl.CostEstimate(flops=1000, bytes_accessed=1000, transcendentals=0)
@@ -39,7 +39,7 @@
     return lax.rem(index, 2), lax.rem(lax.div(index, 2), 2)
 
 
-def quarters_kernel(spectra, theirs, side, up, down, sent):
+def quarters_kernel(spectra, side, up, down, sent):
     rows = side.shape[2]
     core, x = place()
     copies = []
@@ -47,8 +47,6 @@
         (0, core, down),
         (1, core, up),
         (1 - x, core, side),
-        (0, 1 - core, theirs.at[0]),
-        (1, 1 - core, theirs.at[1]),
     ):
         base = pl.multiple_of((2 * k + half) * rows, rows)
         source = spectra.at[0, :, :, pl.ds(base, rows), :]
@@ -64,11 +62,10 @@
     shape = (parts, windows, channels // 4, bins)
     return pl.pallas_call(
         quarters_kernel,
-        out_shape=[jax.ShapeDtypeStruct((2,) + shape, jnp.bfloat16)]
-        + [jax.ShapeDtypeStruct(shape, jnp.bfloat16)] * 3,
+        out_shape=[jax.ShapeDtypeStruct(shape, jnp.bfloat16)] * 3,
         in_specs=[pl.BlockSpec(memory_space=pl.ANY)],
-        out_specs=[pl.BlockSpec(memory_space=OUT_SPACE)] * 4,
-        scratch_shapes=[pltpu.SemaphoreType.DMA((5,))],
+        out_specs=[pl.BlockSpec(memory_space=OUT_SPACE)] * 3,
+        scratch_shapes=[pltpu.SemaphoreType.DMA((3,))],
         compiler_params=pltpu.CompilerParams(vmem_limit_bytes=VMEM_ALL),
         cost_estimate=SMALL,
         name="quarters",
@@ -76,12 +73,13 @@
 
 
 def whiten_got_kernel(got, p_out, q_out, side_out):
-    windows, rows = got.shape[2], got.shape[3]
-    _, x = place()
+    windows, rows = p_out.shape[1:3]
+    core, x = place()
     for k, target in ((0, p_out), (1, q_out)):
+        base = pl.multiple_of((2 * k + core) * rows, rows)
 
         def read(w, block):
-            return got[k, :, w, block, :]
+            return got[0, :, w, pl.ds(base + block.start, block.size), :]
 
         def write(w, block, values):
             target[:, w, block, :] = values
@@ -98,10 +96,12 @@
 
 
 def whiten_got(got):
+    parts, windows, channels, bins = got.shape[1:]
+    shape = (parts, windows, channels // 4, bins)
     vmem = pl.BlockSpec(memory_space=pltpu.VMEM)
     return pl.pallas_call(
         whiten_got_kernel,
-        out_shape=[jax.ShapeDtypeStruct(got.shape[1:], jnp.bfloat16)] * 3,
+        out_shape=[jax.ShapeDtypeStruct(shape, jnp.bfloat16)] * 3,
         in_specs=[vmem],
         out_specs=[vmem] * 3,
         compiler_params=pltpu.CompilerParams(vmem_limit_bytes=VMEM_LIMIT),
@@ -448,8 +448,8 @@
     move = {name: functools.partial(lax.ppermute, axis_name="pairs", perm=perm) for name, perm in moves(n).items()}
     table = jnp.asarray(phase_table(spectra.shape[4], 2 * spectra.shape[4]))
 
-    theirs, side_raw, up_raw, down_raw = quarters(spectra)
-    got = move["chip"](theirs)
+    got = move["chip"](spectra)
+    side_raw, up_raw, down_raw = quarters(spectra)
     down0 = move["down"](down_raw)
     side0 = move["xs"](side_raw)
     up0 = move["up"](up_raw)

time: 45.3 us -> 44.9 us (level)
  transfers between devices with their start and end apart: 12 -> 12, of which waited for: 6 -> 6; matrix products, arithmetic and copies ran while one was open for 0% -> 0% of each run, Pallas kernels for 27% -> 31%
where the time goes in v8:
time: 44.9 us; the launch traced here: 44.2 us
  starting transfers between devices  18.9 us (42%)
  Pallas kernels  14.9 us (33%)
  waiting for transfers between devices  10.2 us (23%)
    ppermute x1, starting transfers between devices, local(): up0 = move['up'](up_raw)  4.58 us
    pallas_call x7, Pallas kernels, cross(): pl.pallas_call(kernel, out_shape=[jax.ShapeDtypeStruct((n, rows, 2 * bins...  4.55 us
    pallas_call x5, Pallas kernels, whiten_block(): pl.pallas_call(whiten_block_kernel, out_shape=jax.ShapeDtypeStruct(block....  4.06 us
    ppermute x1, starting transfers between devices, local(): up1 = move['up'](got_q)  3.94 us
    ppermute x1, waiting for transfers between devices, local(): side0 = move['xs'](side_raw)  3.79 us
    ppermute x1, starting transfers between devices, local(): side0 = move['xs'](side_raw)  2.57 us
    ppermute x1, waiting for transfers between devices, local(): down1 = move['down'](got_p)  2.02 us
    pallas_call x2, Pallas kernels, lag_part(): pl.pallas_call(kernel, out_shape=out_shape, in_specs=[smem] * 2 + [vmem]...  1.94 us
  transfers between devices with their start and end apart: 12, of which 6 were waited for; matrix products, arithmetic and copies ran while one was open for 0% of the time, Pallas kernels for 31%

profile of v8, /device:TPU:0, one launch (start us, length us, event | category | flops | bytes accessed | tf_op | source)
XLA Modules:
  0.0 44.2 jit_solution(17452198026783762267)
XLA Ops:
  0.0 0.5 %collective-permute-start = (bf16[1,2,8,256,256]{4,3,2,1,0:T(8,128)(2,1)}, bf16[1,2,8,256,256]{4,3,2,1,0:T(8,128)(2,1)S(1)}, u32[]{:S(2)}, u32[]{:S(2)}) collective-permute-start(bf16[1,2,8,256,256]{4,3,2,1,0:T(8,128)(2,1)} %spectra.1), channel_id=1, source_target_pairs={{0,1},{1,0},{2,3},{3,2},{4,5},{5,4},{6,7},{7,6},{8,9},{9,8},{10,11... | collective-permute-start | bytes 6291464 | tf_op jit(solution)/shard_map/ppermute | solution.py:451
  0.5 1.4 %quarters.1 = (bf16[2,8,64,256]{3,2,1,0:T(8,128)(2,1)S(1)}, bf16[2,8,64,256]{3,2,1,0:T(8,128)(2,1)S(1)}, bf16[2,8,64,256]{3,2,1,0:T(8,128)(2,1)S(1)}) custom-call(bf16[1,2,8,256,256]{4,3,2,1,0:T(8,128)(2,1)} %spectra.1), custom_call_target="tpu_custom_call" | custom-call | flops 1000 | bytes 1000 | tf_op jit(solution)/shard_map/quarters/pallas_call | solution.py:63
  1.9 2.6 %collective-permute-start.2 = (bf16[2,8,64,256]{3,2,1,0:T(8,128)(2,1)S(1)}, bf16[2,8,64,256]{3,2,1,0:T(8,128)(2,1)S(1)}, u32[]{:S(2)}, u32[]{:S(2)}) collective-permute-start(bf16[2,8,64,256]{3,2,1,0:T(8,128)(2,1)S(1)} %get-tuple-element.20), channel_id=1, source_target_pairs={{0,2},{1,3},{2,0},{3,1},{4,6},{5,7},{6,4},{7,5},{8,10},{9,11},{10,... | collective-permute-start | bytes 1572872 | tf_op jit(solution)/shard_map/ppermute | solution.py:454
  4.4 1.3 %collective-permute-start.1 = (bf16[2,8,64,256]{3,2,1,0:T(8,128)(2,1)S(1)}, bf16[2,8,64,256]{3,2,1,0:T(8,128)(2,1)S(1)}, u32[]{:S(2)}, u32[]{:S(2)}) collective-permute-start(bf16[2,8,64,256]{3,2,1,0:T(8,128)(2,1)S(1)} %get-tuple-element.18.source), channel_id=1, source_target_pairs={{4,0},{5,1},{6,2},{7,3},{8,4},{9,5},{10,6},{11,7},{12,8},{13,9},{1... | collective-permute-start | bytes 1572872 | tf_op jit(solution)/shard_map/ppermute | solution.py:453
  5.7 4.6 %collective-permute-start.6 = (bf16[2,8,64,256]{3,2,1,0:T(8,128)(2,1)S(1)}, bf16[2,8,64,256]{3,2,1,0:T(8,128)(2,1)S(1)}, u32[]{:S(2)}, u32[]{:S(2)}) collective-permute-start(bf16[2,8,64,256]{3,2,1,0:T(8,128)(2,1)S(1)} %get-tuple-element.21.source), channel_id=1, source_target_pairs={{0,4},{1,5},{2,6},{3,7},{4,8},{5,9},{6,10},{7,11},{8,12},{9,13},{1... | collective-permute-start | bytes 1572872 | tf_op jit(solution)/shard_map/ppermute | solution.py:455
  10.3 0.0 collective-permute-done.got
  10.3 1.7 %whiten_got.1 = (bf16[2,8,64,256]{3,2,1,0:T(8,128)(2,1)S(1)}, bf16[2,8,64,256]{3,2,1,0:T(8,128)(2,1)S(1)}, bf16[2,8,64,256]{3,2,1,0:T(8,128)(2,1)S(1)}) custom-call(bf16[1,2,8,256,256]{4,3,2,1,0:T(8,128)(2,1)S(1)} %collective-permute-done.got), custom_call_target="tpu_custom_call" | custom-call | flops 1000 | bytes 1000 | tf_op jit(solution)/shard_map/whiten_got/pallas_call | solution.py:102
  12.0 0.1 collective-permute-start.4
  12.1 1.3 %collective-permute-start.3 = (bf16[2,8,64,256]{3,2,1,0:T(8,128)(2,1)S(1)}, bf16[2,8,64,256]{3,2,1,0:T(8,128)(2,1)S(1)}, u32[]{:S(2)}, u32[]{:S(2)}) collective-permute-start(bf16[2,8,64,256]{3,2,1,0:T(8,128)(2,1)S(1)} %get-tuple-element.19.got_p), channel_id=1, source_target_pairs={{4,0},{5,1},{6,2},{7,3},{8,4},{9,5},{10,6},{11,7},{12,8},{13,9},{1... | collective-permute-start | bytes 1572872 | tf_op jit(solution)/shard_map/ppermute | solution.py:457
  13.4 3.8 %collective-permute-done.2.source = bf16[2,8,64,256]{3,2,1,0:T(8,128)(2,1)S(1)} collective-permute-done((bf16[2,8,64,256]{3,2,1,0:T(8,128)(2,1)S(1)}, bf16[2,8,64,256]{3,2,1,0:T(8,128)(2,1)S(1)}, u32[]{:S(2)}, u32[]{:S(2)}) %collective-permute-start.2) | collective-permute-done | bytes 524320 | tf_op jit(solution)/shard_map/ppermute | solution.py:454
  17.2 3.9 %collective-permute-start.5 = (bf16[2,8,64,256]{3,2,1,0:T(8,128)(2,1)S(1)}, bf16[2,8,64,256]{3,2,1,0:T(8,128)(2,1)S(1)}, u32[]{:S(2)}, u32[]{:S(2)}) collective-permute-start(bf16[2,8,64,256]{3,2,1,0:T(8,128)(2,1)S(1)} %get-tuple-element.22.got_q), channel_id=1, source_target_pairs={{0,4},{1,5},{2,6},{3,7},{4,8},{5,9},{6,10},{7,11},{8,12},{9,13},{1... | collective-permute-start | bytes 1572872 | tf_op jit(solution)/shard_map/ppermute | solution.py:459
  21.1 0.8 %whiten_block.6.mine_q = bf16[2,8,64,256]{3,2,1,0:T(8,128)(2,1)S(1)} custom-call(bf16[2,8,64,256]{3,2,1,0:T(8,128)(2,1)S(1)} %get-tuple-element.21.source), custom_call_target="tpu_custom_call" | custom-call | flops 1000 | bytes 1000 | tf_op jit(solution)/shard_map/whiten_block/pallas_call | solution.py:128
  22.0 0.8 %whiten_block.5.mine_p = bf16[2,8,64,256]{3,2,1,0:T(8,128)(2,1)S(1)} custom-call(bf16[2,8,64,256]{3,2,1,0:T(8,128)(2,1)S(1)} %get-tuple-element.18.source), custom_call_target="tpu_custom_call" | custom-call | flops 1000 | bytes 1000 | tf_op jit(solution)/shard_map/whiten_block/pallas_call | solution.py:128
  22.8 0.7 %chip_kernel.1.rest_0_.pair = bf16[2,64,512]{2,1,0:T(8,128)(2,1)S(1)} custom-call(bf16[2,8,64,256]{3,2,1,0:T(8,128)(2,1)S(1)} %whiten_block.5.mine_p, bf16[2,8,64,256]{3,2,1,0:T(8,128)(2,1)S(1)} %get-tuple-element.19.got_p, bf16[2,8,64,256]{3,2,1,0:T(8,128)(2,1)S(1)} %whiten_block.6.mine_q, bf16[2,8,64,256]{3,2,1,0:T(8,128)(2,1)S(1)} %get-tuple-element.22.got_q), custom_call_target="tpu_custom_call" | custom-call | flops 1000 | bytes 1000 | tf_op jit(solution)/shard_map/chip_kernel/pallas_call | solution.py:279
  23.5 0.8 %whiten_block.7.rest_0_.side0.side = bf16[2,8,64,256]{3,2,1,0:T(8,128)(2,1)S(1)} custom-call(bf16[2,8,64,256]{3,2,1,0:T(8,128)(2,1)S(1)} %collective-permute-done.2.source, bf16[2,64,512]{2,1,0:T(8,128)(2,1)S(1)} %chip_kernel.1.rest_0_.pair), custom_call_target="tpu_custom_call" | custom-call | flops 1000 | bytes 1000 | tf_op jit(solution)/shard_map/whiten_block/pallas_call | solution.py:128
  24.3 0.0 collective-permute-done.1.source
  24.3 0.8 %whiten_block.8.rest_0_.down0 = bf16[2,8,64,256]{3,2,1,0:T(8,128)(2,1)S(1)} custom-call(bf16[2,8,64,256]{3,2,1,0:T(8,128)(2,1)S(1)} %collective-permute-done.1.source, bf16[2,8,64,256]{3,2,1,0:T(8,128)(2,1)S(1)} %whiten_block.7.rest_0_.side0.side), custom_call_target="tpu_custom_call" | custom-call | flops 1000 | bytes 1000 | tf_op jit(solution)/shard_map/whiten_block/pallas_call | solution.py:128
  25.2 0.0 collective-permute-done.6.source
  25.2 0.8 %whiten_block.9.up0.after.up = bf16[2,8,64,256]{3,2,1,0:T(8,128)(2,1)S(1)} custom-call(bf16[2,8,64,256]{3,2,1,0:T(8,128)(2,1)S(1)} %collective-permute-done.6.source, bf16[2,8,64,256]{3,2,1,0:T(8,128)(2,1)S(1)} %whiten_block.8.rest_0_.down0), custom_call_target="tpu_custom_call" | custom-call | flops 1000 | bytes 1000 | tf_op jit(solution)/shard_map/whiten_block/pallas_call | solution.py:128
  26.0 0.9 %early_kernel.1 = (bf16[2,64,512]{2,1,0:T(8,128)(2,1)S(1)}, bf16[2,64,512]{2,1,0:T(8,128)(2,1)S(1)}) custom-call(bf16[2,8,64,256]{3,2,1,0:T(8,128)(2,1)S(1)} %whiten_block.6.mine_q, bf16[2,8,64,256]{3,2,1,0:T(8,128)(2,1)S(1)} %get-tuple-element.22.got_q, bf16[2,8,64,256]{3,2,1,0:T(8,128)(2,1)S(1)} %whiten_block.9.up0.after.up, ...), custom_call_target="tpu_custom_call" | custom-call | flops 1000 | bytes 1000 | tf_op jit(solution)/shard_map/early_kernel/pallas_call | solution.py:279
  26.8 1.4 %collective-permute-done.4.side1.side = bf16[2,8,64,256]{3,2,1,0:T(8,128)(2,1)S(1)} collective-permute-done((bf16[2,8,64,256]{3,2,1,0:T(8,128)(2,1)S(1)}, bf16[2,8,64,256]{3,2,1,0:T(8,128)(2,1)S(1)}, u32[]{:S(2)}, u32[]{:S(2)}) %collective-permute-start.4) | collective-permute-done | bytes 524320 | tf_op jit(solution)/shard_map/ppermute | solution.py:458
  28.3 1.3 %collective-permute-start.11 = (bf16[4,64,512]{2,1,0:T(8,128)(2,1)S(1)}, bf16[4,64,512]{2,1,0:T(8,128)(2,1)S(1)}, u32[]{:S(2)}, u32[]{:S(2)}) collective-permute-start(bf16[4,64,512]{2,1,0:T(8,128)(2,1)S(1)} %back_straight_kernel.1.after), channel_id=1, source_target_pairs={{4,0},{5,1},{6,2},{7,3},{8,4},{9,5},{10,6},{11,7},{12,8},{13,9},{1... | collective-permute-start | bytes 786440 | tf_op jit(solution)/shard_map/ppermute | solution.py:475
  29.6 2.0 %collective-permute-done.3.down1 = bf16[2,8,64,256]{3,2,1,0:T(8,128)(2,1)S(1)} collective-permute-done((bf16[2,8,64,256]{3,2,1,0:T(8,128)(2,1)S(1)}, bf16[2,8,64,256]{3,2,1,0:T(8,128)(2,1)S(1)}, u32[]{:S(2)}, u32[]{:S(2)}) %collective-permute-start.3) | collective-permute-done | bytes 524320 | tf_op jit(solution)/shard_map/ppermute | solution.py:457
  31.6 0.4 near_straight_kernel.1.after
  31.9 0.1 collective-permute-start.10
  32.0 0.7 %collective-permute-done.5.up = bf16[2,8,64,256]{3,2,1,0:T(8,128)(2,1)S(1)} collective-permute-done((bf16[2,8,64,256]{3,2,1,0:T(8,128)(2,1)S(1)}, bf16[2,8,64,256]{3,2,1,0:T(8,128)(2,1)S(1)}, u32[]{:S(2)}, u32[]{:S(2)}) %collective-permute-start.5) | collective-permute-done | bytes 524320 | tf_op jit(solution)/shard_map/ppermute | solution.py:459
  32.8 0.5 %back_kernel.1.after = bf16[4,64,512]{2,1,0:T(8,128)(2,1)S(1)} custom-call(bf16[2,8,64,256]{3,2,1,0:T(8,128)(2,1)S(1)} %whiten_block.6.mine_q, bf16[2,8,64,256]{3,2,1,0:T(8,128)(2,1)S(1)} %get-tuple-element.22.got_q, bf16[2,8,64,256]{3,2,1,0:T(8,128)(2,1)S(1)} %collective-permute-done.5.up, bf16[2,8,64,256]{3,2,1,0:T(8,128)(2,1)S(1)} %whiten_block.7.rest_0_.side0.side, ...), custom_call_target="tpu_custom_call" | custom-call | flops 1000 | bytes 1000 | tf_op jit(solution)/shard_map/back_kernel/pallas_call | solution.py:279
  33.3 1.3 %collective-permute-start.9 = (bf16[4,64,512]{2,1,0:T(8,128)(2,1)S(1)}, bf16[4,64,512]{2,1,0:T(8,128)(2,1)S(1)}, u32[]{:S(2)}, u32[]{:S(2)}) collective-permute-start(bf16[4,64,512]{2,1,0:T(8,128)(2,1)S(1)} %back_kernel.1.after), channel_id=1, source_target_pairs={{4,1},{5,0},{6,3},{7,2},{8,5},{9,4},{10,7},{11,6},{12,9},{13,8},{1... | collective-permute-start | bytes 786440 | tf_op jit(solution)/shard_map/ppermute | solution.py:477
  34.6 0.5 %near_kernel.1.after = bf16[2,64,512]{2,1,0:T(8,128)(2,1)S(1)} custom-call(bf16[2,8,64,256]{3,2,1,0:T(8,128)(2,1)S(1)} %whiten_block.6.mine_q, bf16[2,8,64,256]{3,2,1,0:T(8,128)(2,1)S(1)} %get-tuple-element.22.got_q, bf16[2,8,64,256]{3,2,1,0:T(8,128)(2,1)S(1)} %whiten_block.8.rest_0_.down0, bf16[2,8,64,256]{3,2,1,0:T(8,128)(2,1)S(1)} %collective-permute-done.3.down1, ...), custom_call_target="tpu_custom_call" | custom-call | flops 1000 | bytes 1000 | tf_op jit(solution)/shard_map/near_kernel/pallas_call | solution.py:279
  35.1 0.0 copy-start
  35.1 0.0 copy-start.1
  35.1 0.0 copy-start.2
  35.1 0.5 %collective-permute-start.8 = (bf16[2,64,512]{2,1,0:T(8,128)(2,1)S(1)}, bf16[2,64,512]{2,1,0:T(8,128)(2,1)S(1)}, u32[]{:S(2)}, u32[]{:S(2)}) collective-permute-start(bf16[2,64,512]{2,1,0:T(8,128)(2,1)S(1)} %near_kernel.1.after), channel_id=1, source_target_pairs={{0,3},{1,2},{2,1},{3,0},{4,7},{5,6},{6,5},{7,4},{8,11},{9,10},{10,... | collective-permute-start | bytes 393224 | tf_op jit(solution)/shard_map/ppermute | solution.py:478
  35.6 1.6 %own_kernel.1 = (bf16[6,64,512]{2,1,0:T(8,128)(2,1)S(1)}, bf16[6,64,512]{2,1,0:T(8,128)(2,1)S(1)}) custom-call(bf16[2,8,64,256]{3,2,1,0:T(8,128)(2,1)S(1)} %whiten_block.5.mine_p, bf16[2,8,64,256]{3,2,1,0:T(8,128)(2,1)S(1)} %get-tuple-element.19.got_p, bf16[2,8,64,256]{3,2,1,0:T(8,128)(2,1)S(1)} %whiten_block.8.rest_0_.down0, ...), custom_call_target="tpu_custom_call" | custom-call | flops 1000 | bytes 1000 | tf_op jit(solution)/shard_map/own_kernel/pallas_call | solution.py:279
  37.2 1.5 %collective-permute-start.7 = (bf16[6,64,512]{2,1,0:T(8,128)(2,1)S(1)}, bf16[6,64,512]{2,1,0:T(8,128)(2,1)S(1)}, u32[]{:S(2)}, u32[]{:S(2)}) collective-permute-start(bf16[6,64,512]{2,1,0:T(8,128)(2,1)S(1)} %get-tuple-element.26), channel_id=1, source_target_pairs={{0,1},{1,0},{2,3},{3,2},{4,5},{5,4},{6,7},{7,6},{8,9},{9,8},{10,11... | collective-permute-start | bytes 1179656 | tf_op jit(solution)/shard_map/ppermute | solution.py:479
  38.7 0.0 collective-permute-done.10.refs_3_
  38.7 0.0 collective-permute-done.11.refs_4_
  38.7 0.0 copy-done
  38.7 0.0 copy-done.1
  38.7 0.0 copy-done.2
  38.8 1.0 %lags.2.straight = bf16[4,128,512]{2,1,0:T(8,128)(2,1)S(1)} custom-call(s32[1,4]{1,0:T(1,128)S(1)} %copy-done.1, s32[1,4]{1,0:T(1,128)S(1)} %copy-done.2, bf16[6,64,512]{2,1,0:T(8,128)(2,1)S(1)} %get-tuple-element.27.refs_2_, bf16[2,64,512]{2,1,0:T(8,128)(2,1)S(1)} %collective-permute-done.10.refs_3_, ...), custom_call_target="tpu_custom_call" | custom-call | flops 10000000000 | bytes 40000000 | tf_op jit(solution)/shard_map/lags/pallas_call | solution.py:351
  39.8 0.9 %collective-permute-done.8.refs_3_.side = bf16[2,64,512]{2,1,0:T(8,128)(2,1)S(1)} collective-permute-done((bf16[2,64,512]{2,1,0:T(8,128)(2,1)S(1)}, bf16[2,64,512]{2,1,0:T(8,128)(2,1)S(1)}, u32[]{:S(2)}, u32[]{:S(2)}) %collective-permute-start.8) | collective-permute-done | bytes 131104 | tf_op jit(solution)/shard_map/ppermute | solution.py:478
  40.6 0.0 collective-permute-done.7.refs_2_.own
  40.6 0.9 %lags.3 = (bf16[4,64,512]{2,1,0:T(8,128)(2,1)S(1)}, bf16[256,384]{1,0:T(8,128)(2,1)S(1)}, f32[4,512]{1,0:T(4,128)S(1)}) custom-call(s32[1,4]{1,0:T(1,128)S(1)} %copy-done.1, s32[1,4]{1,0:T(1,128)S(1)} %copy-done.2, bf16[6,64,512]{2,1,0:T(8,128)(2,1)S(1)} %collective-permute-done.7.refs_2_.own, bf16[2,64,512]{2,1,0:T(8,128)(2,1)S(1)} %collective-permute-done.8.refs_3_.side, ...), custom_call_target="tpu_custom_call" | custom-call | flops 10000000000 | bytes 40000000 | tf_op jit(solution)/shard_map/lags/pallas_call | solution.py:351
  41.6 1.4 %collective-permute-done.9.back = bf16[4,64,512]{2,1,0:T(8,128)(2,1)S(1)} collective-permute-done((bf16[4,64,512]{2,1,0:T(8,128)(2,1)S(1)}, bf16[4,64,512]{2,1,0:T(8,128)(2,1)S(1)}, u32[]{:S(2)}, u32[]{:S(2)}) %collective-permute-start.9) | collective-permute-done | bytes 262176 | tf_op jit(solution)/shard_map/ppermute | solution.py:477
  42.9 1.3 %last.1 = bf16[1,4,256,512]{3,2,1,0:T(8,128)(2,1)} custom-call(bf16[6,64,512]{2,1,0:T(8,128)(2,1)S(1)} %collective-permute-done.7.refs_2_.own, bf16[2,64,512]{2,1,0:T(8,128)(2,1)S(1)} %collective-permute-done.8.refs_3_.side, bf16[4,64,512]{2,1,0:T(8,128)(2,1)S(1)} %collective-permute-done.9.back, bf16[512,512]{1,0:T(8,128)(2,1)S(1)} %copy-done, ...), custom_call_target="tpu_custom_call" | custom-call | flops 1000 | bytes 1000 | tf_op jit(solution)/shard_map/last/pallas_call | solution.py:409
  (1 shorter events, 0.0 us)
Async XLA Ops:
  0.0 10.3 %collective-permute-start = (bf16[1,2,8,256,256]{4,3,2,1,0:T(8,128)(2,1)}, bf16[1,2,8,256,256]{4,3,2,1,0:T(8,128)(2,1)S(1)}, u32[]{:S(2)}, u32[]{:S(2)}) collective-permute-start(bf16[1,2,8,256,256]{4,3,2,1,0:T(8,128)(2,1)} %spectra.1), channel_id=1, source_target_pairs={{0,1},{1,0},{2,3},{3,2},{4,5},{5,4},{6,7},{7,6},{8,9},{9,8},{10,11... | collective-permute-start | bytes 6291464 | tf_op jit(solution)/shard_map/ppermute | solution.py:451
  1.9 15.3 %collective-permute-start.2 = (bf16[2,8,64,256]{3,2,1,0:T(8,128)(2,1)S(1)}, bf16[2,8,64,256]{3,2,1,0:T(8,128)(2,1)S(1)}, u32[]{:S(2)}, u32[]{:S(2)}) collective-permute-start(bf16[2,8,64,256]{3,2,1,0:T(8,128)(2,1)S(1)} %get-tuple-element.20), channel_id=1, source_target_pairs={{0,2},{1,3},{2,0},{3,1},{4,6},{5,7},{6,4},{7,5},{8,10},{9,11},{10,... | collective-permute-start | bytes 1572872 | tf_op jit(solution)/shard_map/ppermute | solution.py:454
  4.4 19.9 %collective-permute-start.1 = (bf16[2,8,64,256]{3,2,1,0:T(8,128)(2,1)S(1)}, bf16[2,8,64,256]{3,2,1,0:T(8,128)(2,1)S(1)}, u32[]{:S(2)}, u32[]{:S(2)}) collective-permute-start(bf16[2,8,64,256]{3,2,1,0:T(8,128)(2,1)S(1)} %get-tuple-element.18.source), channel_id=1, source_target_pairs={{4,0},{5,1},{6,2},{7,3},{8,4},{9,5},{10,6},{11,7},{12,8},{13,9},{1... | collective-permute-start | bytes 1572872 | tf_op jit(solution)/shard_map/ppermute | solution.py:453
  5.7 19.4 %collective-permute-start.6 = (bf16[2,8,64,256]{3,2,1,0:T(8,128)(2,1)S(1)}, bf16[2,8,64,256]{3,2,1,0:T(8,128)(2,1)S(1)}, u32[]{:S(2)}, u32[]{:S(2)}) collective-permute-start(bf16[2,8,64,256]{3,2,1,0:T(8,128)(2,1)S(1)} %get-tuple-element.21.source), channel_id=1, source_target_pairs={{0,4},{1,5},{2,6},{3,7},{4,8},{5,9},{6,10},{7,11},{8,12},{9,13},{1... | collective-permute-start | bytes 1572872 | tf_op jit(solution)/shard_map/ppermute | solution.py:455
  12.0 16.2 %collective-permute-start.4 = (bf16[2,8,64,256]{3,2,1,0:T(8,128)(2,1)S(1)}, bf16[2,8,64,256]{3,2,1,0:T(8,128)(2,1)S(1)}, u32[]{:S(2)}, u32[]{:S(2)}) collective-permute-start(bf16[2,8,64,256]{3,2,1,0:T(8,128)(2,1)S(1)} %get-tuple-element.23), channel_id=1, source_target_pairs={{0,2},{1,3},{2,0},{3,1},{4,6},{5,7},{6,4},{7,5},{8,10},{9,11},{10,... | collective-permute-start | bytes 1572872 | tf_op jit(solution)/shard_map/ppermute | solution.py:458
  12.1 19.4 %collective-permute-start.3 = (bf16[2,8,64,256]{3,2,1,0:T(8,128)(2,1)S(1)}, bf16[2,8,64,256]{3,2,1,0:T(8,128)(2,1)S(1)}, u32[]{:S(2)}, u32[]{:S(2)}) collective-permute-start(bf16[2,8,64,256]{3,2,1,0:T(8,128)(2,1)S(1)} %get-tuple-element.19.got_p), channel_id=1, source_target_pairs={{4,0},{5,1},{6,2},{7,3},{8,4},{9,5},{10,6},{11,7},{12,8},{13,9},{1... | collective-permute-start | bytes 1572872 | tf_op jit(solution)/shard_map/ppermute | solution.py:457
  17.2 15.5 %collective-permute-start.5 = (bf16[2,8,64,256]{3,2,1,0:T(8,128)(2,1)S(1)}, bf16[2,8,64,256]{3,2,1,0:T(8,128)(2,1)S(1)}, u32[]{:S(2)}, u32[]{:S(2)}) collective-permute-start(bf16[2,8,64,256]{3,2,1,0:T(8,128)(2,1)S(1)} %get-tuple-element.22.got_q), channel_id=1, source_target_pairs={{0,4},{1,5},{2,6},{3,7},{4,8},{5,9},{6,10},{7,11},{8,12},{9,13},{1... | collective-permute-start | bytes 1572872 | tf_op jit(solution)/shard_map/ppermute | solution.py:459
  28.3 10.5 %collective-permute-start.11 = (bf16[4,64,512]{2,1,0:T(8,128)(2,1)S(1)}, bf16[4,64,512]{2,1,0:T(8,128)(2,1)S(1)}, u32[]{:S(2)}, u32[]{:S(2)}) collective-permute-start(bf16[4,64,512]{2,1,0:T(8,128)(2,1)S(1)} %back_straight_kernel.1.after), channel_id=1, source_target_pairs={{4,0},{5,1},{6,2},{7,3},{8,4},{9,5},{10,6},{11,7},{12,8},{13,9},{1... | collective-permute-start | bytes 786440 | tf_op jit(solution)/shard_map/ppermute | solution.py:475
  31.9 6.8 %collective-permute-start.10 = (bf16[2,64,512]{2,1,0:T(8,128)(2,1)S(1)}, bf16[2,64,512]{2,1,0:T(8,128)(2,1)S(1)}, u32[]{:S(2)}, u32[]{:S(2)}) collective-permute-start(bf16[2,64,512]{2,1,0:T(8,128)(2,1)S(1)} %near_straight_kernel.1.after), channel_id=1, source_target_pairs={{0,2},{1,3},{2,0},{3,1},{4,6},{5,7},{6,4},{7,5},{8,10},{9,11},{10,... | collective-permute-start | bytes 393224 | tf_op jit(solution)/shard_map/ppermute | solution.py:476
  33.3 9.7 %collective-permute-start.9 = (bf16[4,64,512]{2,1,0:T(8,128)(2,1)S(1)}, bf16[4,64,512]{2,1,0:T(8,128)(2,1)S(1)}, u32[]{:S(2)}, u32[]{:S(2)}) collective-permute-start(bf16[4,64,512]{2,1,0:T(8,128)(2,1)S(1)} %back_kernel.1.after), channel_id=1, source_target_pairs={{4,1},{5,0},{6,3},{7,2},{8,5},{9,4},{10,7},{11,6},{12,9},{13,8},{1... | collective-permute-start | bytes 786440 | tf_op jit(solution)/shard_map/ppermute | solution.py:477
  35.1 3.7 %copy-start = (bf16[512,512]{1,0:T(8,128)(2,1)S(1)}, bf16[512,512]{1,0:T(8,128)(2,1)}, u32[]{:S(2)}) copy-start(bf16[512,512]{1,0:T(8,128)(2,1)} %constant.2.clone.refs_5_.refs_4_.table) | copy-start | bytes 1572868
  35.1 3.7 %copy-start.1 = (s32[1,4]{1,0:T(1,128)S(1)}, s32[1,4]{1,0:T(1,128)}, u32[]{:S(2)}) copy-start(s32[1,4]{1,0:T(1,128)} %refs_0_.3) | copy-start | bytes 52
  35.1 3.7 %copy-start.2 = (s32[1,4]{1,0:T(1,128)S(1)}, s32[1,4]{1,0:T(1,128)}, u32[]{:S(2)}) copy-start(s32[1,4]{1,0:T(1,128)} %refs_1_.3) | copy-start | bytes 52
  35.1 5.5 %collective-permute-start.8 = (bf16[2,64,512]{2,1,0:T(8,128)(2,1)S(1)}, bf16[2,64,512]{2,1,0:T(8,128)(2,1)S(1)}, u32[]{:S(2)}, u32[]{:S(2)}) collective-permute-start(bf16[2,64,512]{2,1,0:T(8,128)(2,1)S(1)} %near_kernel.1.after), channel_id=1, source_target_pairs={{0,3},{1,2},{2,1},{3,0},{4,7},{5,6},{6,5},{7,4},{8,11},{9,10},{10,... | collective-permute-start | bytes 393224 | tf_op jit(solution)/shard_map/ppermute | solution.py:478
  37.2 3.4 %collective-permute-start.7 = (bf16[6,64,512]{2,1,0:T(8,128)(2,1)S(1)}, bf16[6,64,512]{2,1,0:T(8,128)(2,1)S(1)}, u32[]{:S(2)}, u32[]{:S(2)}) collective-permute-start(bf16[6,64,512]{2,1,0:T(8,128)(2,1)S(1)} %get-tuple-element.26), channel_id=1, source_target_pairs={{0,1},{1,0},{2,3},{3,2},{4,5},{5,4},{6,7},{7,6},{8,9},{9,8},{10,11... | collective-permute-start | bytes 1179656 | tf_op jit(solution)/shard_map/ppermute | solution.py:479

commit v9 on v8

--- a/solution.py
+++ b/solution.py
@@ -31,7 +31,7 @@
             write(w, block, (values * lax.rsqrt(power + 1e-06)).astype(jnp.bfloat16))
         return 0
 
-    lax.fori_loop(0, windows, one_window, 0)
+    lax.fori_loop(0, windows, one_window, 0, unroll=2)
 
 
 def place():
@@ -163,7 +163,7 @@
                         ).astype(jnp.bfloat16)
         return 0
 
-    lax.fori_loop(0, rows // TILE, one_tile, 0)
+    lax.fori_loop(0, rows // TILE, one_tile, 0, unroll=4)
 
 
 def reader(ref, *lead):
@@ -368,9 +368,9 @@
     slots, rows = lagged.shape[:2]
     copies = []
 
-    def leave(source, k, half):
+    def leave(source, k, half, slot=slice(None)):
         target = pl.multiple_of((2 * k + half) * rows, rows)
-        target = out.at[0, :, pl.ds(target, rows), :]
+        target = out.at[0, slot, pl.ds(target, rows), :]
         copies.append(pltpu.make_async_copy(source, target, sent.at[len(copies)]))
         copies[-1].start()
 
@@ -392,12 +392,14 @@
     spectrum = jnp.dot(
         choice[...], cand[...].reshape(6 * rows, -1), preferred_element_type=jnp.float32
     ).astype(jnp.bfloat16)
-    product = jnp.dot(spectrum, table[...], preferred_element_type=jnp.float32)
-    for slot in range(slots):
-        keep = kept[pl.ds(slot, 1), :] > 0.0
-        part = jnp.where(keep, product[slot * rows : (slot + 1) * rows], 0.0)
-        lagged[slot] = part.astype(jnp.bfloat16)
-    leave(lagged, 1, 1 - core)
+    for slot in range(0, slots, 2):
+        pair = spectrum[slot * rows : (slot + 2) * rows]
+        product = jnp.dot(pair, table[...], preferred_element_type=jnp.float32)
+        for near in range(2):
+            keep = kept[pl.ds(slot + near, 1), :] > 0.0
+            part = jnp.where(keep, product[near * rows : (near + 1) * rows], 0.0)
+            lagged[slot + near] = part.astype(jnp.bfloat16)
+            leave(lagged.at[slot + near], 1, 1 - core, slot + near)
     for copy in copies:
         copy.wait()
 
@@ -414,7 +416,7 @@
         scratch_shapes=[
             pltpu.VMEM((slots, rows, lags), jnp.bfloat16),
             pltpu.VMEM((6, rows, width), jnp.bfloat16),
-            pltpu.SemaphoreType.DMA((4,)),
+            pltpu.SemaphoreType.DMA((3 + slots,)),
         ],
         compiler_params=pltpu.CompilerParams(vmem_limit_bytes=VMEM_LIMIT),
         cost_estimate=SMALL,

time: 44.9 us -> 44.8 us (level)
  Pallas kernels: 14.9 us -> 12 us
  waiting for transfers between devices: 10.2 us -> 13.1 us
    ppermute x1, waiting for transfers between devices: 1.38 us -> 3.37 us  [local(): side1 = move['xs'](got_side)]
    pallas_call x5, Pallas kernels: 4.06 us -> 2.27 us  [whiten_block(): pl.pallas_call(whiten_block_kernel, out_shape=jax.ShapeDtypeStruct(block....]
    ppermute x1, waiting for transfers between devices: 3.79 us -> 4.49 us  [local(): side0 = move['xs'](side_raw)]
    pallas_call x1, Pallas kernels: 1.66 us -> 0.96 us  [whiten_got(): pl.pallas_call(whiten_got_kernel, out_shape=[jax.ShapeDtypeStruct(shape,...]
  transfers between devices with their start and end apart: 12 -> 12, of which waited for: 6 -> 6; matrix products, arithmetic and copies ran while one was open for 0% -> 0% of each run, Pallas kernels for 31% -> 24%
where the time goes in v9:
time: 44.8 us; the launch traced here: 44.2 us
  starting transfers between devices  18.9 us (42%)
  waiting for transfers between devices  13.1 us (29%)
  Pallas kernels  12 us (27%)
    ppermute x1, starting transfers between devices, local(): up0 = move['up'](up_raw)  4.58 us
    ppermute x1, waiting for transfers between devices, local(): side0 = move['xs'](side_raw)  4.49 us
    pallas_call x7, Pallas kernels, cross(): pl.pallas_call(kernel, out_shape=[jax.ShapeDtypeStruct((n, rows, 2 * bins...  4.17 us
    ppermute x1, starting transfers between devices, local(): up1 = move['up'](got_q)  3.94 us
    ppermute x1, waiting for transfers between devices, local(): side1 = move['xs'](got_side)  3.37 us
    ppermute x1, starting transfers between devices, local(): side0 = move['xs'](side_raw)  2.57 us
    pallas_call x5, Pallas kernels, whiten_block(): pl.pallas_call(whiten_block_kernel, out_shape=jax.ShapeDtypeStruct(block....  2.27 us
    ppermute x1, waiting for transfers between devices, local(): down1 = move['down'](got_p)  2.02 us
  transfers between devices with their start and end apart: 12, of which 6 were waited for; matrix products, arithmetic and copies ran while one was open for 0% of the time, Pallas kernels for 24%

profile of v9, /device:TPU:0, one launch (start us, length us, event | category | flops | bytes accessed | tf_op | source)
XLA Modules:
  0.0 44.2 jit_solution(9950803778985778347)
XLA Ops:
  0.0 0.5 %collective-permute-start = (bf16[1,2,8,256,256]{4,3,2,1,0:T(8,128)(2,1)}, bf16[1,2,8,256,256]{4,3,2,1,0:T(8,128)(2,1)S(1)}, u32[]{:S(2)}, u32[]{:S(2)}) collective-permute-start(bf16[1,2,8,256,256]{4,3,2,1,0:T(8,128)(2,1)} %spectra.1), channel_id=1, source_target_pairs={{0,1},{1,0},{2,3},{3,2},{4,5},{5,4},{6,7},{7,6},{8,9},{9,8},{10,11... | collective-permute-start | bytes 6291464 | tf_op jit(solution)/shard_map/ppermute | solution.py:453
  0.5 1.4 %quarters.1 = (bf16[2,8,64,256]{3,2,1,0:T(8,128)(2,1)S(1)}, bf16[2,8,64,256]{3,2,1,0:T(8,128)(2,1)S(1)}, bf16[2,8,64,256]{3,2,1,0:T(8,128)(2,1)S(1)}) custom-call(bf16[1,2,8,256,256]{4,3,2,1,0:T(8,128)(2,1)} %spectra.1), custom_call_target="tpu_custom_call" | custom-call | flops 1000 | bytes 1000 | tf_op jit(solution)/shard_map/quarters/pallas_call | solution.py:63
  1.9 2.6 %collective-permute-start.2 = (bf16[2,8,64,256]{3,2,1,0:T(8,128)(2,1)S(1)}, bf16[2,8,64,256]{3,2,1,0:T(8,128)(2,1)S(1)}, u32[]{:S(2)}, u32[]{:S(2)}) collective-permute-start(bf16[2,8,64,256]{3,2,1,0:T(8,128)(2,1)S(1)} %get-tuple-element.20), channel_id=1, source_target_pairs={{0,2},{1,3},{2,0},{3,1},{4,6},{5,7},{6,4},{7,5},{8,10},{9,11},{10,... | collective-permute-start | bytes 1572872 | tf_op jit(solution)/shard_map/ppermute | solution.py:456
  4.4 1.3 %collective-permute-start.1 = (bf16[2,8,64,256]{3,2,1,0:T(8,128)(2,1)S(1)}, bf16[2,8,64,256]{3,2,1,0:T(8,128)(2,1)S(1)}, u32[]{:S(2)}, u32[]{:S(2)}) collective-permute-start(bf16[2,8,64,256]{3,2,1,0:T(8,128)(2,1)S(1)} %get-tuple-element.18.source), channel_id=1, source_target_pairs={{4,0},{5,1},{6,2},{7,3},{8,4},{9,5},{10,6},{11,7},{12,8},{13,9},{1... | collective-permute-start | bytes 1572872 | tf_op jit(solution)/shard_map/ppermute | solution.py:455
  5.7 4.6 %collective-permute-start.6 = (bf16[2,8,64,256]{3,2,1,0:T(8,128)(2,1)S(1)}, bf16[2,8,64,256]{3,2,1,0:T(8,128)(2,1)S(1)}, u32[]{:S(2)}, u32[]{:S(2)}) collective-permute-start(bf16[2,8,64,256]{3,2,1,0:T(8,128)(2,1)S(1)} %get-tuple-element.21.source), channel_id=1, source_target_pairs={{0,4},{1,5},{2,6},{3,7},{4,8},{5,9},{6,10},{7,11},{8,12},{9,13},{1... | collective-permute-start | bytes 1572872 | tf_op jit(solution)/shard_map/ppermute | solution.py:457
  10.3 0.0 collective-permute-done.got
  10.3 1.0 %whiten_got.1 = (bf16[2,8,64,256]{3,2,1,0:T(8,128)(2,1)S(1)}, bf16[2,8,64,256]{3,2,1,0:T(8,128)(2,1)S(1)}, bf16[2,8,64,256]{3,2,1,0:T(8,128)(2,1)S(1)}) custom-call(bf16[1,2,8,256,256]{4,3,2,1,0:T(8,128)(2,1)S(1)} %collective-permute-done.got), custom_call_target="tpu_custom_call" | custom-call | flops 1000 | bytes 1000 | tf_op jit(solution)/shard_map/whiten_got/pallas_call | solution.py:102
  11.3 0.1 collective-permute-start.4
  11.4 1.3 %collective-permute-start.3 = (bf16[2,8,64,256]{3,2,1,0:T(8,128)(2,1)S(1)}, bf16[2,8,64,256]{3,2,1,0:T(8,128)(2,1)S(1)}, u32[]{:S(2)}, u32[]{:S(2)}) collective-permute-start(bf16[2,8,64,256]{3,2,1,0:T(8,128)(2,1)S(1)} %get-tuple-element.19.got_p), channel_id=1, source_target_pairs={{4,0},{5,1},{6,2},{7,3},{8,4},{9,5},{10,6},{11,7},{12,8},{13,9},{1... | collective-permute-start | bytes 1572872 | tf_op jit(solution)/shard_map/ppermute | solution.py:459
  12.7 4.5 %collective-permute-done.2.source = bf16[2,8,64,256]{3,2,1,0:T(8,128)(2,1)S(1)} collective-permute-done((bf16[2,8,64,256]{3,2,1,0:T(8,128)(2,1)S(1)}, bf16[2,8,64,256]{3,2,1,0:T(8,128)(2,1)S(1)}, u32[]{:S(2)}, u32[]{:S(2)}) %collective-permute-start.2) | collective-permute-done | bytes 524320 | tf_op jit(solution)/shard_map/ppermute | solution.py:456
  17.2 3.9 %collective-permute-start.5 = (bf16[2,8,64,256]{3,2,1,0:T(8,128)(2,1)S(1)}, bf16[2,8,64,256]{3,2,1,0:T(8,128)(2,1)S(1)}, u32[]{:S(2)}, u32[]{:S(2)}) collective-permute-start(bf16[2,8,64,256]{3,2,1,0:T(8,128)(2,1)S(1)} %get-tuple-element.22.got_q), channel_id=1, source_target_pairs={{0,4},{1,5},{2,6},{3,7},{4,8},{5,9},{6,10},{7,11},{8,12},{9,13},{1... | collective-permute-start | bytes 1572872 | tf_op jit(solution)/shard_map/ppermute | solution.py:461
  21.1 0.5 %whiten_block.6.mine_q = bf16[2,8,64,256]{3,2,1,0:T(8,128)(2,1)S(1)} custom-call(bf16[2,8,64,256]{3,2,1,0:T(8,128)(2,1)S(1)} %get-tuple-element.21.source), custom_call_target="tpu_custom_call" | custom-call | flops 1000 | bytes 1000 | tf_op jit(solution)/shard_map/whiten_block/pallas_call | solution.py:128
  21.6 0.5 %whiten_block.5.mine_p = bf16[2,8,64,256]{3,2,1,0:T(8,128)(2,1)S(1)} custom-call(bf16[2,8,64,256]{3,2,1,0:T(8,128)(2,1)S(1)} %get-tuple-element.18.source), custom_call_target="tpu_custom_call" | custom-call | flops 1000 | bytes 1000 | tf_op jit(solution)/shard_map/whiten_block/pallas_call | solution.py:128
  22.1 0.6 %chip_kernel.1.rest_0_.pair = bf16[2,64,512]{2,1,0:T(8,128)(2,1)S(1)} custom-call(bf16[2,8,64,256]{3,2,1,0:T(8,128)(2,1)S(1)} %whiten_block.5.mine_p, bf16[2,8,64,256]{3,2,1,0:T(8,128)(2,1)S(1)} %get-tuple-element.19.got_p, bf16[2,8,64,256]{3,2,1,0:T(8,128)(2,1)S(1)} %whiten_block.6.mine_q, bf16[2,8,64,256]{3,2,1,0:T(8,128)(2,1)S(1)} %get-tuple-element.22.got_q), custom_call_target="tpu_custom_call" | custom-call | flops 1000 | bytes 1000 | tf_op jit(solution)/shard_map/chip_kernel/pallas_call | solution.py:279
  22.7 0.5 %whiten_block.7.rest_0_.side0.side = bf16[2,8,64,256]{3,2,1,0:T(8,128)(2,1)S(1)} custom-call(bf16[2,8,64,256]{3,2,1,0:T(8,128)(2,1)S(1)} %collective-permute-done.2.source, bf16[2,64,512]{2,1,0:T(8,128)(2,1)S(1)} %chip_kernel.1.rest_0_.pair), custom_call_target="tpu_custom_call" | custom-call | flops 1000 | bytes 1000 | tf_op jit(solution)/shard_map/whiten_block/pallas_call | solution.py:128
  23.1 0.0 collective-permute-done.1.source
  23.2 0.5 %whiten_block.8.rest_0_.down0 = bf16[2,8,64,256]{3,2,1,0:T(8,128)(2,1)S(1)} custom-call(bf16[2,8,64,256]{3,2,1,0:T(8,128)(2,1)S(1)} %collective-permute-done.1.source, bf16[2,8,64,256]{3,2,1,0:T(8,128)(2,1)S(1)} %whiten_block.7.rest_0_.side0.side), custom_call_target="tpu_custom_call" | custom-call | flops 1000 | bytes 1000 | tf_op jit(solution)/shard_map/whiten_block/pallas_call | solution.py:128
  23.6 0.0 collective-permute-done.6.source
  23.6 0.5 %whiten_block.9.up0.after.up = bf16[2,8,64,256]{3,2,1,0:T(8,128)(2,1)S(1)} custom-call(bf16[2,8,64,256]{3,2,1,0:T(8,128)(2,1)S(1)} %collective-permute-done.6.source, bf16[2,8,64,256]{3,2,1,0:T(8,128)(2,1)S(1)} %whiten_block.8.rest_0_.down0), custom_call_target="tpu_custom_call" | custom-call | flops 1000 | bytes 1000 | tf_op jit(solution)/shard_map/whiten_block/pallas_call | solution.py:128
  24.1 0.8 %early_kernel.1 = (bf16[2,64,512]{2,1,0:T(8,128)(2,1)S(1)}, bf16[2,64,512]{2,1,0:T(8,128)(2,1)S(1)}) custom-call(bf16[2,8,64,256]{3,2,1,0:T(8,128)(2,1)S(1)} %whiten_block.6.mine_q, bf16[2,8,64,256]{3,2,1,0:T(8,128)(2,1)S(1)} %get-tuple-element.22.got_q, bf16[2,8,64,256]{3,2,1,0:T(8,128)(2,1)S(1)} %whiten_block.9.up0.after.up, ...), custom_call_target="tpu_custom_call" | custom-call | flops 1000 | bytes 1000 | tf_op jit(solution)/shard_map/early_kernel/pallas_call | solution.py:279
  24.9 3.4 %collective-permute-done.4.side1.side = bf16[2,8,64,256]{3,2,1,0:T(8,128)(2,1)S(1)} collective-permute-done((bf16[2,8,64,256]{3,2,1,0:T(8,128)(2,1)S(1)}, bf16[2,8,64,256]{3,2,1,0:T(8,128)(2,1)S(1)}, u32[]{:S(2)}, u32[]{:S(2)}) %collective-permute-start.4) | collective-permute-done | bytes 524320 | tf_op jit(solution)/shard_map/ppermute | solution.py:460
  28.3 1.3 %collective-permute-start.11 = (bf16[4,64,512]{2,1,0:T(8,128)(2,1)S(1)}, bf16[4,64,512]{2,1,0:T(8,128)(2,1)S(1)}, u32[]{:S(2)}, u32[]{:S(2)}) collective-permute-start(bf16[4,64,512]{2,1,0:T(8,128)(2,1)S(1)} %back_straight_kernel.1.after), channel_id=1, source_target_pairs={{4,0},{5,1},{6,2},{7,3},{8,4},{9,5},{10,6},{11,7},{12,8},{13,9},{1... | collective-permute-start | bytes 786440 | tf_op jit(solution)/shard_map/ppermute | solution.py:477
  29.6 2.0 %collective-permute-done.3.down1 = bf16[2,8,64,256]{3,2,1,0:T(8,128)(2,1)S(1)} collective-permute-done((bf16[2,8,64,256]{3,2,1,0:T(8,128)(2,1)S(1)}, bf16[2,8,64,256]{3,2,1,0:T(8,128)(2,1)S(1)}, u32[]{:S(2)}, u32[]{:S(2)}) %collective-permute-start.3) | collective-permute-done | bytes 524320 | tf_op jit(solution)/shard_map/ppermute | solution.py:459
  31.6 0.3 near_straight_kernel.1.after
  31.9 0.2 collective-permute-start.10
  32.0 0.7 %collective-permute-done.5.up = bf16[2,8,64,256]{3,2,1,0:T(8,128)(2,1)S(1)} collective-permute-done((bf16[2,8,64,256]{3,2,1,0:T(8,128)(2,1)S(1)}, bf16[2,8,64,256]{3,2,1,0:T(8,128)(2,1)S(1)}, u32[]{:S(2)}, u32[]{:S(2)}) %collective-permute-start.5) | collective-permute-done | bytes 524320 | tf_op jit(solution)/shard_map/ppermute | solution.py:461
  32.8 0.5 %back_kernel.1.after = bf16[4,64,512]{2,1,0:T(8,128)(2,1)S(1)} custom-call(bf16[2,8,64,256]{3,2,1,0:T(8,128)(2,1)S(1)} %whiten_block.6.mine_q, bf16[2,8,64,256]{3,2,1,0:T(8,128)(2,1)S(1)} %get-tuple-element.22.got_q, bf16[2,8,64,256]{3,2,1,0:T(8,128)(2,1)S(1)} %collective-permute-done.5.up, bf16[2,8,64,256]{3,2,1,0:T(8,128)(2,1)S(1)} %whiten_block.7.rest_0_.side0.side, ...), custom_call_target="tpu_custom_call" | custom-call | flops 1000 | bytes 1000 | tf_op jit(solution)/shard_map/back_kernel/pallas_call | solution.py:279
  33.2 1.3 %collective-permute-start.9 = (bf16[4,64,512]{2,1,0:T(8,128)(2,1)S(1)}, bf16[4,64,512]{2,1,0:T(8,128)(2,1)S(1)}, u32[]{:S(2)}, u32[]{:S(2)}) collective-permute-start(bf16[4,64,512]{2,1,0:T(8,128)(2,1)S(1)} %back_kernel.1.after), channel_id=1, source_target_pairs={{4,1},{5,0},{6,3},{7,2},{8,5},{9,4},{10,7},{11,6},{12,9},{13,8},{1... | collective-permute-start | bytes 786440 | tf_op jit(solution)/shard_map/ppermute | solution.py:479
  34.5 0.5 %near_kernel.1.after = bf16[2,64,512]{2,1,0:T(8,128)(2,1)S(1)} custom-call(bf16[2,8,64,256]{3,2,1,0:T(8,128)(2,1)S(1)} %whiten_block.6.mine_q, bf16[2,8,64,256]{3,2,1,0:T(8,128)(2,1)S(1)} %get-tuple-element.22.got_q, bf16[2,8,64,256]{3,2,1,0:T(8,128)(2,1)S(1)} %whiten_block.8.rest_0_.down0, bf16[2,8,64,256]{3,2,1,0:T(8,128)(2,1)S(1)} %collective-permute-done.3.down1, ...), custom_call_target="tpu_custom_call" | custom-call | flops 1000 | bytes 1000 | tf_op jit(solution)/shard_map/near_kernel/pallas_call | solution.py:279
  35.0 0.0 copy-start
  35.1 0.0 copy-start.1
  35.1 0.0 copy-start.2
  35.1 0.5 %collective-permute-start.8 = (bf16[2,64,512]{2,1,0:T(8,128)(2,1)S(1)}, bf16[2,64,512]{2,1,0:T(8,128)(2,1)S(1)}, u32[]{:S(2)}, u32[]{:S(2)}) collective-permute-start(bf16[2,64,512]{2,1,0:T(8,128)(2,1)S(1)} %near_kernel.1.after), channel_id=1, source_target_pairs={{0,3},{1,2},{2,1},{3,0},{4,7},{5,6},{6,5},{7,4},{8,11},{9,10},{10,... | collective-permute-start | bytes 393224 | tf_op jit(solution)/shard_map/ppermute | solution.py:480
  35.5 1.5 %own_kernel.1 = (bf16[6,64,512]{2,1,0:T(8,128)(2,1)S(1)}, bf16[6,64,512]{2,1,0:T(8,128)(2,1)S(1)}) custom-call(bf16[2,8,64,256]{3,2,1,0:T(8,128)(2,1)S(1)} %whiten_block.5.mine_p, bf16[2,8,64,256]{3,2,1,0:T(8,128)(2,1)S(1)} %get-tuple-element.19.got_p, bf16[2,8,64,256]{3,2,1,0:T(8,128)(2,1)S(1)} %whiten_block.8.rest_0_.down0, ...), custom_call_target="tpu_custom_call" | custom-call | flops 1000 | bytes 1000 | tf_op jit(solution)/shard_map/own_kernel/pallas_call | solution.py:279
  37.0 1.5 %collective-permute-start.7 = (bf16[6,64,512]{2,1,0:T(8,128)(2,1)S(1)}, bf16[6,64,512]{2,1,0:T(8,128)(2,1)S(1)}, u32[]{:S(2)}, u32[]{:S(2)}) collective-permute-start(bf16[6,64,512]{2,1,0:T(8,128)(2,1)S(1)} %get-tuple-element.26), channel_id=1, source_target_pairs={{0,1},{1,0},{2,3},{3,2},{4,5},{5,4},{6,7},{7,6},{8,9},{9,8},{10,11... | collective-permute-start | bytes 1179656 | tf_op jit(solution)/shard_map/ppermute | solution.py:481
  38.5 0.0 collective-permute-done.10.refs_3_
  38.5 0.0 collective-permute-done.11.refs_4_
  38.5 0.0 copy-done
  38.5 0.0 copy-done.1
  38.5 0.0 copy-done.2
  38.6 1.0 %lags.2.straight = bf16[4,128,512]{2,1,0:T(8,128)(2,1)S(1)} custom-call(s32[1,4]{1,0:T(1,128)S(1)} %copy-done.1, s32[1,4]{1,0:T(1,128)S(1)} %copy-done.2, bf16[6,64,512]{2,1,0:T(8,128)(2,1)S(1)} %get-tuple-element.27.refs_2_, bf16[2,64,512]{2,1,0:T(8,128)(2,1)S(1)} %collective-permute-done.10.refs_3_, ...), custom_call_target="tpu_custom_call" | custom-call | flops 10000000000 | bytes 40000000 | tf_op jit(solution)/shard_map/lags/pallas_call | solution.py:351
  39.6 1.1 %collective-permute-done.8.refs_3_.side = bf16[2,64,512]{2,1,0:T(8,128)(2,1)S(1)} collective-permute-done((bf16[2,64,512]{2,1,0:T(8,128)(2,1)S(1)}, bf16[2,64,512]{2,1,0:T(8,128)(2,1)S(1)}, u32[]{:S(2)}, u32[]{:S(2)}) %collective-permute-start.8) | collective-permute-done | bytes 131104 | tf_op jit(solution)/shard_map/ppermute | solution.py:480
  40.7 0.0 collective-permute-done.7.refs_2_.own
  40.7 0.9 %lags.3 = (bf16[4,64,512]{2,1,0:T(8,128)(2,1)S(1)}, bf16[256,384]{1,0:T(8,128)(2,1)S(1)}, f32[4,512]{1,0:T(4,128)S(1)}) custom-call(s32[1,4]{1,0:T(1,128)S(1)} %copy-done.1, s32[1,4]{1,0:T(1,128)S(1)} %copy-done.2, bf16[6,64,512]{2,1,0:T(8,128)(2,1)S(1)} %collective-permute-done.7.refs_2_.own, bf16[2,64,512]{2,1,0:T(8,128)(2,1)S(1)} %collective-permute-done.8.refs_3_.side, ...), custom_call_target="tpu_custom_call" | custom-call | flops 10000000000 | bytes 40000000 | tf_op jit(solution)/shard_map/lags/pallas_call | solution.py:351
  41.6 1.4 %collective-permute-done.9.back = bf16[4,64,512]{2,1,0:T(8,128)(2,1)S(1)} collective-permute-done((bf16[4,64,512]{2,1,0:T(8,128)(2,1)S(1)}, bf16[4,64,512]{2,1,0:T(8,128)(2,1)S(1)}, u32[]{:S(2)}, u32[]{:S(2)}) %collective-permute-start.9) | collective-permute-done | bytes 262176 | tf_op jit(solution)/shard_map/ppermute | solution.py:479
  43.0 1.2 %last.1 = bf16[1,4,256,512]{3,2,1,0:T(8,128)(2,1)} custom-call(bf16[6,64,512]{2,1,0:T(8,128)(2,1)S(1)} %collective-permute-done.7.refs_2_.own, bf16[2,64,512]{2,1,0:T(8,128)(2,1)S(1)} %collective-permute-done.8.refs_3_.side, bf16[4,64,512]{2,1,0:T(8,128)(2,1)S(1)} %collective-permute-done.9.back, bf16[512,512]{1,0:T(8,128)(2,1)S(1)} %copy-done, ...), custom_call_target="tpu_custom_call" | custom-call | flops 1000 | bytes 1000 | tf_op jit(solution)/shard_map/last/pallas_call | solution.py:411
  (1 shorter events, 0.0 us)
Async XLA Ops:
  0.0 10.3 %collective-permute-start = (bf16[1,2,8,256,256]{4,3,2,1,0:T(8,128)(2,1)}, bf16[1,2,8,256,256]{4,3,2,1,0:T(8,128)(2,1)S(1)}, u32[]{:S(2)}, u32[]{:S(2)}) collective-permute-start(bf16[1,2,8,256,256]{4,3,2,1,0:T(8,128)(2,1)} %spectra.1), channel_id=1, source_target_pairs={{0,1},{1,0},{2,3},{3,2},{4,5},{5,4},{6,7},{7,6},{8,9},{9,8},{10,11... | collective-permute-start | bytes 6291464 | tf_op jit(solution)/shard_map/ppermute | solution.py:453
  1.9 15.3 %collective-permute-start.2 = (bf16[2,8,64,256]{3,2,1,0:T(8,128)(2,1)S(1)}, bf16[2,8,64,256]{3,2,1,0:T(8,128)(2,1)S(1)}, u32[]{:S(2)}, u32[]{:S(2)}) collective-permute-start(bf16[2,8,64,256]{3,2,1,0:T(8,128)(2,1)S(1)} %get-tuple-element.20), channel_id=1, source_target_pairs={{0,2},{1,3},{2,0},{3,1},{4,6},{5,7},{6,4},{7,5},{8,10},{9,11},{10,... | collective-permute-start | bytes 1572872 | tf_op jit(solution)/shard_map/ppermute | solution.py:456
  4.4 18.7 %collective-permute-start.1 = (bf16[2,8,64,256]{3,2,1,0:T(8,128)(2,1)S(1)}, bf16[2,8,64,256]{3,2,1,0:T(8,128)(2,1)S(1)}, u32[]{:S(2)}, u32[]{:S(2)}) collective-permute-start(bf16[2,8,64,256]{3,2,1,0:T(8,128)(2,1)S(1)} %get-tuple-element.18.source), channel_id=1, source_target_pairs={{4,0},{5,1},{6,2},{7,3},{8,4},{9,5},{10,6},{11,7},{12,8},{13,9},{1... | collective-permute-start | bytes 1572872 | tf_op jit(solution)/shard_map/ppermute | solution.py:455
  5.7 17.9 %collective-permute-start.6 = (bf16[2,8,64,256]{3,2,1,0:T(8,128)(2,1)S(1)}, bf16[2,8,64,256]{3,2,1,0:T(8,128)(2,1)S(1)}, u32[]{:S(2)}, u32[]{:S(2)}) collective-permute-start(bf16[2,8,64,256]{3,2,1,0:T(8,128)(2,1)S(1)} %get-tuple-element.21.source), channel_id=1, source_target_pairs={{0,4},{1,5},{2,6},{3,7},{4,8},{5,9},{6,10},{7,11},{8,12},{9,13},{1... | collective-permute-start | bytes 1572872 | tf_op jit(solution)/shard_map/ppermute | solution.py:457
  11.3 16.9 %collective-permute-start.4 = (bf16[2,8,64,256]{3,2,1,0:T(8,128)(2,1)S(1)}, bf16[2,8,64,256]{3,2,1,0:T(8,128)(2,1)S(1)}, u32[]{:S(2)}, u32[]{:S(2)}) collective-permute-start(bf16[2,8,64,256]{3,2,1,0:T(8,128)(2,1)S(1)} %get-tuple-element.23), channel_id=1, source_target_pairs={{0,2},{1,3},{2,0},{3,1},{4,6},{5,7},{6,4},{7,5},{8,10},{9,11},{10,... | collective-permute-start | bytes 1572872 | tf_op jit(solution)/shard_map/ppermute | solution.py:460
  11.4 20.1 %collective-permute-start.3 = (bf16[2,8,64,256]{3,2,1,0:T(8,128)(2,1)S(1)}, bf16[2,8,64,256]{3,2,1,0:T(8,128)(2,1)S(1)}, u32[]{:S(2)}, u32[]{:S(2)}) collective-permute-start(bf16[2,8,64,256]{3,2,1,0:T(8,128)(2,1)S(1)} %get-tuple-element.19.got_p), channel_id=1, source_target_pairs={{4,0},{5,1},{6,2},{7,3},{8,4},{9,5},{10,6},{11,7},{12,8},{13,9},{1... | collective-permute-start | bytes 1572872 | tf_op jit(solution)/shard_map/ppermute | solution.py:459
  17.2 15.5 %collective-permute-start.5 = (bf16[2,8,64,256]{3,2,1,0:T(8,128)(2,1)S(1)}, bf16[2,8,64,256]{3,2,1,0:T(8,128)(2,1)S(1)}, u32[]{:S(2)}, u32[]{:S(2)}) collective-permute-start(bf16[2,8,64,256]{3,2,1,0:T(8,128)(2,1)S(1)} %get-tuple-element.22.got_q), channel_id=1, source_target_pairs={{0,4},{1,5},{2,6},{3,7},{4,8},{5,9},{6,10},{7,11},{8,12},{9,13},{1... | collective-permute-start | bytes 1572872 | tf_op jit(solution)/shard_map/ppermute | solution.py:461
  28.3 10.3 %collective-permute-start.11 = (bf16[4,64,512]{2,1,0:T(8,128)(2,1)S(1)}, bf16[4,64,512]{2,1,0:T(8,128)(2,1)S(1)}, u32[]{:S(2)}, u32[]{:S(2)}) collective-permute-start(bf16[4,64,512]{2,1,0:T(8,128)(2,1)S(1)} %back_straight_kernel.1.after), channel_id=1, source_target_pairs={{4,0},{5,1},{6,2},{7,3},{8,4},{9,5},{10,6},{11,7},{12,8},{13,9},{1... | collective-permute-start | bytes 786440 | tf_op jit(solution)/shard_map/ppermute | solution.py:477
  31.9 6.6 %collective-permute-start.10 = (bf16[2,64,512]{2,1,0:T(8,128)(2,1)S(1)}, bf16[2,64,512]{2,1,0:T(8,128)(2,1)S(1)}, u32[]{:S(2)}, u32[]{:S(2)}) collective-permute-start(bf16[2,64,512]{2,1,0:T(8,128)(2,1)S(1)} %near_straight_kernel.1.after), channel_id=1, source_target_pairs={{0,2},{1,3},{2,0},{3,1},{4,6},{5,7},{6,4},{7,5},{8,10},{9,11},{10,... | collective-permute-start | bytes 393224 | tf_op jit(solution)/shard_map/ppermute | solution.py:478
  33.2 9.7 %collective-permute-start.9 = (bf16[4,64,512]{2,1,0:T(8,128)(2,1)S(1)}, bf16[4,64,512]{2,1,0:T(8,128)(2,1)S(1)}, u32[]{:S(2)}, u32[]{:S(2)}) collective-permute-start(bf16[4,64,512]{2,1,0:T(8,128)(2,1)S(1)} %back_kernel.1.after), channel_id=1, source_target_pairs={{4,1},{5,0},{6,3},{7,2},{8,5},{9,4},{10,7},{11,6},{12,9},{13,8},{1... | collective-permute-start | bytes 786440 | tf_op jit(solution)/shard_map/ppermute | solution.py:479
  35.0 3.5 %copy-start = (bf16[512,512]{1,0:T(8,128)(2,1)S(1)}, bf16[512,512]{1,0:T(8,128)(2,1)}, u32[]{:S(2)}) copy-start(bf16[512,512]{1,0:T(8,128)(2,1)} %constant.2.clone.refs_5_.refs_4_.table) | copy-start | bytes 1572868
  35.1 3.5 %copy-start.1 = (s32[1,4]{1,0:T(1,128)S(1)}, s32[1,4]{1,0:T(1,128)}, u32[]{:S(2)}) copy-start(s32[1,4]{1,0:T(1,128)} %refs_0_.3) | copy-start | bytes 52
  35.1 3.5 %copy-start.2 = (s32[1,4]{1,0:T(1,128)S(1)}, s32[1,4]{1,0:T(1,128)}, u32[]{:S(2)}) copy-start(s32[1,4]{1,0:T(1,128)} %refs_1_.3) | copy-start | bytes 52
  35.1 5.6 %collective-permute-start.8 = (bf16[2,64,512]{2,1,0:T(8,128)(2,1)S(1)}, bf16[2,64,512]{2,1,0:T(8,128)(2,1)S(1)}, u32[]{:S(2)}, u32[]{:S(2)}) collective-permute-start(bf16[2,64,512]{2,1,0:T(8,128)(2,1)S(1)} %near_kernel.1.after), channel_id=1, source_target_pairs={{0,3},{1,2},{2,1},{3,0},{4,7},{5,6},{6,5},{7,4},{8,11},{9,10},{10,... | collective-permute-start | bytes 393224 | tf_op jit(solution)/shard_map/ppermute | solution.py:480
  37.0 3.6 %collective-permute-start.7 = (bf16[6,64,512]{2,1,0:T(8,128)(2,1)S(1)}, bf16[6,64,512]{2,1,0:T(8,128)(2,1)S(1)}, u32[]{:S(2)}, u32[]{:S(2)}) collective-permute-start(bf16[6,64,512]{2,1,0:T(8,128)(2,1)S(1)} %get-tuple-element.26), channel_id=1, source_target_pairs={{0,1},{1,0},{2,3},{3,2},{4,5},{5,4},{6,7},{7,6},{8,9},{9,8},{10,11... | collective-permute-start | bytes 1179656 | tf_op jit(solution)/shard_map/ppermute | solution.py:481
